TPU v7x, 32 devices: a whole 2x2x4 slice. The times are simulated.
32 devices in a mesh: grp: 2 (over y), op: 4 (over x, core), sec: 4 (over z).
Axes of the slice: x: 2, y: 2, z: 4, core: 2. Of those that a mesh axis runs over, the one named last changes fastest.
Arguments:
- psi: bfloat16 [32, 2, 256, 256], P(('grp', 'sec')), parts along dimension 0, may hold values from -6 to 6
- left_env: bfloat16 [8, 32, 256, 256], P('op', ('grp', 'sec')), parts along dimension 1, may hold values from -0.375 to 0.375
- right_env: bfloat16 [8, 32, 256, 256], P('op', ('grp', 'sec')), parts along dimension 1, may hold values from -0.125 to 0.125
- sector_dims: int32 [2, 32], P(None, 'grp'), parts along dimension 1, may hold values from 64 to 256, as said below
- right_place: int32 [32], P('grp'), parts along dimension 0, may hold values from 0 to 15, as said below
Outputs:
- sigma: bfloat16 [32, 2, 256, 256], P(('grp', 'sec'), None, 'op'), parts along dimension 0
There are 2 independent parts, one for each index of `grp`. A program takes and returns all parts, laid end to end along the dimension named above; each array names one. Nothing has to cross between parts.
Inputs may be any that keep to these rules, and one draw needn't show every extreme that they name: `sector_dims`: in each row one block has exactly 256. `right_place`: A permutation of the blocks; the 4 blocks i * 4 to i * 4 + 3 go to positions of 4 different ranges j * 4 to j * 4 + 3.
All inputs are finite; a program needn't handle non-finite values.
Results may differ from a plain program's by a relative error of at most 0.0049.
Values may be sent and summed in bfloat16 or wider, within the bound.
No kernel may reach another device: no remote copies, remote signals or barrier semaphores. Data moves between devices by JAX's collectives and lax.ppermute only.
A program may use at most 64 MiB of HBM per device.

v0:
```python
import jax
import jax.numpy as jnp
from jax import lax
from jax.sharding import PartitionSpec as P


def local(psi, left_env, right_env, sector_dims, right_place):
    nsec = lax.axis_size("sec")
    here = lax.axis_index("sec")
    nb_dev = psi.shape[0]
    width = psi.shape[-1]
    total_blocks = right_place.shape[0]
    local_ids = jnp.arange(nb_dev, dtype=jnp.int32)
    peer_ids = jnp.arange(nsec, dtype=jnp.int32)
    cols = jnp.arange(width, dtype=jnp.int32)
    my_blocks = here * nb_dev + local_ids
    place_mine = lax.dynamic_slice_in_dim(right_place, here * nb_dev, nb_dev)
    dest_mine = place_mine // nb_dev
    hits = dest_mine[None, :] == peer_ids[:, None]
    has_block = jnp.any(hits, axis=1)
    pick_block = jnp.sum(jnp.where(hits, local_ids[None, :], 0), axis=1)
    my_slots = here * nb_dev + local_ids
    matches = right_place[None, :] == my_slots[:, None]
    block_of_slot = jnp.sum(
        jnp.where(matches, jnp.arange(total_blocks, dtype=jnp.int32)[None, :], 0), axis=1
    )
    source_dev = block_of_slot // nb_dev
    left_rows = sector_dims[0][my_blocks]
    left_cols = sector_dims[1][my_blocks]
    keep_left = (cols[None, :, None] < left_rows[:, None, None]) & (
        cols[None, None, :] < left_cols[:, None, None]
    )
    masked = jnp.where(keep_left[:, None], psi, jnp.zeros_like(psi))
    trans = jnp.einsum(
        "kbpq,bvqr->bkvpr", left_env, masked, preferred_element_type=jnp.float32
    ).astype(jnp.bfloat16)
    outgoing = jnp.take(trans, pick_block, axis=0)
    outgoing = jnp.where(has_block[:, None, None, None, None], outgoing, jnp.zeros_like(outgoing))
    incoming = lax.all_to_all(outgoing, "sec", split_axis=0, concat_axis=0, tiled=True)
    arrived = jnp.take(incoming, source_dev, axis=0)
    partial_value = jnp.einsum(
        "skvpq,ksqr->svpr", arrived, right_env, preferred_element_type=jnp.float32
    )
    slot_rows = sector_dims[0][block_of_slot]
    slot_cols = sector_dims[1][block_of_slot]
    keep_slot = (cols[None, :, None] < slot_rows[:, None, None]) & (
        cols[None, None, :] < slot_cols[:, None, None]
    )
    partial_value = jnp.where(keep_slot[:, None], partial_value, 0.0)
    sigma = lax.psum_scatter(partial_value, "op", scatter_dimension=2, tiled=True).astype(
        jnp.bfloat16
    )
    return sigma


def solution(mesh):
    return jax.shard_map(
        local,
        mesh=mesh,
        in_specs=(
            P(("grp", "sec"), None, None, None),
            P("op", ("grp", "sec"), None, None),
            P("op", ("grp", "sec"), None, None),
            P(None, "grp"),
            P("grp"),
        ),
        out_specs=P(("grp", "sec"), None, "op", None),
        check_vma=False,
    )
```

profile of v0, /device:TPU:0, one launch (start us, length us, event | category | flops | bytes accessed | tf_op | source)
XLA Modules:
  0.0 118.3 jit_solution(2424457507263125555)
XLA Ops:
  6.5 0.0 copy-start
  6.5 0.8 and_select_fusion.1
  7.4 0.1 select_reduce_fusion
  7.5 0.1 fusion.13
  7.6 0.8 slice_bitcast_fusion.1
  8.4 0.6 gather_fusion.2
  9.0 0.6 gather_fusion.3
  9.7 0.1 iota_compare_fusion
  9.7 0.2 broadcast_and_fusion
  10.0 0.0 copy-done
  10.0 2.1 %convert_bitcast_fusion = bf16[4,2,2,256,256]{3,4,2,1,0:T(8,128)(2,1)S(1)} fusion(bf16[4,2,256,256]{3,2,1,0:T(8,128)(2,1)} %param.7, pred[4,256,256]{2,1,0:T(8,128)(4,1)S(1)} %broadcast_and_fusion, bf16[2,4,256,256]{3,2,1,0:T(8,128)(2,1)S(1)} %copy-done), kind=kOutput, calls=%fused_computation.10 | convolution fusion | flops 538443776 | bytes 4456448 | tf_op jit(solution)/shard_map/kbpq,bvqr->bkvpr/dot_general | solution.py:34
  12.1 2.4 %copy.11 = bf16[4,2,2,256,256]{4,3,2,1,0:T(8,128)(2,1)} copy(bf16[4,2,2,256,256]{3,4,2,1,0:T(8,128)(2,1)S(1)} %convert_bitcast_fusion) | data formatting | bytes 4194304 | tf_op jit(solution)/shard_map/convert_element_type | solution.py:36
  14.4 2.3 %gather_fusion.4 = bf16[4,2,2,256,256]{4,3,2,1,0:T(8,128)(2,1)S(1)} fusion(bf16[4,2,2,256,256]{4,3,2,1,0:T(8,128)(2,1)} %copy.11, s32[1024]{0:T(1024)S(1)} %pad_clamp_fusion.1), kind=kCustom, calls=%fused_computation.clone | custom fusion | bytes 4194320 | tf_op jit(solution)/shard_map/jit(_take)/gather | solution.py:37
  16.7 1.6 %select_select_fusion = bf16[4,2,2,256,256]{4,3,2,1,0:T(8,128)(2,1)} fusion(bf16[4,2,2,256,256]{4,3,2,1,0:T(8,128)(2,1)S(1)} %gather_fusion.4, pred[4]{0:T(512)(128)(4,1)S(1)} %compare_and_fusion.1, pred[4]{0:T(512)(128)(4,1)S(1)} %fusion.13), kind=kLoop, calls=%fused_computation.9 | loop fusion | flops 2097152 | bytes 4194312 | tf_op jit(solution)/shard_map/jit(_where)/select_n | solution.py:38
  18.4 0.0 copy-start.1
  18.4 6.4 %all-to-all-start = ((bf16[4,2,2,256,256]{4,3,2,1,0:T(8,128)(2,1)}), bf16[4,2,2,256,256]{4,3,2,1,0:T(8,128)(2,1)S(1)}, u32[]{:S(2)}, u32[]{:S(2)}) async-start(bf16[4,2,2,256,256]{4,3,2,1,0:T(8,128)(2,1)} %select_select_fusion), calls=%async_computation | async-start | bytes 4194304 | tf_op jit(solution)/shard_map/all_to_all | solution.py:39
  24.8 0.0 reduce-scatter.2.cloned.1.call-start
  24.8 0.0 copy-done.1
  24.8 0.2 select_reduce_fusion.1
  25.0 0.6 gather_fusion
  25.7 0.6 gather_fusion.1
  26.3 0.1 iota_compare_fusion.2
  26.4 0.2 broadcast_and_fusion.1
  26.6 46.4 %all-to-all-done = bf16[4,2,2,256,256]{4,3,2,1,0:T(8,128)(2,1)S(1)} async-done(((bf16[4,2,2,256,256]{4,3,2,1,0:T(8,128)(2,1)}), bf16[4,2,2,256,256]{4,3,2,1,0:T(8,128)(2,1)S(1)}, u32[]{:S(2)}, u32[]{:S(2)}) %all-to-all-start) | async-done | bytes 2097184 | tf_op jit(solution)/shard_map/all_to_all | solution.py:39
  73.0 2.0 %gather_fusion.5 = bf16[4,2,2,256,256]{4,3,2,1,0:T(8,128)(2,1)} fusion(bf16[4,2,2,256,256]{4,3,2,1,0:T(8,128)(2,1)S(1)} %all-to-all-done, s32[1024]{0:T(1024)S(1)} %pad_clamp_fusion), kind=kCustom, calls=%fused_computation.1.clone | custom fusion | bytes 4194320 | tf_op jit(solution)/shard_map/jit(_take)/gather | solution.py:40
  75.0 4.0 %bitcast_select_fusion = f32[4,2,256,256]{3,2,1,0:T(8,128)} fusion(bf16[4,2,2,256,256]{4,3,2,1,0:T(8,128)(2,1)} %gather_fusion.5, pred[4]{0:T(512)(128)(4,1)S(1)} %get-tuple-element.6, pred[4,256,256]{2,1,0:T(8,128)(4,1)S(1)} %broadcast_and_fusion.1, bf16[2,4,256,256]{3,2,1,0:T(8,128)(2,1)} %param.9), kind=kOutput, calls=%fused_computation.6 | convolution fusion | flops 538443776 | bytes 5505028 | tf_op jit(solution)/shard_map/skvpq,ksqr->svpr/dot_general | solution.py:41
  79.0 0.0 reduce-scatter.2.cloned.1.call-update
  79.0 30.7 %reduce-scatter.2.cloned.1.call-done = f32[4,2,64,256]{3,2,1,0:T(8,128)} async-done(((f32[4,2,256,256]{3,2,1,0:T(8,128)}), f32[4,2,64,256]{3,2,1,0:T(8,128)}) %reduce-scatter.2.cloned.1.call-update) | async-done | bytes 524304 | tf_op jit(solution)/shard_map/reduce_scatter | solution.py:50
  109.7 1.8 %convert_element_type.11 = bf16[4,2,64,256]{3,2,1,0:T(8,128)(2,1)} convert(f32[4,2,64,256]{3,2,1,0:T(8,128)} %reduce-scatter.2.cloned.1.call-done) | non-fusion elementwise | flops 131072 | bytes 786432 | tf_op jit(solution)/shard_map/convert_element_type | solution.py:50
  (10 shorter events, 0.1 us)
Async XLA Ops:
  6.5 3.4 %copy-start = (bf16[2,4,256,256]{3,2,1,0:T(8,128)(2,1)S(1)}, bf16[2,4,256,256]{3,2,1,0:T(8,128)(2,1)}, u32[]{:S(2)}) copy-start(bf16[2,4,256,256]{3,2,1,0:T(8,128)(2,1)} %param.8) | copy-start | bytes 3145732
  18.4 6.5 %copy-start.1 = (s32[16]{0:T(128)S(1)}, s32[16]{0:T(128)}, u32[]{:S(2)}) copy-start(s32[16]{0:T(128)} %param.11) | copy-start | bytes 196
  18.4 54.6 %all-to-all-start = ((bf16[4,2,2,256,256]{4,3,2,1,0:T(8,128)(2,1)}), bf16[4,2,2,256,256]{4,3,2,1,0:T(8,128)(2,1)S(1)}, u32[]{:S(2)}, u32[]{:S(2)}) async-start(bf16[4,2,2,256,256]{4,3,2,1,0:T(8,128)(2,1)} %select_select_fusion), calls=%async_computation | async-start | bytes 4194304 | tf_op jit(solution)/shard_map/all_to_all | solution.py:39
  24.8 84.9 %reduce-scatter.2.cloned.1.call-start = ((), (), s32[]{:S(2)}) async-start(), calls=%async_computation.2 | async-start | bytes 2621440 | tf_op jit(solution)/shard_map/reduce_scatter | solution.py:50
Sparse Core Ops, SparseCore 0:
  79.1 30.5 reduce-scatter.1
where the time goes:
time: 119 us; the launch traced here: 118 us
  waiting for transfers between devices  77.1 us (65%)
  between operations  13.5 us (11%)
  local copies, waits for them, and re-layouts  9.94 us (8%)
  starting transfers between devices  6.45 us (5%)
  matrix products  6.08 us (5%)
  other arithmetic  5.3 us (4%)
    all_to_all x1, waiting for transfers between devices, local(): lax.all_to_all(outgoing, 'sec', split_axis=0, concat_axis=0, tiled=True)  46.4 us
    reduce_scatter x1, waiting for transfers between devices, local(): lax.psum_scatter(partial_value, 'op', scatter_dimension=2, tiled=True)  30.7 us
    all_to_all x1, starting transfers between devices, local(): lax.all_to_all(outgoing, 'sec', split_axis=0, concat_axis=0, tiled=True)  6.45 us
    dot_general x1, matrix products, local(): jnp.einsum('skvpq,ksqr->svpr', arrived, right_env, preferred_element_type...  4 us
  transfers between devices with their start and end apart: 2, of which 2 were waited for; matrix products, arithmetic and copies ran while one was open for 2% of the time, Pallas kernels for 0%

commit v1 on v0

v1 whole, which is shorter than its diff:
```python
import functools

import jax
import jax.numpy as jnp
from jax import lax
from jax.experimental import pallas as pl
from jax.experimental.pallas import tpu as pltpu
from jax.sharding import PartitionSpec as P

ANY = pl.BlockSpec(memory_space=pl.ANY)
SMEM = pl.BlockSpec(memory_space=pltpu.SMEM)
VMEM = pl.BlockSpec(memory_space=pltpu.VMEM)


def peer(i, d, n):
    return i ^ d if n & (n - 1) == 0 else (i + d) % n


def back(i, d, n):
    return i ^ d if n & (n - 1) == 0 else (i + n - d) % n


def find(place, nb, left, right):
    block, slot, found = jnp.int32(0), jnp.int32(0), jnp.bool_(False)
    for i in range(nb):
        at = place[left * nb + i]
        hit = lax.div(at, jnp.int32(nb)) == right
        block = jnp.where(hit, jnp.int32(i), block)
        slot = jnp.where(hit, lax.rem(at, jnp.int32(nb)), slot)
        found = found | hit
    return block, slot, found


def pick_kernel(nsec, nb, place, right_env, *rest):
    outs, sems = rest[:-1], rest[-1]
    me = lax.axis_index("sec")
    copies = []
    for n, d in enumerate(range(1, nsec)):
        _, slot, _ = find(place, nb, peer(me, d, nsec), me)
        copies.append(pltpu.make_async_copy(right_env.at[:, slot], outs[n], sems.at[n]))
        copies[-1].start()
    for copy in copies:
        copy.wait()


def work_kernel(rounds, nsec, nop, nb, place, dims, psi, left_env, *rest):
    count = len(rounds)
    rights, rest = rest[:count], rest[count:]
    keep, sends, rest = rest[0], rest[1:nop], rest[nop:]
    psi_v, left_v, right_v, total, sems = rest
    me = lax.axis_index("sec")
    mine = lax.axis_index("op")
    terms, vecs, width = left_v.shape[1], psi_v.shape[1], psi_v.shape[-1]
    rows = width // nop
    places, copies = [], []
    for e, d in enumerate(rounds):
        block, slot, found = find(place, nb, me, back(me, d, nsec))
        places.append((block, found))
        right = rights[e].at[:, slot] if d == 0 else rights[e]
        group = [
            pltpu.make_async_copy(psi.at[block], psi_v.at[e], sems.at[e, 0]),
            pltpu.make_async_copy(left_env.at[:, block], left_v.at[e], sems.at[e, 1]),
            pltpu.make_async_copy(right, right_v.at[e], sems.at[e, 2]),
        ]
        for copy in group:
            copy.start()
        copies.append(group)
    row = lax.broadcasted_iota(jnp.int32, (width, width), 0)
    col = lax.broadcasted_iota(jnp.int32, (width, width), 1)
    for e in range(count):
        block, found = places[e]
        live_rows = jnp.where(found, dims[0, me * nb + block], 0)
        live_cols = jnp.where(found, dims[1, me * nb + block], 0)
        keep_block = (row < live_rows) & (col < live_cols)
        copies[e][0].wait()
        copies[e][1].wait()
        masked = [jnp.where(keep_block, psi_v[e, v], jnp.zeros_like(psi_v[e, v])) for v in range(vecs)]
        trans = [
            [
                jnp.dot(left_v[e, k], masked[v], preferred_element_type=jnp.float32).astype(jnp.bfloat16)
                for k in range(terms)
            ]
            for v in range(vecs)
        ]
        copies[e][2].wait()
        for v in range(vecs):
            value = jnp.dot(trans[v][0], right_v[e, 0], preferred_element_type=jnp.float32)
            for k in range(1, terms):
                value = value + jnp.dot(trans[v][k], right_v[e, k], preferred_element_type=jnp.float32)
            total[v] = jnp.where(keep_block, value, 0.0)
        for d in range(nop):
            start = pl.multiple_of(peer(mine, d, nop) * rows, rows)
            part = total[:, pl.ds(start, rows), :]
            if d == 0:
                keep[e] = part
            else:
                sends[d - 1][e] = part.astype(jnp.bfloat16)


def place_kernel(nsec, nb, place, *rest):
    parts, out = rest[:-1], rest[-1]
    me = lax.axis_index("sec")
    for d in range(nsec):
        _, slot, found = find(place, nb, peer(me, d, nsec), me)

        @pl.when(found)
        def _():
            out[slot] = parts[d][...]


def local(psi, left_env, right_env, sector_dims, right_place):
    nsec, nop = lax.axis_size("sec"), lax.axis_size("op")
    nb, vecs, width, _ = psi.shape
    terms = left_env.shape[0]
    rows = width // nop
    block = width * width

    def ship(x, axis, way, d):
        n = lax.axis_size(axis)
        return lax.ppermute(x, axis, [(i, way(i, d, n)) for i in range(n)])

    picked = pl.pallas_call(
        functools.partial(pick_kernel, nsec, nb),
        in_specs=[SMEM, ANY],
        out_specs=[ANY] * (nsec - 1),
        out_shape=[jax.ShapeDtypeStruct((terms, width, width), right_env.dtype)] * (nsec - 1),
        scratch_shapes=[pltpu.SemaphoreType.DMA((nsec - 1,))],
        cost_estimate=pl.CostEstimate(flops=0, bytes_accessed=4 * nsec * terms * block, transcendentals=0),
        name="pick",
    )(right_place, right_env)
    rights = [right_env] + [ship(picked[d - 1], "sec", peer, d) for d in range(1, nsec)]

    def work(rounds):
        count = len(rounds)
        outs = pl.pallas_call(
            functools.partial(work_kernel, rounds, nsec, nop, nb),
            in_specs=[SMEM, SMEM, ANY, ANY] + [ANY] * count,
            out_specs=[VMEM] * nop,
            out_shape=[jax.ShapeDtypeStruct((count, vecs, rows, width), jnp.float32)]
            + [jax.ShapeDtypeStruct((count, vecs, rows, width), jnp.bfloat16)] * (nop - 1),
            scratch_shapes=[
                pltpu.VMEM((count, vecs, width, width), jnp.bfloat16),
                pltpu.VMEM((count, terms, width, width), jnp.bfloat16),
                pltpu.VMEM((count, terms, width, width), jnp.bfloat16),
                pltpu.VMEM((vecs, width, width), jnp.float32),
                pltpu.SemaphoreType.DMA((count, 3)),
            ],
            compiler_params=pltpu.CompilerParams(vmem_limit_bytes=48 * 2**20),
            cost_estimate=pl.CostEstimate(
                flops=count * terms * vecs * 4 * width**3,
                bytes_accessed=count * block * 2 * (2 * terms + 2 * vecs),
                transcendentals=0,
            ),
            name="work",
        )(right_place, sector_dims, psi, left_env, *[rights[d] for d in rounds])
        value = outs[0]
        for d in range(1, nop):
            value = value + ship(outs[d], "op", peer, d).astype(jnp.float32)
        return value.astype(jnp.bfloat16)

    groups = [[d] for d in range(nsec)] if nsec <= 4 else [list(range(nsec // 2)), list(range(nsec // 2, nsec))]
    parts = []
    for rounds in groups:
        value = work(rounds)
        for e, d in enumerate(rounds):
            parts.append(value[e] if d == 0 else ship(value[e], "sec", back, d))

    return pl.pallas_call(
        functools.partial(place_kernel, nsec, nb),
        in_specs=[SMEM] + [VMEM] * nsec,
        out_specs=VMEM,
        out_shape=jax.ShapeDtypeStruct((nb, vecs, rows, width), jnp.bfloat16),
        name="place",
    )(right_place, *parts)


def solution(mesh):
    return jax.shard_map(
        local,
        mesh=mesh,
        in_specs=(
            P(("grp", "sec"), None, None, None),
            P("op", ("grp", "sec"), None, None),
            P("op", ("grp", "sec"), None, None),
            P(None, "grp"),
            P("grp"),
        ),
        out_specs=P(("grp", "sec"), None, "op", None),
        check_vma=False,
    )
```

time: 119 us -> 80.3 us (0.67)
  waiting for transfers between devices: 77.1 us -> 25 us
  Pallas kernels: 0 us -> 32.9 us
  between operations: 13.5 us -> 0.12 us
  starting transfers between devices: 6.45 us -> 19.1 us
  local copies, waits for them, and re-layouts: 9.94 us -> 2.18 us
  matrix products: 6.08 us -> 0 us
  other arithmetic: 5.3 us -> 0.76 us
    all_to_all x1 -> x0, waiting for transfers between devices: 46.4 us -> none  [local(): lax.all_to_all(outgoing, 'sec', split_axis=0, concat_axis=0, tiled=True)]
    pallas_call x0 -> x6, Pallas kernels: none -> 32.9 us  [the longest x1 25.8 us: local(): pl.pallas_call(functools.partial(pick_kernel, nsec, nb), in_specs=[SMEM,...]
    reduce_scatter x1 -> x0, waiting for transfers between devices: 30.7 us -> none  [local(): lax.psum_scatter(partial_value, 'op', scatter_dimension=2, tiled=True)]
    ppermute x0 -> x18, waiting for transfers between devices: none -> 25 us  [ship(): return lax.ppermute(x, axis, [(i, way(i, d, n)) for i in range(n)])]
    ppermute x0 -> x18, starting transfers between devices: none -> 19.1 us  [ship(): return lax.ppermute(x, axis, [(i, way(i, d, n)) for i in range(n)])]
    gather x6 -> x0, local copies, waits for them, and re-layouts: 6.8 us -> none  [the longest x1 2.27 us: local(): outgoing = jnp.take(trans, pick_block, axis=0)]
    all_to_all x1 -> x0, starting transfers between devices: 6.45 us -> none  [local(): lax.all_to_all(outgoing, 'sec', split_axis=0, concat_axis=0, tiled=True)]
    dot_general x2 -> x0, matrix products: 6.08 us -> none  [the longest x1 4 us: local(): jnp.einsum('skvpq,ksqr->svpr', arrived, right_env, preferred_element_type...]
  transfers between devices with their start and end apart: 2 -> 18, of which waited for: 2 -> 7; matrix products, arithmetic and copies ran while one was open for 2% -> 1% of each run, Pallas kernels for 0% -> 7%
where the time goes in v1:
time: 80.3 us; the launch traced here: 80 us
  Pallas kernels  32.9 us (41%)
  waiting for transfers between devices  25 us (31%)
  starting transfers between devices  19.1 us (24%)
  local copies, waits for them, and re-layouts  2.18 us (3%)
    pallas_call x1, Pallas kernels, local(): pl.pallas_call(functools.partial(pick_kernel, nsec, nb), in_specs=[SMEM,...  25.8 us
    ppermute x18, waiting for transfers between devices, ship(): return lax.ppermute(x, axis, [(i, way(i, d, n)) for i in range(n)])  25 us
    ppermute x18, starting transfers between devices, ship(): return lax.ppermute(x, axis, [(i, way(i, d, n)) for i in range(n)])  19.1 us
    pallas_call x4, Pallas kernels, work(): pl.pallas_call(functools.partial(work_kernel, rounds, nsec, nop, nb), in_...  5.39 us
    unnamed x16, local copies, waits for them, and re-layouts  2.18 us
    pallas_call x1, Pallas kernels, local(): pl.pallas_call(functools.partial(place_kernel, nsec, nb), in_specs=[SMEM]...  1.74 us
  transfers between devices with their start and end apart: 18, of which 7 were waited for; matrix products, arithmetic and copies ran while one was open for 1% of the time, Pallas kernels for 7%

profile of v1, /device:TPU:0, one launch (start us, length us, event | category | flops | bytes accessed | tf_op | source)
XLA Modules:
  0.0 80.0 jit_solution(3009725083787597496)
XLA Ops:
  0.0 0.0 copy-start
  0.0 25.8 %pick.1 = (bf16[2,256,256]{2,1,0:T(8,128)(2,1)}, bf16[2,256,256]{2,1,0:T(8,128)(2,1)}, bf16[2,256,256]{2,1,0:T(8,128)(2,1)}) custom-call(s32[16]{0:T(128)} %place.13, bf16[2,4,256,256]{3,2,1,0:T(8,128)(2,1)} %right_env.1), custom_call_target="tpu_custom_call" | custom-call | bytes 2097152 | tf_op jit(solution)/shard_map/pick/pallas_call | solution.py:122
  25.8 5.1 %collective-permute-start.13 = (bf16[2,256,256]{2,1,0:T(8,128)(2,1)}, bf16[2,256,256]{2,1,0:T(8,128)(2,1)S(1)}, u32[]{:S(2)}, u32[]{:S(2)}) collective-permute-start(bf16[2,256,256]{2,1,0:T(8,128)(2,1)} %get-tuple-element.38), channel_id=1, source_target_pairs={{0,3},{1,2},{2,1},{3,0},{4,7},{5,6},{6,5},{7,4},{8,11},{9,10},{10,... | collective-permute-start | bytes 786440 | tf_op jit(solution)/shard_map/ppermute | solution.py:120
  30.9 0.0 copy-start.3
  30.9 0.0 copy-start.4
  30.9 0.0 collective-permute-start.8
  30.9 0.7 collective-permute-start.3
  31.6 6.8 %collective-permute-done.13.rest_0_ = bf16[2,256,256]{2,1,0:T(8,128)(2,1)S(1)} collective-permute-done((bf16[2,256,256]{2,1,0:T(8,128)(2,1)}, bf16[2,256,256]{2,1,0:T(8,128)(2,1)S(1)}, u32[]{:S(2)}, u32[]{:S(2)}) %collective-permute-start.13) | collective-permute-done | bytes 262176 | tf_op jit(solution)/shard_map/ppermute | solution.py:120
  38.4 0.0 copy-done
  38.4 0.0 copy-done.3
  38.4 0.0 copy-done.4
  38.4 0.0 copy-start.1
  38.4 1.2 %copy-done.1 = bf16[2,4,256,256]{3,2,1,0:T(8,128)(2,1)S(1)} copy-done((bf16[2,4,256,256]{3,2,1,0:T(8,128)(2,1)S(1)}, bf16[2,4,256,256]{3,2,1,0:T(8,128)(2,1)}, u32[]{:S(2)}) %copy-start.1) | copy-done | bytes 1048600
  39.6 0.0 copy-start.2
  39.6 1.3 %work.7 = (f32[1,2,64,256]{3,2,1,0:T(8,128)S(1)}, bf16[1,2,64,256]{3,2,1,0:T(8,128)(2,1)S(1)}, bf16[1,2,64,256]{3,2,1,0:T(8,128)(2,1)S(1)}, bf16[1,2,64,256]{3,2,1,0:T(8,128)(2,1)S(1)}) custom-call(s32[16]{0:T(128)S(1)} %copy-done.3, s32[2,16]{1,0:T(2,128)S(1)} %copy-done.4, bf16[4,2,256,256]{3,2,1,0:T(8,128)(2,1)S(1)} %copy-done, ...), custom_call_target="tpu_custom_call" | custom-call | flops 268435456 | bytes 1048576 | tf_op jit(solution)/shard_map/work/pallas_call | solution.py:135
  41.0 0.1 collective-permute-start.14
  41.1 1.8 %collective-permute-start.15 = (bf16[1,2,64,256]{3,2,1,0:T(8,128)(2,1)S(1)}, bf16[1,2,64,256]{3,2,1,0:T(8,128)(2,1)S(1)}, u32[]{:S(2)}, u32[]{:S(2)}) collective-permute-start(bf16[1,2,64,256]{3,2,1,0:T(8,128)(2,1)S(1)} %get-tuple-element.41), channel_id=1, source_target_pairs={{0,8},{4,12},{8,0},{12,4},{1,9},{5,13},{9,1},{13,5},{2,10},{6,14},... | collective-permute-start | bytes 196616 | tf_op jit(solution)/shard_map/ppermute | solution.py:120
  42.8 0.1 collective-permute-start.16
  42.9 0.0 copy-done.2
  42.9 1.4 %work.4 = (f32[1,2,64,256]{3,2,1,0:T(8,128)S(1)}, bf16[1,2,64,256]{3,2,1,0:T(8,128)(2,1)S(1)}, bf16[1,2,64,256]{3,2,1,0:T(8,128)(2,1)S(1)}, bf16[1,2,64,256]{3,2,1,0:T(8,128)(2,1)S(1)}) custom-call(s32[16]{0:T(128)S(1)} %copy-done.3, s32[2,16]{1,0:T(2,128)S(1)} %copy-done.4, bf16[4,2,256,256]{3,2,1,0:T(8,128)(2,1)S(1)} %copy-done, ...), custom_call_target="tpu_custom_call" | custom-call | flops 268435456 | bytes 1048576 | tf_op jit(solution)/shard_map/work/pallas_call | solution.py:135
  44.3 9.1 %collective-permute-done.8.rest_0_ = bf16[2,256,256]{2,1,0:T(8,128)(2,1)S(1)} collective-permute-done((bf16[2,256,256]{2,1,0:T(8,128)(2,1)}, bf16[2,256,256]{2,1,0:T(8,128)(2,1)S(1)}, u32[]{:S(2)}, u32[]{:S(2)}) %collective-permute-start.8) | collective-permute-done | bytes 262176 | tf_op jit(solution)/shard_map/ppermute | solution.py:120
  53.4 0.0 collective-permute-start
  53.4 1.3 %work.6 = (f32[1,2,64,256]{3,2,1,0:T(8,128)S(1)}, bf16[1,2,64,256]{3,2,1,0:T(8,128)(2,1)S(1)}, bf16[1,2,64,256]{3,2,1,0:T(8,128)(2,1)S(1)}, bf16[1,2,64,256]{3,2,1,0:T(8,128)(2,1)S(1)}) custom-call(s32[16]{0:T(128)S(1)} %copy-done.3, s32[2,16]{1,0:T(2,128)S(1)} %copy-done.4, bf16[4,2,256,256]{3,2,1,0:T(8,128)(2,1)S(1)} %copy-done, ...), custom_call_target="tpu_custom_call" | custom-call | flops 268435456 | bytes 1048576 | tf_op jit(solution)/shard_map/work/pallas_call | solution.py:135
  54.8 0.0 collective-permute-done.3.rest_0_
  54.8 1.6 %collective-permute-start.1 = (bf16[1,2,64,256]{3,2,1,0:T(8,128)(2,1)S(1)}, bf16[1,2,64,256]{3,2,1,0:T(8,128)(2,1)S(1)}, u32[]{:S(2)}, u32[]{:S(2)}) collective-permute-start(bf16[1,2,64,256]{3,2,1,0:T(8,128)(2,1)S(1)} %get-tuple-element.26), channel_id=1, source_target_pairs={{0,8},{4,12},{8,0},{12,4},{1,9},{5,13},{9,1},{13,5},{2,10},{6,14},... | collective-permute-start | bytes 196616 | tf_op jit(solution)/shard_map/ppermute | solution.py:120
  56.3 1.3 %work.5 = (f32[1,2,64,256]{3,2,1,0:T(8,128)S(1)}, bf16[1,2,64,256]{3,2,1,0:T(8,128)(2,1)S(1)}, bf16[1,2,64,256]{3,2,1,0:T(8,128)(2,1)S(1)}, bf16[1,2,64,256]{3,2,1,0:T(8,128)(2,1)S(1)}) custom-call(s32[16]{0:T(128)S(1)} %copy-done.3, s32[2,16]{1,0:T(2,128)S(1)} %copy-done.4, bf16[4,2,256,256]{3,2,1,0:T(8,128)(2,1)S(1)} %copy-done, ...), custom_call_target="tpu_custom_call" | custom-call | flops 268435456 | bytes 1048576 | tf_op jit(solution)/shard_map/work/pallas_call | solution.py:135
  57.7 0.0 collective-permute-done.14
  57.7 0.6 collective-permute-start.10
  58.3 0.0 collective-permute-done.15
  58.3 1.1 %collective-permute-start.11 = (bf16[1,2,64,256]{3,2,1,0:T(8,128)(2,1)S(1)}, bf16[1,2,64,256]{3,2,1,0:T(8,128)(2,1)S(1)}, u32[]{:S(2)}, u32[]{:S(2)}) collective-permute-start(bf16[1,2,64,256]{3,2,1,0:T(8,128)(2,1)S(1)} %get-tuple-element.37), channel_id=1, source_target_pairs={{0,12},{4,8},{8,4},{12,0},{1,13},{5,9},{9,5},{13,1},{2,14},{6,10},... | collective-permute-start | bytes 196616 | tf_op jit(solution)/shard_map/ppermute | solution.py:120
  59.4 0.0 collective-permute-done.16
  59.4 0.6 collective-permute-start.9
  60.0 2.7 %collective-permute-done.10 = bf16[1,2,64,256]{3,2,1,0:T(8,128)(2,1)S(1)} collective-permute-done((bf16[1,2,64,256]{3,2,1,0:T(8,128)(2,1)S(1)}, bf16[1,2,64,256]{3,2,1,0:T(8,128)(2,1)S(1)}, u32[]{:S(2)}, u32[]{:S(2)}) %collective-permute-start.10) | collective-permute-done | bytes 65568 | tf_op jit(solution)/shard_map/ppermute | solution.py:120
  62.7 0.0 collective-permute-start.4
  62.7 0.0 collective-permute-done.11
  62.7 1.4 %collective-permute-start.5 = (bf16[1,2,64,256]{3,2,1,0:T(8,128)(2,1)S(1)}, bf16[1,2,64,256]{3,2,1,0:T(8,128)(2,1)S(1)}, u32[]{:S(2)}, u32[]{:S(2)}) collective-permute-start(bf16[1,2,64,256]{3,2,1,0:T(8,128)(2,1)S(1)} %get-tuple-element.31), channel_id=1, source_target_pairs={{0,8},{4,12},{8,0},{12,4},{1,9},{5,13},{9,1},{13,5},{2,10},{6,14},... | collective-permute-start | bytes 196616 | tf_op jit(solution)/shard_map/ppermute | solution.py:120
  64.1 0.0 collective-permute-done.9
  64.1 0.5 collective-permute-start.6
  64.6 0.0 collective-permute-done.4
  64.6 1.3 %collective-permute-start.2 = (bf16[1,2,64,256]{3,2,1,0:T(8,128)(2,1)S(1)}, bf16[1,2,64,256]{3,2,1,0:T(8,128)(2,1)S(1)}, u32[]{:S(2)}, u32[]{:S(2)}) collective-permute-start(bf16[1,2,64,256]{3,2,1,0:T(8,128)(2,1)S(1)} %get-tuple-element.27), channel_id=1, source_target_pairs={{0,12},{4,8},{8,4},{12,0},{1,13},{5,9},{9,5},{13,1},{2,14},{6,10},... | collective-permute-start | bytes 196616 | tf_op jit(solution)/shard_map/ppermute | solution.py:120
  65.9 1.5 %collective-permute-done.5 = bf16[1,2,64,256]{3,2,1,0:T(8,128)(2,1)S(1)} collective-permute-done((bf16[1,2,64,256]{3,2,1,0:T(8,128)(2,1)S(1)}, bf16[1,2,64,256]{3,2,1,0:T(8,128)(2,1)S(1)}, u32[]{:S(2)}, u32[]{:S(2)}) %collective-permute-start.5) | collective-permute-done | bytes 65568 | tf_op jit(solution)/shard_map/ppermute | solution.py:120
  67.4 2.5 %collective-permute-start.17 = (bf16[2,64,256]{2,1,0:T(8,128)(2,1)S(1)}, bf16[2,64,256]{2,1,0:T(8,128)(2,1)S(1)}, u32[]{:S(2)}, u32[]{:S(2)}) collective-permute-start(bf16[2,64,256]{2,1,0:T(8,128)(2,1)S(1)} %fusion.3), channel_id=1, source_target_pairs={{0,3},{1,2},{2,1},{3,0},{4,7},{5,6},{6,5},{7,4},{8,11},{9,10},{10,... | collective-permute-start | bytes 196616 | tf_op jit(solution)/shard_map/ppermute | solution.py:120
  69.9 0.0 collective-permute-done.6
  69.9 1.9 %collective-permute-start.12 = (bf16[2,64,256]{2,1,0:T(8,128)(2,1)S(1)}, bf16[2,64,256]{2,1,0:T(8,128)(2,1)S(1)}, u32[]{:S(2)}, u32[]{:S(2)}) collective-permute-start(bf16[2,64,256]{2,1,0:T(8,128)(2,1)S(1)} %fusion.2), channel_id=1, source_target_pairs={{0,2},{1,3},{2,0},{3,1},{4,6},{5,7},{6,4},{7,5},{8,10},{9,11},{10,... | collective-permute-start | bytes 196616 | tf_op jit(solution)/shard_map/ppermute | solution.py:120
  71.8 0.0 collective-permute-done
  71.8 0.1 collective-permute-start.7
  71.9 0.0 collective-permute-done.1
  71.9 0.0 collective-permute-done.2
  71.9 0.7 fusion.rest_0_
  72.6 1.0 %collective-permute-done.17.rest_3_ = bf16[2,64,256]{2,1,0:T(8,128)(2,1)S(1)} collective-permute-done((bf16[2,64,256]{2,1,0:T(8,128)(2,1)S(1)}, bf16[2,64,256]{2,1,0:T(8,128)(2,1)S(1)}, u32[]{:S(2)}, u32[]{:S(2)}) %collective-permute-start.17) | collective-permute-done | bytes 65568 | tf_op jit(solution)/shard_map/ppermute | solution.py:120
  73.6 0.0 copy-start.5
  73.6 3.5 %collective-permute-done.12.rest_2_ = bf16[2,64,256]{2,1,0:T(8,128)(2,1)S(1)} collective-permute-done((bf16[2,64,256]{2,1,0:T(8,128)(2,1)S(1)}, bf16[2,64,256]{2,1,0:T(8,128)(2,1)S(1)}, u32[]{:S(2)}, u32[]{:S(2)}) %collective-permute-start.12) | collective-permute-done | bytes 65568 | tf_op jit(solution)/shard_map/ppermute | solution.py:120
  77.0 0.0 copy-start.6
  77.1 0.3 collective-permute-done.7.rest_1_
  77.4 0.0 copy-done.5
  77.4 0.3 copy-done.6
  77.7 0.0 copy-start.7
  77.7 0.6 copy-done.7
  78.3 1.7 %place.12 = bf16[4,2,64,256]{3,2,1,0:T(8,128)(2,1)} custom-call(s32[16]{0:T(128)} %place.13, bf16[2,64,256]{2,1,0:T(8,128)(2,1)} %fusion.rest_0_, bf16[2,64,256]{2,1,0:T(8,128)(2,1)} %copy-done.7, bf16[2,64,256]{2,1,0:T(8,128)(2,1)} %copy-done.6, bf16[2,64,256]{2,1,0:T(8,128)(2,1)} %copy-done.5), custom_call_target="tpu_custom_call" | custom-call | tf_op jit(solution)/shard_map/place/pallas_call | solution.py:168
  (3 shorter events, 0.1 us)
Async XLA Ops:
  0.0 38.4 %copy-start = (bf16[4,2,256,256]{3,2,1,0:T(8,128)(2,1)S(1)}, bf16[4,2,256,256]{3,2,1,0:T(8,128)(2,1)}, u32[]{:S(2)}) copy-start(bf16[4,2,256,256]{3,2,1,0:T(8,128)(2,1)} %psi.7) | copy-start | bytes 3145732
  25.8 12.6 %collective-permute-start.13 = (bf16[2,256,256]{2,1,0:T(8,128)(2,1)}, bf16[2,256,256]{2,1,0:T(8,128)(2,1)S(1)}, u32[]{:S(2)}, u32[]{:S(2)}) collective-permute-start(bf16[2,256,256]{2,1,0:T(8,128)(2,1)} %get-tuple-element.38), channel_id=1, source_target_pairs={{0,3},{1,2},{2,1},{3,0},{4,7},{5,6},{6,5},{7,4},{8,11},{9,10},{10,... | collective-permute-start | bytes 786440 | tf_op jit(solution)/shard_map/ppermute | solution.py:120
  30.9 7.5 %copy-start.3 = (s32[16]{0:T(128)S(1)}, s32[16]{0:T(128)}, u32[]{:S(2)}) copy-start(s32[16]{0:T(128)} %place.13) | copy-start | bytes 196
  30.9 7.5 %copy-start.4 = (s32[2,16]{1,0:T(2,128)S(1)}, s32[2,16]{1,0:T(2,128)}, u32[]{:S(2)}) copy-start(s32[2,16]{1,0:T(2,128)} %dims.7) | copy-start | bytes 388
  30.9 22.5 %collective-permute-start.8 = (bf16[2,256,256]{2,1,0:T(8,128)(2,1)}, bf16[2,256,256]{2,1,0:T(8,128)(2,1)S(1)}, u32[]{:S(2)}, u32[]{:S(2)}) collective-permute-start(bf16[2,256,256]{2,1,0:T(8,128)(2,1)} %get-tuple-element.33), channel_id=1, source_target_pairs={{0,2},{1,3},{2,0},{3,1},{4,6},{5,7},{6,4},{7,5},{8,10},{9,11},{10,... | collective-permute-start | bytes 786440 | tf_op jit(solution)/shard_map/ppermute | solution.py:120
  30.9 23.9 %collective-permute-start.3 = (bf16[2,256,256]{2,1,0:T(8,128)(2,1)}, bf16[2,256,256]{2,1,0:T(8,128)(2,1)S(1)}, u32[]{:S(2)}, u32[]{:S(2)}) collective-permute-start(bf16[2,256,256]{2,1,0:T(8,128)(2,1)} %get-tuple-element.28), channel_id=1, source_target_pairs={{0,1},{1,0},{2,3},{3,2},{4,5},{5,4},{6,7},{7,6},{8,9},{9,8},{10,11... | collective-permute-start | bytes 786440 | tf_op jit(solution)/shard_map/ppermute | solution.py:120
  38.4 1.2 %copy-start.1 = (bf16[2,4,256,256]{3,2,1,0:T(8,128)(2,1)S(1)}, bf16[2,4,256,256]{3,2,1,0:T(8,128)(2,1)}, u32[]{:S(2)}) copy-start(bf16[2,4,256,256]{3,2,1,0:T(8,128)(2,1)} %left_env.7) | copy-start | bytes 3145732
  39.6 3.3 %copy-start.2 = (bf16[2,4,256,256]{3,2,1,0:T(8,128)(2,1)S(1)}, bf16[2,4,256,256]{3,2,1,0:T(8,128)(2,1)}, u32[]{:S(2)}) copy-start(bf16[2,4,256,256]{3,2,1,0:T(8,128)(2,1)} %right_env.1) | copy-start | bytes 3145732
  41.0 16.7 %collective-permute-start.14 = (bf16[1,2,64,256]{3,2,1,0:T(8,128)(2,1)S(1)}, bf16[1,2,64,256]{3,2,1,0:T(8,128)(2,1)S(1)}, u32[]{:S(2)}, u32[]{:S(2)}) collective-permute-start(bf16[1,2,64,256]{3,2,1,0:T(8,128)(2,1)S(1)} %get-tuple-element.40), channel_id=1, source_target_pairs={{0,4},{4,0},{8,12},{12,8},{1,5},{5,1},{9,13},{13,9},{2,6},{6,2},{1... | collective-permute-start | bytes 196616 | tf_op jit(solution)/shard_map/ppermute | solution.py:120
  41.1 17.2 %collective-permute-start.15 = (bf16[1,2,64,256]{3,2,1,0:T(8,128)(2,1)S(1)}, bf16[1,2,64,256]{3,2,1,0:T(8,128)(2,1)S(1)}, u32[]{:S(2)}, u32[]{:S(2)}) collective-permute-start(bf16[1,2,64,256]{3,2,1,0:T(8,128)(2,1)S(1)} %get-tuple-element.41), channel_id=1, source_target_pairs={{0,8},{4,12},{8,0},{12,4},{1,9},{5,13},{9,1},{13,5},{2,10},{6,14},... | collective-permute-start | bytes 196616 | tf_op jit(solution)/shard_map/ppermute | solution.py:120
  42.8 16.5 %collective-permute-start.16 = (bf16[1,2,64,256]{3,2,1,0:T(8,128)(2,1)S(1)}, bf16[1,2,64,256]{3,2,1,0:T(8,128)(2,1)S(1)}, u32[]{:S(2)}, u32[]{:S(2)}) collective-permute-start(bf16[1,2,64,256]{3,2,1,0:T(8,128)(2,1)S(1)} %get-tuple-element.42), channel_id=1, source_target_pairs={{0,12},{4,8},{8,4},{12,0},{1,13},{5,9},{9,5},{13,1},{2,14},{6,10},... | collective-permute-start | bytes 196616 | tf_op jit(solution)/shard_map/ppermute | solution.py:120
  53.4 18.4 %collective-permute-start = (bf16[1,2,64,256]{3,2,1,0:T(8,128)(2,1)S(1)}, bf16[1,2,64,256]{3,2,1,0:T(8,128)(2,1)S(1)}, u32[]{:S(2)}, u32[]{:S(2)}) collective-permute-start(bf16[1,2,64,256]{3,2,1,0:T(8,128)(2,1)S(1)} %get-tuple-element.25), channel_id=1, source_target_pairs={{0,4},{4,0},{8,12},{12,8},{1,5},{5,1},{9,13},{13,9},{2,6},{6,2},{1... | collective-permute-start | bytes 196616 | tf_op jit(solution)/shard_map/ppermute | solution.py:120
  54.8 17.2 %collective-permute-start.1 = (bf16[1,2,64,256]{3,2,1,0:T(8,128)(2,1)S(1)}, bf16[1,2,64,256]{3,2,1,0:T(8,128)(2,1)S(1)}, u32[]{:S(2)}, u32[]{:S(2)}) collective-permute-start(bf16[1,2,64,256]{3,2,1,0:T(8,128)(2,1)S(1)} %get-tuple-element.26), channel_id=1, source_target_pairs={{0,8},{4,12},{8,0},{12,4},{1,9},{5,13},{9,1},{13,5},{2,10},{6,14},... | collective-permute-start | bytes 196616 | tf_op jit(solution)/shard_map/ppermute | solution.py:120
  57.7 5.0 %collective-permute-start.10 = (bf16[1,2,64,256]{3,2,1,0:T(8,128)(2,1)S(1)}, bf16[1,2,64,256]{3,2,1,0:T(8,128)(2,1)S(1)}, u32[]{:S(2)}, u32[]{:S(2)}) collective-permute-start(bf16[1,2,64,256]{3,2,1,0:T(8,128)(2,1)S(1)} %get-tuple-element.36), channel_id=1, source_target_pairs={{0,8},{4,12},{8,0},{12,4},{1,9},{5,13},{9,1},{13,5},{2,10},{6,14},... | collective-permute-start | bytes 196616 | tf_op jit(solution)/shard_map/ppermute | solution.py:120
  58.3 4.4 %collective-permute-start.11 = (bf16[1,2,64,256]{3,2,1,0:T(8,128)(2,1)S(1)}, bf16[1,2,64,256]{3,2,1,0:T(8,128)(2,1)S(1)}, u32[]{:S(2)}, u32[]{:S(2)}) collective-permute-start(bf16[1,2,64,256]{3,2,1,0:T(8,128)(2,1)S(1)} %get-tuple-element.37), channel_id=1, source_target_pairs={{0,12},{4,8},{8,4},{12,0},{1,13},{5,9},{9,5},{13,1},{2,14},{6,10},... | collective-permute-start | bytes 196616 | tf_op jit(solution)/shard_map/ppermute | solution.py:120
  59.4 4.7 %collective-permute-start.9 = (bf16[1,2,64,256]{3,2,1,0:T(8,128)(2,1)S(1)}, bf16[1,2,64,256]{3,2,1,0:T(8,128)(2,1)S(1)}, u32[]{:S(2)}, u32[]{:S(2)}) collective-permute-start(bf16[1,2,64,256]{3,2,1,0:T(8,128)(2,1)S(1)} %get-tuple-element.35), channel_id=1, source_target_pairs={{0,4},{4,0},{8,12},{12,8},{1,5},{5,1},{9,13},{13,9},{2,6},{6,2},{1... | collective-permute-start | bytes 196616 | tf_op jit(solution)/shard_map/ppermute | solution.py:120
  62.7 1.9 %collective-permute-start.4 = (bf16[1,2,64,256]{3,2,1,0:T(8,128)(2,1)S(1)}, bf16[1,2,64,256]{3,2,1,0:T(8,128)(2,1)S(1)}, u32[]{:S(2)}, u32[]{:S(2)}) collective-permute-start(bf16[1,2,64,256]{3,2,1,0:T(8,128)(2,1)S(1)} %get-tuple-element.30), channel_id=1, source_target_pairs={{0,4},{4,0},{8,12},{12,8},{1,5},{5,1},{9,13},{13,9},{2,6},{6,2},{1... | collective-permute-start | bytes 196616 | tf_op jit(solution)/shard_map/ppermute | solution.py:120
  62.7 4.7 %collective-permute-start.5 = (bf16[1,2,64,256]{3,2,1,0:T(8,128)(2,1)S(1)}, bf16[1,2,64,256]{3,2,1,0:T(8,128)(2,1)S(1)}, u32[]{:S(2)}, u32[]{:S(2)}) collective-permute-start(bf16[1,2,64,256]{3,2,1,0:T(8,128)(2,1)S(1)} %get-tuple-element.31), channel_id=1, source_target_pairs={{0,8},{4,12},{8,0},{12,4},{1,9},{5,13},{9,1},{13,5},{2,10},{6,14},... | collective-permute-start | bytes 196616 | tf_op jit(solution)/shard_map/ppermute | solution.py:120
  64.1 5.8 %collective-permute-start.6 = (bf16[1,2,64,256]{3,2,1,0:T(8,128)(2,1)S(1)}, bf16[1,2,64,256]{3,2,1,0:T(8,128)(2,1)S(1)}, u32[]{:S(2)}, u32[]{:S(2)}) collective-permute-start(bf16[1,2,64,256]{3,2,1,0:T(8,128)(2,1)S(1)} %get-tuple-element.32), channel_id=1, source_target_pairs={{0,12},{4,8},{8,4},{12,0},{1,13},{5,9},{9,5},{13,1},{2,14},{6,10},... | collective-permute-start | bytes 196616 | tf_op jit(solution)/shard_map/ppermute | solution.py:120
  64.6 7.3 %collective-permute-start.2 = (bf16[1,2,64,256]{3,2,1,0:T(8,128)(2,1)S(1)}, bf16[1,2,64,256]{3,2,1,0:T(8,128)(2,1)S(1)}, u32[]{:S(2)}, u32[]{:S(2)}) collective-permute-start(bf16[1,2,64,256]{3,2,1,0:T(8,128)(2,1)S(1)} %get-tuple-element.27), channel_id=1, source_target_pairs={{0,12},{4,8},{8,4},{12,0},{1,13},{5,9},{9,5},{13,1},{2,14},{6,10},... | collective-permute-start | bytes 196616 | tf_op jit(solution)/shard_map/ppermute | solution.py:120
  67.4 6.2 %collective-permute-start.17 = (bf16[2,64,256]{2,1,0:T(8,128)(2,1)S(1)}, bf16[2,64,256]{2,1,0:T(8,128)(2,1)S(1)}, u32[]{:S(2)}, u32[]{:S(2)}) collective-permute-start(bf16[2,64,256]{2,1,0:T(8,128)(2,1)S(1)} %fusion.3), channel_id=1, source_target_pairs={{0,3},{1,2},{2,1},{3,0},{4,7},{5,6},{6,5},{7,4},{8,11},{9,10},{10,... | collective-permute-start | bytes 196616 | tf_op jit(solution)/shard_map/ppermute | solution.py:120
  69.9 7.2 %collective-permute-start.12 = (bf16[2,64,256]{2,1,0:T(8,128)(2,1)S(1)}, bf16[2,64,256]{2,1,0:T(8,128)(2,1)S(1)}, u32[]{:S(2)}, u32[]{:S(2)}) collective-permute-start(bf16[2,64,256]{2,1,0:T(8,128)(2,1)S(1)} %fusion.2), channel_id=1, source_target_pairs={{0,2},{1,3},{2,0},{3,1},{4,6},{5,7},{6,4},{7,5},{8,10},{9,11},{10,... | collective-permute-start | bytes 196616 | tf_op jit(solution)/shard_map/ppermute | solution.py:120
  71.8 5.6 %collective-permute-start.7 = (bf16[2,64,256]{2,1,0:T(8,128)(2,1)S(1)}, bf16[2,64,256]{2,1,0:T(8,128)(2,1)S(1)}, u32[]{:S(2)}, u32[]{:S(2)}) collective-permute-start(bf16[2,64,256]{2,1,0:T(8,128)(2,1)S(1)} %fusion.1), channel_id=1, source_target_pairs={{0,1},{1,0},{2,3},{3,2},{4,5},{5,4},{6,7},{7,6},{8,9},{9,8},{10,11... | collective-permute-start | bytes 196616 | tf_op jit(solution)/shard_map/ppermute | solution.py:120
  73.6 3.8 %copy-start.5 = (bf16[2,64,256]{2,1,0:T(8,128)(2,1)}, bf16[2,64,256]{2,1,0:T(8,128)(2,1)S(1)}, u32[]{:S(2)}) copy-start(bf16[2,64,256]{2,1,0:T(8,128)(2,1)S(1)} %collective-permute-done.17.rest_3_) | copy-start | bytes 196612
  77.0 0.6 copy-start.6
  77.7 0.6 copy-start.7

commit v2 on v0

v2 whole, which is shorter than its diff:
```python
import functools

import jax
import jax.numpy as jnp
from jax import lax
from jax.experimental import pallas as pl
from jax.experimental.pallas import tpu as pltpu
from jax.sharding import PartitionSpec as P

ANY = pl.BlockSpec(memory_space=pl.ANY)
HBM = pl.BlockSpec(memory_space=pltpu.HBM)
SMEM = pl.BlockSpec(memory_space=pltpu.SMEM)
VMEM = pl.BlockSpec(memory_space=pltpu.VMEM)
F32 = jnp.float32
BF16 = jnp.bfloat16


def peer(i, d, n):
    return i ^ d if n & (n - 1) == 0 else (i + d) % n


def back(i, d, n):
    return i ^ d if n & (n - 1) == 0 else (i + n - d) % n


def find(place, nb, left, right):
    block, slot, found = jnp.int32(0), jnp.int32(0), jnp.bool_(False)
    for i in range(nb):
        at = place[left * nb + i]
        hit = lax.div(at, jnp.int32(nb)) == right
        block = jnp.where(hit, jnp.int32(i), block)
        slot = jnp.where(hit, lax.rem(at, jnp.int32(nb)), slot)
        found = found | hit
    return block, slot, found


def chunk(ref, lead, index, rows):
    return ref.at[(*lead, pl.ds(pl.multiple_of(index * rows, rows), rows))]


def run(copies):
    for copy in copies:
        copy.start()
    return copies


def pick_kernel(nsec, nop, nb, place, psi, left_env, *rest):
    outs, sems = rest[:-1], rest[-1]
    me, mine = lax.axis_index("sec"), lax.axis_index("op")
    rows = psi.shape[-2] // nop
    every = slice(None)
    copies = []
    for n in range(nsec - 1):
        piece, others, own = outs[n], outs[nsec - 1 + n], outs[2 * (nsec - 1) + n]
        block, _, _ = find(place, nb, me, peer(me, n + 1, nsec))
        sources = [(chunk(psi, (block, every), mine, rows), piece)]
        for o in range(1, nop):
            at = pl.ds((o - 1) * rows, rows)
            sources.append((chunk(left_env, (every, block), peer(mine, o, nop), rows), others.at[:, at]))
        sources.append((chunk(left_env, (every, block), mine, rows), own))
        for m, (src, dst) in enumerate(sources):
            copies.append(pltpu.make_async_copy(src, dst, sems.at[n, m]))
    for copy in run(copies):
        copy.wait()


def mask_kernel(nsec, nop, nb, place, dims, psi, *rest):
    pieces, out, sems = rest[:nop], rest[nop], rest[nop + 1]
    me, mine = lax.axis_index("sec"), lax.axis_index("op")
    rows, width = out.shape[-2] // nop, out.shape[-1]
    every = slice(None)
    block, _, _ = find(place, nb, me, me)
    copies = [[pltpu.make_async_copy(psi.at[block], out.at[0], sems.at[0, 0])]]
    for d in range(1, nsec):
        copies.append(
            [
                pltpu.make_async_copy(
                    pieces[o].at[d - 1], chunk(out, (d, every), back(mine, o, nop), rows), sems.at[d, o]
                )
                for o in range(nop)
            ]
        )
    for group in copies:
        run(group)
    row = lax.broadcasted_iota(jnp.int32, (width, width), 0)
    col = lax.broadcasted_iota(jnp.int32, (width, width), 1)
    for d in range(nsec):
        source = back(me, d, nsec)
        block, _, found = find(place, nb, source, me)
        live_rows = jnp.where(found, dims[0, source * nb + block], 0)
        live_cols = jnp.where(found, dims[1, source * nb + block], 0)
        alive = (row < live_rows) & (col < live_cols)
        for copy in copies[d]:
            copy.wait()
        for v in range(out.shape[1]):
            out[d, v] = jnp.where(alive, out[d, v], jnp.zeros_like(out[d, v]))


def both(left, masked, right, terms, vecs):
    values = []
    for v in range(vecs):
        value = None
        for k in range(terms):
            trans = jnp.dot(left(k), masked(v), preferred_element_type=F32).astype(BF16)
            term = jnp.dot(trans, right(k), preferred_element_type=F32)
            value = term if value is None else value + term
        values.append(value)
    return values


def others_kernel(rounds, nsec, nop, nb, place, dims, masked, right_env, left_env, *rest):
    count = len(rounds)
    given = count - (0 in rounds)
    lefts, sends, rest = rest[:given], rest[given : given + nop - 1], rest[given + nop - 1 :]
    masked_v, left_v, right_v, sems = rest
    me, mine = lax.axis_index("sec"), lax.axis_index("op")
    terms, vecs, width = left_v.shape[1], masked_v.shape[1], masked_v.shape[-1]
    rows = width // nop
    every = slice(None)
    copies = []
    for e, d in enumerate(rounds):
        block, slot, _ = find(place, nb, back(me, d, nsec), me)
        group = [
            pltpu.make_async_copy(masked.at[d], masked_v.at[e], sems.at[e, 0]),
            pltpu.make_async_copy(right_env.at[:, slot], right_v.at[e], sems.at[e, 1]),
        ]
        if d == 0:
            for o in range(1, nop):
                src = chunk(left_env, (every, block), peer(mine, o, nop), rows)
                dst = left_v.at[e, :, pl.ds((o - 1) * rows, rows)]
                group.append(pltpu.make_async_copy(src, dst, sems.at[e, 1 + o]))
        else:
            group.append(pltpu.make_async_copy(lefts[e - (0 in rounds)], left_v.at[e], sems.at[e, 2]))
        copies.append(run(group))
    row = lax.broadcasted_iota(jnp.int32, (rows, width), 0)
    col = lax.broadcasted_iota(jnp.int32, (rows, width), 1)
    for e, d in enumerate(rounds):
        source = back(me, d, nsec)
        block, _, found = find(place, nb, source, me)
        live_rows = jnp.where(found, dims[0, source * nb + block], 0)
        live_cols = jnp.where(found, dims[1, source * nb + block], 0)
        for copy in copies[e]:
            copy.wait()
        values = both(lambda k: left_v[e, k], lambda v: masked_v[e, v], lambda k: right_v[e, k], terms, vecs)
        for o in range(1, nop):
            alive = (row + peer(mine, o, nop) * rows < live_rows) & (col < live_cols)
            for v in range(vecs):
                part = values[v][(o - 1) * rows : o * rows]
                sends[o - 1][e, v] = jnp.where(alive, part, 0.0).astype(BF16)


def own_kernel(groups, nsec, nop, nb, place, dims, masked, right_env, left_env, *rest):
    lefts, rest = rest[: nsec - 1], rest[nsec - 1 :]
    heard, rest = rest[: len(groups) * (nop - 1)], rest[len(groups) * (nop - 1) :]
    out, masked_v, left_v, right_v, heard_v, sems = rest
    me, mine = lax.axis_index("sec"), lax.axis_index("op")
    terms, vecs, width = left_v.shape[1], masked_v.shape[1], masked_v.shape[-1]
    rows = width // nop
    every = slice(None)
    copies = []
    for d in range(nsec):
        block, slot, _ = find(place, nb, back(me, d, nsec), me)
        left = chunk(left_env, (every, block), mine, rows) if d == 0 else lefts[d - 1]
        copies.append(
            [
                pltpu.make_async_copy(masked.at[d], masked_v.at[d], sems.at[d, 0]),
                pltpu.make_async_copy(right_env.at[:, slot], right_v.at[d], sems.at[d, 1]),
                pltpu.make_async_copy(left, left_v.at[d], sems.at[d, 2]),
            ]
        )
        for g, rounds in enumerate(groups):
            if d in rounds:
                for o in range(nop - 1):
                    src = heard[g * (nop - 1) + o].at[rounds.index(d)]
                    copies[-1].append(pltpu.make_async_copy(src, heard_v.at[d, o], sems.at[d, 3 + o]))
    for group in copies:
        run(group)
    row = lax.broadcasted_iota(jnp.int32, (rows, width), 0) + mine * rows
    col = lax.broadcasted_iota(jnp.int32, (rows, width), 1)
    for d in range(nsec):
        source = back(me, d, nsec)
        block, slot, found = find(place, nb, source, me)
        live_rows = jnp.where(found, dims[0, source * nb + block], 0)
        live_cols = jnp.where(found, dims[1, source * nb + block], 0)
        alive = (row < live_rows) & (col < live_cols)
        for copy in copies[d]:
            copy.wait()
        values = both(lambda k: left_v[d, k], lambda v: masked_v[d, v], lambda k: right_v[d, k], terms, vecs)
        sums = []
        for v in range(vecs):
            value = jnp.where(alive, values[v], 0.0)
            for o in range(nop - 1):
                value = value + heard_v[d, o, v].astype(F32)
            sums.append(value.astype(BF16))

        @pl.when(found)
        def _():
            for v in range(vecs):
                out[slot, v] = sums[v]


def local(psi, left_env, right_env, sector_dims, right_place):
    nsec, nop = lax.axis_size("sec"), lax.axis_size("op")
    nb, vecs, width, _ = psi.shape
    terms = left_env.shape[0]
    rows = width // nop
    away = nsec - 1
    params = pltpu.CompilerParams(vmem_limit_bytes=40 * 2**20)
    shape = lambda *dims: jax.ShapeDtypeStruct(dims, BF16)
    dma = lambda *dims: pltpu.SemaphoreType.DMA(dims)

    def ship(x, axis, d):
        n = lax.axis_size(axis)
        return lax.ppermute(x, axis, [(i, peer(i, d, n)) for i in range(n)])

    def cost(flops, values):
        return pl.CostEstimate(flops=flops, bytes_accessed=2 * values, transcendentals=0)

    picked = pl.pallas_call(
        functools.partial(pick_kernel, nsec, nop, nb),
        in_specs=[SMEM, HBM, HBM],
        out_specs=[VMEM] * (3 * away),
        out_shape=[shape(vecs, rows, width)] * away
        + [shape(terms, width - rows, width)] * away
        + [shape(terms, rows, width)] * away,
        scratch_shapes=[dma(away, nop + 1)],
        compiler_params=params,
        cost_estimate=cost(0, 2 * away * terms * width * width),
        name="pick",
    )(right_place, psi, left_env)

    pieces = [ship(picked[d - 1], "sec", d) for d in range(1, nsec)]
    lefts_others = [ship(picked[away + d - 1], "sec", d) for d in range(1, nsec)]
    lefts_own = [ship(picked[2 * away + d - 1], "sec", d) for d in range(1, nsec)]

    gathered = {0: jnp.stack(pieces)}
    if nop & (nop - 1) == 0:
        bit = nop // 2
        while bit:
            for o in sorted(gathered):
                gathered[o ^ bit] = ship(gathered[o], "op", bit)
            bit //= 2
    else:
        for o in range(1, nop):
            gathered[o] = ship(gathered[0], "op", o)

    masked = pl.pallas_call(
        functools.partial(mask_kernel, nsec, nop, nb),
        in_specs=[SMEM, SMEM, HBM] + [ANY] * nop,
        out_specs=VMEM,
        out_shape=shape(nsec, vecs, width, width),
        scratch_shapes=[dma(nsec, nop)],
        compiler_params=params,
        cost_estimate=cost(0, 2 * nsec * vecs * width * width),
        name="mask",
    )(right_place, sector_dims, psi, *[gathered[o] for o in range(nop)])

    groups = [[0, 1], [2], [3]] if nsec == 4 else [list(range(nsec // 2)), list(range(nsec // 2, nsec))]
    heard = []
    for rounds in groups:
        count = len(rounds)
        given = [lefts_others[d - 1] for d in rounds if d]
        sends = pl.pallas_call(
            functools.partial(others_kernel, rounds, nsec, nop, nb),
            in_specs=[SMEM, SMEM, ANY, HBM, HBM] + [ANY] * len(given),
            out_specs=[VMEM] * (nop - 1),
            out_shape=[shape(count, vecs, rows, width)] * (nop - 1),
            scratch_shapes=[
                pltpu.VMEM((count, vecs, width, width), BF16),
                pltpu.VMEM((count, terms, width - rows, width), BF16),
                pltpu.VMEM((count, terms, width, width), BF16),
                dma(count, nop + 1),
            ],
            compiler_params=params,
            cost_estimate=cost(count * terms * vecs * 3 * width**3, count * width * width * (2 * terms + 2 * vecs)),
            name="others",
        )(right_place, sector_dims, masked, right_env, left_env, *given)
        heard += [ship(sends[o - 1], "op", o) for o in range(1, nop)]

    return pl.pallas_call(
        functools.partial(own_kernel, groups, nsec, nop, nb),
        in_specs=[SMEM, SMEM, ANY, HBM, HBM] + [ANY] * (away + len(heard)),
        out_specs=VMEM,
        out_shape=shape(nb, vecs, rows, width),
        scratch_shapes=[
            pltpu.VMEM((nsec, vecs, width, width), BF16),
            pltpu.VMEM((nsec, terms, rows, width), BF16),
            pltpu.VMEM((nsec, terms, width, width), BF16),
            pltpu.VMEM((nsec, nop - 1, vecs, rows, width), BF16),
            dma(nsec, nop + 2),
        ],
        compiler_params=params,
        cost_estimate=cost(nsec * terms * vecs * width**3, nsec * width * width * (2 * terms + 2 * vecs)),
        name="own",
    )(right_place, sector_dims, masked, right_env, left_env, *lefts_own, *heard)


def solution(mesh):
    return jax.shard_map(
        local,
        mesh=mesh,
        in_specs=(
            P(("grp", "sec"), None, None, None),
            P("op", ("grp", "sec"), None, None),
            P("op", ("grp", "sec"), None, None),
            P(None, "grp"),
            P("grp"),
        ),
        out_specs=P(("grp", "sec"), None, "op", None),
        check_vma=False,
    )
```

time: 119 us -> 66.3 us (0.56)
  the two profiles are of different devices: /device:TPU:0 before, /device:TPU:9 now
where the time goes in v2:
time: 66.3 us; the launch traced here: 66.1 us
  starting transfers between devices  25.5 us (38%)
  waiting for transfers between devices  24.3 us (37%)
  Pallas kernels  13.1 us (20%)
  local copies, waits for them, and re-layouts  3.11 us (5%)
    ppermute x21, starting transfers between devices, ship(): return lax.ppermute(x, axis, [(i, peer(i, d, n)) for i in range(n)])  25.5 us
    ppermute x21, waiting for transfers between devices, ship(): return lax.ppermute(x, axis, [(i, peer(i, d, n)) for i in range(n)])  24.3 us
    pallas_call x3, Pallas kernels, local(): pl.pallas_call(functools.partial(others_kernel, rounds, nsec, nop, nb), i...  5.14 us
    pallas_call x1, Pallas kernels, local(): pl.pallas_call(functools.partial(own_kernel, groups, nsec, nop, nb), in_s...  5.01 us
    unnamed x12, local copies, waits for them, and re-layouts  3.11 us
    pallas_call x1, Pallas kernels, local(): pl.pallas_call(functools.partial(mask_kernel, nsec, nop, nb), in_specs=[S...  1.53 us
    pallas_call x1, Pallas kernels, local(): pl.pallas_call(functools.partial(pick_kernel, nsec, nop, nb), in_specs=[S...  1.38 us
  transfers between devices with their start and end apart: 21, of which 9 were waited for; matrix products, arithmetic and copies ran while one was open for 0% of the time, Pallas kernels for 10%

profile of v2, /device:TPU:9, one launch (start us, length us, event | category | flops | bytes accessed | tf_op | source)
XLA Modules:
  0.0 66.1 jit_solution(12878258097636090120)
XLA Ops:
  0.0 0.0 copy-start
  0.0 1.2 %copy-done = bf16[2,4,256,256]{3,2,1,0:T(8,128)(2,1)S(1)} copy-done((bf16[2,4,256,256]{3,2,1,0:T(8,128)(2,1)S(1)}, bf16[2,4,256,256]{3,2,1,0:T(8,128)(2,1)}, u32[]{:S(2)}) %copy-start) | copy-done | bytes 1048600
  1.2 0.0 copy-start.3
  1.2 1.2 %copy-done.3 = bf16[4,2,256,256]{3,2,1,0:T(8,128)(2,1)S(1)} copy-done((bf16[4,2,256,256]{3,2,1,0:T(8,128)(2,1)S(1)}, bf16[4,2,256,256]{3,2,1,0:T(8,128)(2,1)}, u32[]{:S(2)}) %copy-start.3) | copy-done | bytes 1048600
  2.5 0.0 copy-start.5
  2.5 0.7 copy-done.5
  3.1 1.4 %pick.1 = (bf16[2,64,256]{2,1,0:T(8,128)(2,1)S(1)}, bf16[2,64,256]{2,1,0:T(8,128)(2,1)S(1)}, bf16[2,64,256]{2,1,0:T(8,128)(2,1)S(1)}, bf16[2,192,256]{2,1,0:T(8,...) custom-call(s32[16]{0:T(128)S(1)} %copy-done.5, ...), custom_call_target="tpu_custom_call" | custom-call | bytes 1572864 | tf_op jit(solution)/shard_map/pick/pallas_call | solution.py:219
  4.5 0.1 collective-permute-start
  4.6 2.5 %collective-permute-start.1 = (bf16[2,64,256]{2,1,0:T(8,128)(2,1)S(1)}, bf16[2,64,256]{2,1,0:T(8,128)(2,1)S(1)}, u32[]{:S(2)}, u32[]{:S(2)}) collective-permute-start(bf16[2,64,256]{2,1,0:T(8,128)(2,1)S(1)} %get-tuple-element.24), channel_id=1, source_target_pairs={{0,2},{1,3},{2,0},{3,1},{4,6},{5,7},{6,4},{7,5},{8,10},{9,11},{10,... | collective-permute-start | bytes 196616 | tf_op jit(solution)/shard_map/ppermute | solution.py:214
  7.0 0.2 collective-permute-start.2
  7.2 0.5 collective-permute-done
  7.7 2.0 %collective-permute-done.1 = bf16[2,64,256]{2,1,0:T(8,128)(2,1)S(1)} collective-permute-done((bf16[2,64,256]{2,1,0:T(8,128)(2,1)S(1)}, bf16[2,64,256]{2,1,0:T(8,128)(2,1)S(1)}, u32[]{:S(2)}, u32[]{:S(2)}) %collective-permute-start.1) | collective-permute-done | bytes 65568 | tf_op jit(solution)/shard_map/ppermute | solution.py:214
  9.6 2.6 %collective-permute-done.2 = bf16[2,64,256]{2,1,0:T(8,128)(2,1)S(1)} collective-permute-done((bf16[2,64,256]{2,1,0:T(8,128)(2,1)S(1)}, bf16[2,64,256]{2,1,0:T(8,128)(2,1)S(1)}, u32[]{:S(2)}, u32[]{:S(2)}) %collective-permute-start.2) | collective-permute-done | bytes 65568 | tf_op jit(solution)/shard_map/ppermute | solution.py:214
  12.3 1.3 %collective-permute-start.4 = (bf16[3,2,64,256]{3,2,1,0:T(8,128)(2,1)S(1)}, bf16[3,2,64,256]{3,2,1,0:T(8,128)(2,1)S(1)}, u32[]{:S(2)}, u32[]{:S(2)}) collective-permute-start(bf16[3,2,64,256]{3,2,1,0:T(8,128)(2,1)S(1)} %pad_maximum_fusion.rest_0_), channel_id=1, source_target_pairs={{0,8},{4,12},{8,0},{12,4},{1,9},{5,13},{9,1},{13,5},{2,10},{6,14},... | collective-permute-start | bytes 589832 | tf_op jit(solution)/shard_map/ppermute | solution.py:214
  13.6 1.8 %collective-permute-start.3 = (bf16[3,2,64,256]{3,2,1,0:T(8,128)(2,1)S(1)}, bf16[3,2,64,256]{3,2,1,0:T(8,128)(2,1)S(1)}, u32[]{:S(2)}, u32[]{:S(2)}) collective-permute-start(bf16[3,2,64,256]{3,2,1,0:T(8,128)(2,1)S(1)} %pad_maximum_fusion.rest_0_), channel_id=1, source_target_pairs={{0,4},{4,0},{8,12},{12,8},{1,5},{5,1},{9,13},{13,9},{2,6},{6,2},{1... | collective-permute-start | bytes 589832 | tf_op jit(solution)/shard_map/ppermute | solution.py:214
  15.4 1.9 %collective-permute-done.4.rest_2_ = bf16[3,2,64,256]{3,2,1,0:T(8,128)(2,1)S(1)} collective-permute-done((bf16[3,2,64,256]{3,2,1,0:T(8,128)(2,1)S(1)}, bf16[3,2,64,256]{3,2,1,0:T(8,128)(2,1)S(1)}, u32[]{:S(2)}, u32[]{:S(2)}) %collective-permute-start.4) | collective-permute-done | bytes 196640 | tf_op jit(solution)/shard_map/ppermute | solution.py:214
  17.2 2.4 %collective-permute-start.5 = (bf16[3,2,64,256]{3,2,1,0:T(8,128)(2,1)S(1)}, bf16[3,2,64,256]{3,2,1,0:T(8,128)(2,1)S(1)}, u32[]{:S(2)}, u32[]{:S(2)}) collective-permute-start(bf16[3,2,64,256]{3,2,1,0:T(8,128)(2,1)S(1)} %collective-permute-done.4.rest_2_), channel_id=1, source_target_pairs={{0,4},{4,0},{8,12},{12,8},{1,5},{5,1},{9,13},{13,9},{2,6},{6,2},{1... | collective-permute-start | bytes 589832 | tf_op jit(solution)/shard_map/ppermute | solution.py:214
  19.7 2.0 %collective-permute-start.13 = (bf16[2,192,256]{2,1,0:T(8,128)(2,1)S(1)}, bf16[2,192,256]{2,1,0:T(8,128)(2,1)S(1)}, u32[]{:S(2)}, u32[]{:S(2)}) collective-permute-start(bf16[2,192,256]{2,1,0:T(8,128)(2,1)S(1)} %get-tuple-element.33), channel_id=1, source_target_pairs={{0,2},{1,3},{2,0},{3,1},{4,6},{5,7},{6,4},{7,5},{8,10},{9,11},{10,... | collective-permute-start | bytes 589832 | tf_op jit(solution)/shard_map/ppermute | solution.py:214
  21.7 1.0 %collective-permute-start.9 = (bf16[2,192,256]{2,1,0:T(8,128)(2,1)S(1)}, bf16[2,192,256]{2,1,0:T(8,128)(2,1)S(1)}, u32[]{:S(2)}, u32[]{:S(2)}) collective-permute-start(bf16[2,192,256]{2,1,0:T(8,128)(2,1)S(1)} %get-tuple-element.29), channel_id=1, source_target_pairs={{0,1},{1,0},{2,3},{3,2},{4,5},{5,4},{6,7},{7,6},{8,9},{9,8},{10,11... | collective-permute-start | bytes 589832 | tf_op jit(solution)/shard_map/ppermute | solution.py:214
  22.7 0.0 collective-permute-start.17
  22.7 0.0 collective-permute-done.3.rest_1_
  22.7 0.0 copy-start.4
  22.7 2.2 %collective-permute-start.6 = (bf16[2,64,256]{2,1,0:T(8,128)(2,1)S(1)}, bf16[2,64,256]{2,1,0:T(8,128)(2,1)S(1)}, u32[]{:S(2)}, u32[]{:S(2)}) collective-permute-start(bf16[2,64,256]{2,1,0:T(8,128)(2,1)S(1)} %get-tuple-element.26), channel_id=1, source_target_pairs={{0,1},{1,0},{2,3},{3,2},{4,5},{5,4},{6,7},{7,6},{8,9},{9,8},{10,11... | collective-permute-start | bytes 196616 | tf_op jit(solution)/shard_map/ppermute | solution.py:214
  25.0 0.0 collective-permute-done.5.rest_3_
  25.0 0.0 copy-start.1
  25.0 0.0 copy-start.2
  25.0 0.4 collective-permute-start.7
  25.4 0.0 copy-done.4
  25.4 1.5 %mask.1.masked = bf16[4,2,256,256]{3,2,1,0:T(8,128)(2,1)S(1)} custom-call(s32[16]{0:T(128)S(1)} %copy-done.5, s32[2,16]{1,0:T(2,128)S(1)} %copy-done.4, bf16[4,2,256,256]{3,2,1,0:T(8,128)(2,1)S(1)} %copy-done.3, bf16[3,2,64,256]{3,2,1,0:T(8,128)(2,1)S(1)} %pad_maximum_fusion.rest_0_, bf16[3,2,64,256]{3,2,1,0:T(8,128)(2,1)S(1)} %collective-permute-done.3.rest_1_, ...), custom_call_target="tpu_custom_call" | custom-call | bytes 2097152 | tf_op jit(solution)/shard_map/mask/pallas_call | solution.py:247
  27.0 3.4 %collective-permute-done.13.rest_0_ = bf16[2,192,256]{2,1,0:T(8,128)(2,1)S(1)} collective-permute-done((bf16[2,192,256]{2,1,0:T(8,128)(2,1)S(1)}, bf16[2,192,256]{2,1,0:T(8,128)(2,1)S(1)}, u32[]{:S(2)}, u32[]{:S(2)}) %collective-permute-start.13) | collective-permute-done | bytes 196640 | tf_op jit(solution)/shard_map/ppermute | solution.py:214
  30.3 0.5 collective-permute-start.8
  30.9 0.0 copy-done.1
  30.9 0.0 copy-done.2
  30.9 1.5 %others.4 = (bf16[1,2,64,256]{3,2,1,0:T(8,128)(2,1)S(1)}, bf16[1,2,64,256]{3,2,1,0:T(8,128)(2,1)S(1)}, bf16[1,2,64,256]{3,2,1,0:T(8,128)(2,1)S(1)}) custom-call(s32[16]{0:T(128)S(1)} %copy-done.5, s32[2,16]{1,0:T(2,128)S(1)} %copy-done.4, bf16[4,2,256,256]{3,2,1,0:T(8,128)(2,1)S(1)} %mask.1.masked, bf16[2,4,256,256]{3,2,1,0:T(8,128)(2,1)S(1)} %copy-done.2, ...), custom_call_target="tpu_custom_call" | custom-call | flops 201326592 | bytes 1048576 | tf_op jit(solution)/shard_map/others/pallas_call | solution.py:263
  32.3 0.0 collective-permute-done.9.rest_0_
  32.3 4.5 %collective-permute-start.14 = (bf16[1,2,64,256]{3,2,1,0:T(8,128)(2,1)S(1)}, bf16[1,2,64,256]{3,2,1,0:T(8,128)(2,1)S(1)}, u32[]{:S(2)}, u32[]{:S(2)}) collective-permute-start(bf16[1,2,64,256]{3,2,1,0:T(8,128)(2,1)S(1)} %get-tuple-element.34), channel_id=1, source_target_pairs={{0,4},{4,0},{8,12},{12,8},{1,5},{5,1},{9,13},{13,9},{2,6},{6,2},{1... | collective-permute-start | bytes 196616 | tf_op jit(solution)/shard_map/ppermute | solution.py:214
  36.9 6.1 %collective-permute-done.17.rest_0_ = bf16[2,192,256]{2,1,0:T(8,128)(2,1)S(1)} collective-permute-done((bf16[2,192,256]{2,1,0:T(8,128)(2,1)S(1)}, bf16[2,192,256]{2,1,0:T(8,128)(2,1)S(1)}, u32[]{:S(2)}, u32[]{:S(2)}) %collective-permute-start.17) | collective-permute-done | bytes 196640 | tf_op jit(solution)/shard_map/ppermute | solution.py:214
  43.0 1.2 %collective-permute-start.15 = (bf16[1,2,64,256]{3,2,1,0:T(8,128)(2,1)S(1)}, bf16[1,2,64,256]{3,2,1,0:T(8,128)(2,1)S(1)}, u32[]{:S(2)}, u32[]{:S(2)}) collective-permute-start(bf16[1,2,64,256]{3,2,1,0:T(8,128)(2,1)S(1)} %get-tuple-element.35), channel_id=1, source_target_pairs={{0,8},{4,12},{8,0},{12,4},{1,9},{5,13},{9,1},{13,5},{2,10},{6,14},... | collective-permute-start | bytes 196616 | tf_op jit(solution)/shard_map/ppermute | solution.py:214
  44.2 1.5 %others.5 = (bf16[1,2,64,256]{3,2,1,0:T(8,128)(2,1)S(1)}, bf16[1,2,64,256]{3,2,1,0:T(8,128)(2,1)S(1)}, bf16[1,2,64,256]{3,2,1,0:T(8,128)(2,1)S(1)}) custom-call(s32[16]{0:T(128)S(1)} %copy-done.5, s32[2,16]{1,0:T(2,128)S(1)} %copy-done.4, bf16[4,2,256,256]{3,2,1,0:T(8,128)(2,1)S(1)} %mask.1.masked, bf16[2,4,256,256]{3,2,1,0:T(8,128)(2,1)S(1)} %copy-done.2, ...), custom_call_target="tpu_custom_call" | custom-call | flops 201326592 | bytes 1048576 | tf_op jit(solution)/shard_map/others/pallas_call | solution.py:263
  45.6 2.2 %others.3 = (bf16[2,2,64,256]{3,2,1,0:T(8,128)(2,1)S(1)}, bf16[2,2,64,256]{3,2,1,0:T(8,128)(2,1)S(1)}, bf16[2,2,64,256]{3,2,1,0:T(8,128)(2,1)S(1)}) custom-call(s32[16]{0:T(128)S(1)} %copy-done.5, s32[2,16]{1,0:T(2,128)S(1)} %copy-done.4, bf16[4,2,256,256]{3,2,1,0:T(8,128)(2,1)S(1)} %mask.1.masked, bf16[2,4,256,256]{3,2,1,0:T(8,128)(2,1)S(1)} %copy-done.2, ...), custom_call_target="tpu_custom_call" | custom-call | flops 402653184 | bytes 2097152 | tf_op jit(solution)/shard_map/others/pallas_call | solution.py:263
  47.9 0.0 collective-permute-done.6.rest_0_
  47.9 1.0 %collective-permute-start.16 = (bf16[1,2,64,256]{3,2,1,0:T(8,128)(2,1)S(1)}, bf16[1,2,64,256]{3,2,1,0:T(8,128)(2,1)S(1)}, u32[]{:S(2)}, u32[]{:S(2)}) collective-permute-start(bf16[1,2,64,256]{3,2,1,0:T(8,128)(2,1)S(1)} %get-tuple-element.36), channel_id=1, source_target_pairs={{0,12},{4,8},{8,4},{12,0},{1,13},{5,9},{9,5},{13,1},{2,14},{6,10},... | collective-permute-start | bytes 196616 | tf_op jit(solution)/shard_map/ppermute | solution.py:214
  48.8 0.0 collective-permute-done.7.rest_1_
  48.8 0.0 collective-permute-start.18
  48.8 0.0 collective-permute-done.8.rest_2_
  48.8 0.5 collective-permute-start.10
  49.4 0.0 collective-permute-done.14.rest_6_
  49.4 1.2 %collective-permute-start.11 = (bf16[2,2,64,256]{3,2,1,0:T(8,128)(2,1)S(1)}, bf16[2,2,64,256]{3,2,1,0:T(8,128)(2,1)S(1)}, u32[]{:S(2)}, u32[]{:S(2)}) collective-permute-start(bf16[2,2,64,256]{3,2,1,0:T(8,128)(2,1)S(1)} %get-tuple-element.31), channel_id=1, source_target_pairs={{0,8},{4,12},{8,0},{12,4},{1,9},{5,13},{9,1},{13,5},{2,10},{6,14},... | collective-permute-start | bytes 393224 | tf_op jit(solution)/shard_map/ppermute | solution.py:214
  50.6 0.0 collective-permute-done.15.rest_7_
  50.6 0.5 collective-permute-start.12
  51.1 1.5 %collective-permute-done.16.rest_8_ = bf16[1,2,64,256]{3,2,1,0:T(8,128)(2,1)S(1)} collective-permute-done((bf16[1,2,64,256]{3,2,1,0:T(8,128)(2,1)S(1)}, bf16[1,2,64,256]{3,2,1,0:T(8,128)(2,1)S(1)}, u32[]{:S(2)}, u32[]{:S(2)}) %collective-permute-start.16) | collective-permute-done | bytes 65568 | tf_op jit(solution)/shard_map/ppermute | solution.py:214
  52.6 0.3 collective-permute-start.19
  52.9 0.0 collective-permute-done.18.rest_9_
  52.9 1.8 %collective-permute-start.20 = (bf16[1,2,64,256]{3,2,1,0:T(8,128)(2,1)S(1)}, bf16[1,2,64,256]{3,2,1,0:T(8,128)(2,1)S(1)}, u32[]{:S(2)}, u32[]{:S(2)}) collective-permute-start(bf16[1,2,64,256]{3,2,1,0:T(8,128)(2,1)S(1)} %get-tuple-element.40), channel_id=1, source_target_pairs={{0,12},{4,8},{8,4},{12,0},{1,13},{5,9},{9,5},{13,1},{2,14},{6,10},... | collective-permute-start | bytes 196616 | tf_op jit(solution)/shard_map/ppermute | solution.py:214
  54.7 5.0 %collective-permute-done.19.rest_10_ = bf16[1,2,64,256]{3,2,1,0:T(8,128)(2,1)S(1)} collective-permute-done((bf16[1,2,64,256]{3,2,1,0:T(8,128)(2,1)S(1)}, bf16[1,2,64,256]{3,2,1,0:T(8,128)(2,1)S(1)}, u32[]{:S(2)}, u32[]{:S(2)}) %collective-permute-start.19) | collective-permute-done | bytes 65568 | tf_op jit(solution)/shard_map/ppermute | solution.py:214
  59.6 1.4 %collective-permute-done.20.rest_11_ = bf16[1,2,64,256]{3,2,1,0:T(8,128)(2,1)S(1)} collective-permute-done((bf16[1,2,64,256]{3,2,1,0:T(8,128)(2,1)S(1)}, bf16[1,2,64,256]{3,2,1,0:T(8,128)(2,1)S(1)}, u32[]{:S(2)}, u32[]{:S(2)}) %collective-permute-start.20) | collective-permute-done | bytes 65568 | tf_op jit(solution)/shard_map/ppermute | solution.py:214
  61.0 0.0 collective-permute-done.10.rest_3_
  61.1 0.0 collective-permute-done.11.rest_4_
  61.1 0.0 collective-permute-done.12.rest_5_
  61.1 5.0 %own.1 = bf16[4,2,64,256]{3,2,1,0:T(8,128)(2,1)} custom-call(s32[16]{0:T(128)S(1)} %copy-done.5, s32[2,16]{1,0:T(2,128)S(1)} %copy-done.4, bf16[4,2,256,256]{3,2,1,0:T(8,128)(2,1)S(1)} %mask.1.masked, bf16[2,4,256,256]{3,2,1,0:T(8,128)(2,1)S(1)} %copy-done.2, bf16[2,4,256,256]{3,2,1,0:T(8,128)(2,1)S(1)} %copy-done.1, ...), custom_call_target="tpu_custom_call" | custom-call | flops 268435456 | bytes 4194304 | tf_op jit(solution)/shard_map/own/pallas_call | solution.py:280
  (1 shorter events, 0.0 us)
Async XLA Ops:
  0.0 1.2 %copy-start = (bf16[2,4,256,256]{3,2,1,0:T(8,128)(2,1)S(1)}, bf16[2,4,256,256]{3,2,1,0:T(8,128)(2,1)}, u32[]{:S(2)}) copy-start(bf16[2,4,256,256]{3,2,1,0:T(8,128)(2,1)} %left_env.9) | copy-start | bytes 3145732
  1.2 1.2 %copy-start.3 = (bf16[4,2,256,256]{3,2,1,0:T(8,128)(2,1)S(1)}, bf16[4,2,256,256]{3,2,1,0:T(8,128)(2,1)}, u32[]{:S(2)}) copy-start(bf16[4,2,256,256]{3,2,1,0:T(8,128)(2,1)} %psi.3) | copy-start | bytes 3145732
  2.5 0.7 copy-start.5
  4.5 3.2 %collective-permute-start = (bf16[2,64,256]{2,1,0:T(8,128)(2,1)S(1)}, bf16[2,64,256]{2,1,0:T(8,128)(2,1)S(1)}, u32[]{:S(2)}, u32[]{:S(2)}) collective-permute-start(bf16[2,64,256]{2,1,0:T(8,128)(2,1)S(1)} %get-tuple-element.23), channel_id=1, source_target_pairs={{0,1},{1,0},{2,3},{3,2},{4,5},{5,4},{6,7},{7,6},{8,9},{9,8},{10,11... | collective-permute-start | bytes 196616 | tf_op jit(solution)/shard_map/ppermute | solution.py:214
  4.6 5.1 %collective-permute-start.1 = (bf16[2,64,256]{2,1,0:T(8,128)(2,1)S(1)}, bf16[2,64,256]{2,1,0:T(8,128)(2,1)S(1)}, u32[]{:S(2)}, u32[]{:S(2)}) collective-permute-start(bf16[2,64,256]{2,1,0:T(8,128)(2,1)S(1)} %get-tuple-element.24), channel_id=1, source_target_pairs={{0,2},{1,3},{2,0},{3,1},{4,6},{5,7},{6,4},{7,5},{8,10},{9,11},{10,... | collective-permute-start | bytes 196616 | tf_op jit(solution)/shard_map/ppermute | solution.py:214
  7.0 5.2 %collective-permute-start.2 = (bf16[2,64,256]{2,1,0:T(8,128)(2,1)S(1)}, bf16[2,64,256]{2,1,0:T(8,128)(2,1)S(1)}, u32[]{:S(2)}, u32[]{:S(2)}) collective-permute-start(bf16[2,64,256]{2,1,0:T(8,128)(2,1)S(1)} %get-tuple-element.25), channel_id=1, source_target_pairs={{0,3},{1,2},{2,1},{3,0},{4,7},{5,6},{6,5},{7,4},{8,11},{9,10},{10,... | collective-permute-start | bytes 196616 | tf_op jit(solution)/shard_map/ppermute | solution.py:214
  12.3 5.0 %collective-permute-start.4 = (bf16[3,2,64,256]{3,2,1,0:T(8,128)(2,1)S(1)}, bf16[3,2,64,256]{3,2,1,0:T(8,128)(2,1)S(1)}, u32[]{:S(2)}, u32[]{:S(2)}) collective-permute-start(bf16[3,2,64,256]{3,2,1,0:T(8,128)(2,1)S(1)} %pad_maximum_fusion.rest_0_), channel_id=1, source_target_pairs={{0,8},{4,12},{8,0},{12,4},{1,9},{5,13},{9,1},{13,5},{2,10},{6,14},... | collective-permute-start | bytes 589832 | tf_op jit(solution)/shard_map/ppermute | solution.py:214
  13.6 9.1 %collective-permute-start.3 = (bf16[3,2,64,256]{3,2,1,0:T(8,128)(2,1)S(1)}, bf16[3,2,64,256]{3,2,1,0:T(8,128)(2,1)S(1)}, u32[]{:S(2)}, u32[]{:S(2)}) collective-permute-start(bf16[3,2,64,256]{3,2,1,0:T(8,128)(2,1)S(1)} %pad_maximum_fusion.rest_0_), channel_id=1, source_target_pairs={{0,4},{4,0},{8,12},{12,8},{1,5},{5,1},{9,13},{13,9},{2,6},{6,2},{1... | collective-permute-start | bytes 589832 | tf_op jit(solution)/shard_map/ppermute | solution.py:214
  17.2 7.7 %collective-permute-start.5 = (bf16[3,2,64,256]{3,2,1,0:T(8,128)(2,1)S(1)}, bf16[3,2,64,256]{3,2,1,0:T(8,128)(2,1)S(1)}, u32[]{:S(2)}, u32[]{:S(2)}) collective-permute-start(bf16[3,2,64,256]{3,2,1,0:T(8,128)(2,1)S(1)} %collective-permute-done.4.rest_2_), channel_id=1, source_target_pairs={{0,4},{4,0},{8,12},{12,8},{1,5},{5,1},{9,13},{13,9},{2,6},{6,2},{1... | collective-permute-start | bytes 589832 | tf_op jit(solution)/shard_map/ppermute | solution.py:214
  19.7 10.6 %collective-permute-start.13 = (bf16[2,192,256]{2,1,0:T(8,128)(2,1)S(1)}, bf16[2,192,256]{2,1,0:T(8,128)(2,1)S(1)}, u32[]{:S(2)}, u32[]{:S(2)}) collective-permute-start(bf16[2,192,256]{2,1,0:T(8,128)(2,1)S(1)} %get-tuple-element.33), channel_id=1, source_target_pairs={{0,2},{1,3},{2,0},{3,1},{4,6},{5,7},{6,4},{7,5},{8,10},{9,11},{10,... | collective-permute-start | bytes 589832 | tf_op jit(solution)/shard_map/ppermute | solution.py:214
  21.7 10.6 %collective-permute-start.9 = (bf16[2,192,256]{2,1,0:T(8,128)(2,1)S(1)}, bf16[2,192,256]{2,1,0:T(8,128)(2,1)S(1)}, u32[]{:S(2)}, u32[]{:S(2)}) collective-permute-start(bf16[2,192,256]{2,1,0:T(8,128)(2,1)S(1)} %get-tuple-element.29), channel_id=1, source_target_pairs={{0,1},{1,0},{2,3},{3,2},{4,5},{5,4},{6,7},{7,6},{8,9},{9,8},{10,11... | collective-permute-start | bytes 589832 | tf_op jit(solution)/shard_map/ppermute | solution.py:214
  22.7 20.2 %collective-permute-start.17 = (bf16[2,192,256]{2,1,0:T(8,128)(2,1)S(1)}, bf16[2,192,256]{2,1,0:T(8,128)(2,1)S(1)}, u32[]{:S(2)}, u32[]{:S(2)}) collective-permute-start(bf16[2,192,256]{2,1,0:T(8,128)(2,1)S(1)} %get-tuple-element.37), channel_id=1, source_target_pairs={{0,3},{1,2},{2,1},{3,0},{4,7},{5,6},{6,5},{7,4},{8,11},{9,10},{10,... | collective-permute-start | bytes 589832 | tf_op jit(solution)/shard_map/ppermute | solution.py:214
  22.7 2.7 %copy-start.4 = (s32[2,16]{1,0:T(2,128)S(1)}, s32[2,16]{1,0:T(2,128)}, u32[]{:S(2)}) copy-start(s32[2,16]{1,0:T(2,128)} %dims.9) | copy-start | bytes 388
  22.7 25.1 %collective-permute-start.6 = (bf16[2,64,256]{2,1,0:T(8,128)(2,1)S(1)}, bf16[2,64,256]{2,1,0:T(8,128)(2,1)S(1)}, u32[]{:S(2)}, u32[]{:S(2)}) collective-permute-start(bf16[2,64,256]{2,1,0:T(8,128)(2,1)S(1)} %get-tuple-element.26), channel_id=1, source_target_pairs={{0,1},{1,0},{2,3},{3,2},{4,5},{5,4},{6,7},{7,6},{8,9},{9,8},{10,11... | collective-permute-start | bytes 196616 | tf_op jit(solution)/shard_map/ppermute | solution.py:214
  25.0 5.9 %copy-start.1 = (bf16[2,4,256,256]{3,2,1,0:T(8,128)(2,1)S(1)}, bf16[2,4,256,256]{3,2,1,0:T(8,128)(2,1)}, u32[]{:S(2)}) copy-start(bf16[2,4,256,256]{3,2,1,0:T(8,128)(2,1)} %left_env.9) | copy-start | bytes 3145732
  25.0 5.9 %copy-start.2 = (bf16[2,4,256,256]{3,2,1,0:T(8,128)(2,1)S(1)}, bf16[2,4,256,256]{3,2,1,0:T(8,128)(2,1)}, u32[]{:S(2)}) copy-start(bf16[2,4,256,256]{3,2,1,0:T(8,128)(2,1)} %right_env.7) | copy-start | bytes 3145732
  25.0 23.9 %collective-permute-start.7 = (bf16[2,64,256]{2,1,0:T(8,128)(2,1)S(1)}, bf16[2,64,256]{2,1,0:T(8,128)(2,1)S(1)}, u32[]{:S(2)}, u32[]{:S(2)}) collective-permute-start(bf16[2,64,256]{2,1,0:T(8,128)(2,1)S(1)} %get-tuple-element.27), channel_id=1, source_target_pairs={{0,2},{1,3},{2,0},{3,1},{4,6},{5,7},{6,4},{7,5},{8,10},{9,11},{10,... | collective-permute-start | bytes 196616 | tf_op jit(solution)/shard_map/ppermute | solution.py:214
  30.3 18.5 %collective-permute-start.8 = (bf16[2,64,256]{2,1,0:T(8,128)(2,1)S(1)}, bf16[2,64,256]{2,1,0:T(8,128)(2,1)S(1)}, u32[]{:S(2)}, u32[]{:S(2)}) collective-permute-start(bf16[2,64,256]{2,1,0:T(8,128)(2,1)S(1)} %get-tuple-element.28), channel_id=1, source_target_pairs={{0,3},{1,2},{2,1},{3,0},{4,7},{5,6},{6,5},{7,4},{8,11},{9,10},{10,... | collective-permute-start | bytes 196616 | tf_op jit(solution)/shard_map/ppermute | solution.py:214
  32.3 17.0 %collective-permute-start.14 = (bf16[1,2,64,256]{3,2,1,0:T(8,128)(2,1)S(1)}, bf16[1,2,64,256]{3,2,1,0:T(8,128)(2,1)S(1)}, u32[]{:S(2)}, u32[]{:S(2)}) collective-permute-start(bf16[1,2,64,256]{3,2,1,0:T(8,128)(2,1)S(1)} %get-tuple-element.34), channel_id=1, source_target_pairs={{0,4},{4,0},{8,12},{12,8},{1,5},{5,1},{9,13},{13,9},{2,6},{6,2},{1... | collective-permute-start | bytes 196616 | tf_op jit(solution)/shard_map/ppermute | solution.py:214
  43.0 7.6 %collective-permute-start.15 = (bf16[1,2,64,256]{3,2,1,0:T(8,128)(2,1)S(1)}, bf16[1,2,64,256]{3,2,1,0:T(8,128)(2,1)S(1)}, u32[]{:S(2)}, u32[]{:S(2)}) collective-permute-start(bf16[1,2,64,256]{3,2,1,0:T(8,128)(2,1)S(1)} %get-tuple-element.35), channel_id=1, source_target_pairs={{0,8},{4,12},{8,0},{12,4},{1,9},{5,13},{9,1},{13,5},{2,10},{6,14},... | collective-permute-start | bytes 196616 | tf_op jit(solution)/shard_map/ppermute | solution.py:214
  47.9 4.7 %collective-permute-start.16 = (bf16[1,2,64,256]{3,2,1,0:T(8,128)(2,1)S(1)}, bf16[1,2,64,256]{3,2,1,0:T(8,128)(2,1)S(1)}, u32[]{:S(2)}, u32[]{:S(2)}) collective-permute-start(bf16[1,2,64,256]{3,2,1,0:T(8,128)(2,1)S(1)} %get-tuple-element.36), channel_id=1, source_target_pairs={{0,12},{4,8},{8,4},{12,0},{1,13},{5,9},{9,5},{13,1},{2,14},{6,10},... | collective-permute-start | bytes 196616 | tf_op jit(solution)/shard_map/ppermute | solution.py:214
  48.8 4.1 %collective-permute-start.18 = (bf16[1,2,64,256]{3,2,1,0:T(8,128)(2,1)S(1)}, bf16[1,2,64,256]{3,2,1,0:T(8,128)(2,1)S(1)}, u32[]{:S(2)}, u32[]{:S(2)}) collective-permute-start(bf16[1,2,64,256]{3,2,1,0:T(8,128)(2,1)S(1)} %get-tuple-element.38), channel_id=1, source_target_pairs={{0,4},{4,0},{8,12},{12,8},{1,5},{5,1},{9,13},{13,9},{2,6},{6,2},{1... | collective-permute-start | bytes 196616 | tf_op jit(solution)/shard_map/ppermute | solution.py:214
  48.8 12.2 %collective-permute-start.10 = (bf16[2,2,64,256]{3,2,1,0:T(8,128)(2,1)S(1)}, bf16[2,2,64,256]{3,2,1,0:T(8,128)(2,1)S(1)}, u32[]{:S(2)}, u32[]{:S(2)}) collective-permute-start(bf16[2,2,64,256]{3,2,1,0:T(8,128)(2,1)S(1)} %get-tuple-element.30), channel_id=1, source_target_pairs={{0,4},{4,0},{8,12},{12,8},{1,5},{5,1},{9,13},{13,9},{2,6},{6,2},{1... | collective-permute-start | bytes 393224 | tf_op jit(solution)/shard_map/ppermute | solution.py:214
  49.4 11.7 %collective-permute-start.11 = (bf16[2,2,64,256]{3,2,1,0:T(8,128)(2,1)S(1)}, bf16[2,2,64,256]{3,2,1,0:T(8,128)(2,1)S(1)}, u32[]{:S(2)}, u32[]{:S(2)}) collective-permute-start(bf16[2,2,64,256]{3,2,1,0:T(8,128)(2,1)S(1)} %get-tuple-element.31), channel_id=1, source_target_pairs={{0,8},{4,12},{8,0},{12,4},{1,9},{5,13},{9,1},{13,5},{2,10},{6,14},... | collective-permute-start | bytes 393224 | tf_op jit(solution)/shard_map/ppermute | solution.py:214
  50.6 10.5 %collective-permute-start.12 = (bf16[2,2,64,256]{3,2,1,0:T(8,128)(2,1)S(1)}, bf16[2,2,64,256]{3,2,1,0:T(8,128)(2,1)S(1)}, u32[]{:S(2)}, u32[]{:S(2)}) collective-permute-start(bf16[2,2,64,256]{3,2,1,0:T(8,128)(2,1)S(1)} %get-tuple-element.32), channel_id=1, source_target_pairs={{0,12},{4,8},{8,4},{12,0},{1,13},{5,9},{9,5},{13,1},{2,14},{6,10},... | collective-permute-start | bytes 393224 | tf_op jit(solution)/shard_map/ppermute | solution.py:214
  52.6 7.1 %collective-permute-start.19 = (bf16[1,2,64,256]{3,2,1,0:T(8,128)(2,1)S(1)}, bf16[1,2,64,256]{3,2,1,0:T(8,128)(2,1)S(1)}, u32[]{:S(2)}, u32[]{:S(2)}) collective-permute-start(bf16[1,2,64,256]{3,2,1,0:T(8,128)(2,1)S(1)} %get-tuple-element.39), channel_id=1, source_target_pairs={{0,8},{4,12},{8,0},{12,4},{1,9},{5,13},{9,1},{13,5},{2,10},{6,14},... | collective-permute-start | bytes 196616 | tf_op jit(solution)/shard_map/ppermute | solution.py:214
  52.9 8.1 %collective-permute-start.20 = (bf16[1,2,64,256]{3,2,1,0:T(8,128)(2,1)S(1)}, bf16[1,2,64,256]{3,2,1,0:T(8,128)(2,1)S(1)}, u32[]{:S(2)}, u32[]{:S(2)}) collective-permute-start(bf16[1,2,64,256]{3,2,1,0:T(8,128)(2,1)S(1)} %get-tuple-element.40), channel_id=1, source_target_pairs={{0,12},{4,8},{8,4},{12,0},{1,13},{5,9},{9,5},{13,1},{2,14},{6,10},... | collective-permute-start | bytes 196616 | tf_op jit(solution)/shard_map/ppermute | solution.py:214

commit v3 on v0

v3 whole, which is shorter than its diff:
```python
import functools

import jax
import jax.numpy as jnp
from jax import lax
from jax.experimental import pallas as pl
from jax.experimental.pallas import tpu as pltpu
from jax.sharding import PartitionSpec as P

ANY = pl.BlockSpec(memory_space=pl.ANY)
HBM = pl.BlockSpec(memory_space=pltpu.HBM)
SMEM = pl.BlockSpec(memory_space=pltpu.SMEM)
VMEM = pl.BlockSpec(memory_space=pltpu.VMEM)
F32 = jnp.float32
BF16 = jnp.bfloat16
EVERY = slice(None)
LONG = 10**11


def peer(i, d, n):
    return i ^ d if n & (n - 1) == 0 else (i + d) % n


def back(i, d, n):
    return i ^ d if n & (n - 1) == 0 else (i + n - d) % n


def find(place, nb, left, right):
    block, slot, found = jnp.int32(0), jnp.int32(0), jnp.bool_(False)
    for i in range(nb):
        at = place[left * nb + i]
        hit = lax.div(at, jnp.int32(nb)) == right
        block = jnp.where(hit, jnp.int32(i), block)
        slot = jnp.where(hit, lax.rem(at, jnp.int32(nb)), slot)
        found = found | hit
    return block, slot, found


def chunk(ref, lead, index, rows):
    return ref.at[(*lead, pl.ds(pl.multiple_of(index * rows, rows), rows))]


class Copies:
    def __init__(self, sems):
        self.sems, self.used, self.groups = sems, 0, {}

    def add(self, group, src, dst):
        copy = pltpu.make_async_copy(src, dst, self.sems.at[self.used])
        self.used += 1
        copy.start()
        self.groups.setdefault(group, []).append(copy)

    def wait(self, group):
        for copy in self.groups.pop(group):
            copy.wait()


def pick_kernel(nsec, nop, nb, place, psi, left_env, *rest):
    outs, copies = rest[:-1], Copies(rest[-1])
    me, mine = lax.axis_index("sec"), lax.axis_index("op")
    terms, vecs = left_env.shape[0], psi.shape[1]
    rows = psi.shape[-2] // nop
    found = [find(place, nb, me, peer(me, d, nsec))[0] for d in range(1, nsec)]
    for n in range(1, nsec - 1):
        copies.add(0, chunk(psi, (found[n], EVERY), mine, rows), outs[n])
    copies.add(0, psi.at[found[0]], outs[0].at[pl.ds(0, vecs)])
    copies.add(0, left_env.at[:, found[0]], outs[0].at[pl.ds(vecs, terms)])
    for n in range(1, nsec - 1):
        copies.add(0, left_env.at[:, found[n]], outs[nsec - 2 + n])
    copies.wait(0)


def stack_kernel(*refs):
    pieces, out, copies = refs[:-2], refs[-2], Copies(refs[-1])
    for n, piece in enumerate(pieces):
        copies.add(0, piece, out.at[n])
    copies.wait(0)


def work_kernel(rounds, waits, nsec, nop, nb, place, dims, psi, left_env, right_env, near, *rest):
    count = len(rounds)
    far = [d for d in rounds if d > 1]
    pieces, rest = (rest[:nop], rest[nop:]) if far else ((), rest)
    rest = rest[waits:]
    lefts, rest = rest[: len(far)], rest[len(far) :]
    keep, sends, rest = rest[0], rest[1:nop], rest[nop:]
    psi_v, left_v, right_v, total, sems = rest
    copies = Copies(sems)
    me, mine = lax.axis_index("sec"), lax.axis_index("op")
    terms, vecs, width = left_v.shape[1], psi_v.shape[1], psi_v.shape[-1]
    rows = width // nop
    found = [find(place, nb, back(me, d, nsec), me) for d in rounds]
    for e, d in enumerate(rounds):
        block, slot, _ = found[e]
        if d == 0:
            copies.add((e, 0), psi.at[block], psi_v.at[e])
            copies.add((e, 0), left_env.at[:, block], left_v.at[e])
        elif d == 1:
            copies.add((e, 0), near.at[pl.ds(0, vecs)], psi_v.at[e])
            copies.add((e, 0), near.at[pl.ds(vecs, terms)], left_v.at[e])
        else:
            for o in range(nop):
                copies.add((e, 0), pieces[o].at[d - 2], chunk(psi_v, (e, EVERY), back(mine, o, nop), rows))
            copies.add((e, 0), lefts[far.index(d)], left_v.at[e])
        copies.add((e, 1), right_env.at[:, slot], right_v.at[e])
    row = lax.broadcasted_iota(jnp.int32, (width, width), 0)
    col = lax.broadcasted_iota(jnp.int32, (width, width), 1)
    for e, d in enumerate(rounds):
        block, _, there = found[e]
        source = back(me, d, nsec)
        live_rows = jnp.where(there, dims[0, source * nb + block], 0)
        live_cols = jnp.where(there, dims[1, source * nb + block], 0)
        alive = (row < live_rows) & (col < live_cols)
        copies.wait((e, 0))
        left = left_v[e].reshape(terms * width, width)
        trans = []
        for v in range(vecs):
            masked = jnp.where(alive, psi_v[e, v], jnp.zeros_like(psi_v[e, v]))
            trans.append(jnp.dot(left, masked, preferred_element_type=F32).astype(BF16))
        copies.wait((e, 1))
        for v in range(vecs):
            value = None
            for k in range(terms):
                term = jnp.dot(trans[v][k * width : (k + 1) * width], right_v[e, k], preferred_element_type=F32)
                value = term if value is None else value + term
            total[v] = jnp.where(alive, value, 0.0)
        for o in range(nop):
            start = pl.multiple_of(peer(mine, o, nop) * rows, rows)
            part = total[:, pl.ds(start, rows), :]
            if o == 0:
                keep[e] = part
            else:
                sends[o - 1][e] = part.astype(BF16)


def final_kernel(groups, nsec, nop, nb, place, *rest):
    ready, keep, heard, rest = rest[: len(groups) - 1], rest[len(groups) - 1], rest[len(groups) : -5], rest[-5:]
    out, ready_v, keep_v, heard_v, sems = rest
    copies = Copies(sems)
    me = lax.axis_index("sec")
    count = keep.shape[0]
    copies.add("last", keep, keep_v)
    for n, part in enumerate(heard):
        copies.add("last", part, heard_v.at[n])
    at = 0
    for n, part in enumerate(ready):
        copies.add("ready", part, ready_v.at[pl.ds(at, part.shape[0])])
        at += part.shape[0]
    copies.wait("ready")

    def store(d, value):
        _, slot, there = find(place, nb, back(me, d, nsec), me)

        @pl.when(there)
        def _():
            out[slot] = value

    for n, d in enumerate(d for rounds in groups[:-1] for d in rounds):
        store(d, ready_v[n])
    copies.wait("last")
    for e, d in enumerate(groups[-1]):
        value = keep_v[e]
        for o in range(nop - 1):
            value = value + heard_v[o, e].astype(F32)
        store(d, value.astype(BF16))


def local(psi, left_env, right_env, sector_dims, right_place):
    nsec, nop = lax.axis_size("sec"), lax.axis_size("op")
    nb, vecs, width, _ = psi.shape
    terms = left_env.shape[0]
    rows = width // nop
    far = nsec - 2
    params = pltpu.CompilerParams(vmem_limit_bytes=40 * 2**20)
    shape = lambda *dims: jax.ShapeDtypeStruct(dims, BF16)
    dma = lambda *dims: pltpu.SemaphoreType.DMA(dims)

    def ship(x, axis, d):
        n = lax.axis_size(axis)
        return lax.ppermute(x, axis, [(i, peer(i, d, n)) for i in range(n)])

    def cost(flops, values):
        return pl.CostEstimate(flops=flops, bytes_accessed=2 * values, transcendentals=0)

    picked = pl.pallas_call(
        functools.partial(pick_kernel, nsec, nop, nb),
        in_specs=[SMEM, HBM, HBM],
        out_specs=[VMEM] * (1 + 2 * far),
        out_shape=[shape(vecs + terms, width, width)]
        + [shape(vecs, rows, width)] * far
        + [shape(terms, width, width)] * far,
        scratch_shapes=[dma(2 + 2 * far)],
        compiler_params=pltpu.CompilerParams(vmem_limit_bytes=PICK * 2**20),
        cost_estimate=cost(0, 2 * nsec * terms * width * width),
        name="pick",
    )(right_place, psi, left_env)

    pieces = [ship(picked[d - 1], "sec", d) for d in range(2, nsec)]
    near = ship(picked[0], "sec", 1)
    lefts = {d: ship(picked[far + d - 1], "sec", d) for d in range(2, nsec)}

    stacked = pl.pallas_call(
        stack_kernel,
        in_specs=[ANY] * far,
        out_specs=VMEM,
        out_shape=shape(far, vecs, rows, width),
        scratch_shapes=[dma(far)],
        compiler_params=params,
        cost_estimate=cost(STACK, 0),
        name="stack",
    )(*pieces)
    gathered = {0: stacked}
    if nop & (nop - 1) == 0:
        bit = nop // 2
        while bit:
            for o in sorted(gathered):
                gathered[o ^ bit] = ship(gathered[o], "op", bit)
            bit //= 2
    else:
        for o in range(1, nop):
            gathered[o] = ship(stacked, "op", o)

    half = 2 + far // 2
    groups = [[0, 1], list(range(2, half)), list(range(half, nsec))]
    after, ready = [], []
    for rounds in groups:
        count = len(rounds)
        given = [lefts[d] for d in rounds if d > 1]
        if given:
            given = [gathered[o] for o in range(nop)] + list(after) + given
        outs = pl.pallas_call(
            functools.partial(work_kernel, rounds, len(after), nsec, nop, nb),
            in_specs=[SMEM, SMEM, HBM, HBM, HBM] + [ANY] * (1 + len(given)),
            out_specs=[VMEM] * nop,
            out_shape=[jax.ShapeDtypeStruct((count, vecs, rows, width), F32)]
            + [shape(count, vecs, rows, width)] * (nop - 1),
            scratch_shapes=[
                pltpu.VMEM((count, vecs, width, width), BF16),
                pltpu.VMEM((count, terms, width, width), BF16),
                pltpu.VMEM((count, terms, width, width), BF16),
                pltpu.VMEM((vecs, width, width), F32),
                dma(count * (nop + 2)),
            ],
            compiler_params=params,
            cost_estimate=cost(WORK, 0),
            name="work",
        )(right_place, sector_dims, psi, left_env, right_env, near, *given)
        after = [outs[1]]
        heard = [ship(outs[o], "op", o) for o in range(1, nop)]
        if rounds is not groups[-1]:
            value = outs[0]
            for part in heard:
                value = value + part.astype(F32)
            ready.append(value.astype(BF16))

    count = len(groups[-1])
    return pl.pallas_call(
        functools.partial(final_kernel, groups, nsec, nop, nb),
        in_specs=[SMEM] + [ANY] * (len(ready) + nop),
        out_specs=VMEM,
        out_shape=shape(nb, vecs, rows, width),
        scratch_shapes=[
            pltpu.VMEM((nsec - count, vecs, rows, width), BF16),
            pltpu.VMEM((count, vecs, rows, width), F32),
            pltpu.VMEM((nop - 1, count, vecs, rows, width), BF16),
            dma(len(ready) + nop),
        ],
        compiler_params=params,
        cost_estimate=cost(0, 0),
        name="final",
    )(right_place, *ready, outs[0], *heard)


PICK, STACK, WORK = 61, 0, 0


def solution(mesh):
    return jax.shard_map(
        local,
        mesh=mesh,
        in_specs=(
            P(("grp", "sec"), None, None, None),
            P("op", ("grp", "sec"), None, None),
            P("op", ("grp", "sec"), None, None),
            P(None, "grp"),
            P("grp"),
        ),
        out_specs=P(("grp", "sec"), None, "op", None),
        check_vma=False,
    )
```

time: 119 us -> 52.8 us (0.44)
  the two profiles are of different devices: /device:TPU:0 before, /device:TPU:25 now
where the time goes in v3:
time: 52.8 us; the launch traced here: 52.6 us
  starting transfers between devices  22.1 us (42%)
  waiting for transfers between devices  18.5 us (35%)
  Pallas kernels  10.6 us (20%)
  local copies, waits for them, and re-layouts  1.24 us (2%)
    ppermute x17, starting transfers between devices, ship(): return lax.ppermute(x, axis, [(i, peer(i, d, n)) for i in range(n)])  22.1 us
    ppermute x17, waiting for transfers between devices, ship(): return lax.ppermute(x, axis, [(i, peer(i, d, n)) for i in range(n)])  18.5 us
    pallas_call x3, Pallas kernels, local(): pl.pallas_call(functools.partial(work_kernel, rounds, len(after), nsec, n...  5.19 us
    pallas_call x1, Pallas kernels, local(): pl.pallas_call(functools.partial(pick_kernel, nsec, nop, nb), in_specs=[S...  3.13 us
    pallas_call x1, Pallas kernels, local(): pl.pallas_call(functools.partial(final_kernel, groups, nsec, nop, nb), in...  2.08 us
    unnamed x12, local copies, waits for them, and re-layouts  1.24 us
  transfers between devices with their start and end apart: 17, of which 7 were waited for; matrix products, arithmetic and copies ran while one was open for 0% of the time, Pallas kernels for 10%

profile of v3, /device:TPU:25, one launch (start us, length us, event | category | flops | bytes accessed | tf_op | source)
XLA Modules:
  0.0 52.6 jit_solution(8060662056389214791)
XLA Ops:
  0.0 0.0 copy-start
  0.0 0.0 copy-start.1
  0.0 3.1 %pick.1 = (bf16[4,256,256]{2,1,0:T(8,128)(2,1)}, bf16[2,64,256]{2,1,0:T(8,128)(2,1)}, bf16[2,64,256]{2,1,0:T(8,128)(2,1)}, bf16[2,256,256]{2,1,0:T(8,128)(2,1)}, bf16[2,256,256]{2,1,0:T(8,128)(2,1)}) custom-call(s32[16]{0:T(128)} %place.9, bf16[4,2,256,256]{3,2,1,0:T(8,128)(2,1)} %psi.7, bf16[2,4,256,256]{3,2,1,0:T(8,128)(2,1)} %left_env.7), custom_call_target="tpu_custom_call" | custom-call | bytes 2097152 | tf_op jit(solution)/shard_map/pick/pallas_call | solution.py:185
  3.1 0.0 copy-start.5
  3.2 0.2 collective-permute-start
  3.4 0.0 collective-permute-start.4
  3.4 3.4 %collective-permute-start.5 = (bf16[2,64,256]{2,1,0:T(8,128)(2,1)}, bf16[2,64,256]{2,1,0:T(8,128)(2,1)S(1)}, u32[]{:S(2)}, u32[]{:S(2)}) collective-permute-start(bf16[2,64,256]{2,1,0:T(8,128)(2,1)} %get-tuple-element.28), channel_id=1, source_target_pairs={{0,3},{1,2},{2,1},{3,0},{4,7},{5,6},{6,5},{7,4},{8,11},{9,10},{10,... | collective-permute-start | bytes 196616 | tf_op jit(solution)/shard_map/ppermute | solution.py:180
  6.8 0.0 collective-permute-start.9
  6.8 8.9 %collective-permute-done.4.refs_0_ = bf16[2,64,256]{2,1,0:T(8,128)(2,1)S(1)} collective-permute-done((bf16[2,64,256]{2,1,0:T(8,128)(2,1)}, bf16[2,64,256]{2,1,0:T(8,128)(2,1)S(1)}, u32[]{:S(2)}, u32[]{:S(2)}) %collective-permute-start.4) | collective-permute-done | bytes 65568 | tf_op jit(solution)/shard_map/ppermute | solution.py:180
  15.7 2.8 %collective-permute-done.5.refs_1_ = bf16[2,64,256]{2,1,0:T(8,128)(2,1)S(1)} collective-permute-done((bf16[2,64,256]{2,1,0:T(8,128)(2,1)}, bf16[2,64,256]{2,1,0:T(8,128)(2,1)S(1)}, u32[]{:S(2)}, u32[]{:S(2)}) %collective-permute-start.5) | collective-permute-done | bytes 65568 | tf_op jit(solution)/shard_map/ppermute | solution.py:180
  18.5 0.2 stack.1.rest_0_
  18.7 0.0 copy-start.3
  18.7 0.0 copy-start.4
  18.7 1.3 %collective-permute-start.7 = (bf16[2,2,64,256]{3,2,1,0:T(8,128)(2,1)S(1)}, bf16[2,2,64,256]{3,2,1,0:T(8,128)(2,1)S(1)}, u32[]{:S(2)}, u32[]{:S(2)}) collective-permute-start(bf16[2,2,64,256]{3,2,1,0:T(8,128)(2,1)S(1)} %stack.1.rest_0_), channel_id=1, source_target_pairs={{0,8},{4,12},{8,0},{12,4},{1,9},{5,13},{9,1},{13,5},{2,10},{6,14},... | collective-permute-start | bytes 393224 | tf_op jit(solution)/shard_map/ppermute | solution.py:180
  20.0 0.0 copy-done.5
  20.0 2.2 %collective-permute-start.13 = (bf16[2,256,256]{2,1,0:T(8,128)(2,1)S(1)}, bf16[2,256,256]{2,1,0:T(8,128)(2,1)S(1)}, u32[]{:S(2)}, u32[]{:S(2)}) collective-permute-start(bf16[2,256,256]{2,1,0:T(8,128)(2,1)S(1)} %copy-done.5), channel_id=1, source_target_pairs={{0,3},{1,2},{2,1},{3,0},{4,7},{5,6},{6,5},{7,4},{8,11},{9,10},{10,... | collective-permute-start | bytes 786440 | tf_op jit(solution)/shard_map/ppermute | solution.py:180
  22.2 3.6 %collective-permute-start.6 = (bf16[2,2,64,256]{3,2,1,0:T(8,128)(2,1)S(1)}, bf16[2,2,64,256]{3,2,1,0:T(8,128)(2,1)S(1)}, u32[]{:S(2)}, u32[]{:S(2)}) collective-permute-start(bf16[2,2,64,256]{3,2,1,0:T(8,128)(2,1)S(1)} %stack.1.rest_0_), channel_id=1, source_target_pairs={{0,4},{4,0},{8,12},{12,8},{1,5},{5,1},{9,13},{13,9},{2,6},{6,2},{1... | collective-permute-start | bytes 393224 | tf_op jit(solution)/shard_map/ppermute | solution.py:180
  25.8 0.0 collective-permute-done.7.rest_2_
  25.8 0.9 %collective-permute-start.8 = (bf16[2,2,64,256]{3,2,1,0:T(8,128)(2,1)S(1)}, bf16[2,2,64,256]{3,2,1,0:T(8,128)(2,1)S(1)}, u32[]{:S(2)}, u32[]{:S(2)}) collective-permute-start(bf16[2,2,64,256]{3,2,1,0:T(8,128)(2,1)S(1)} %collective-permute-done.7.rest_2_), channel_id=1, source_target_pairs={{0,4},{4,0},{8,12},{12,8},{1,5},{5,1},{9,13},{13,9},{2,6},{6,2},{1... | collective-permute-start | bytes 393224 | tf_op jit(solution)/shard_map/ppermute | solution.py:180
  26.7 0.0 collective-permute-done.near
  26.7 0.0 copy-done
  26.7 0.0 copy-done.1
  26.7 0.0 copy-done.3
  26.7 0.0 copy-done.4
  26.8 0.0 copy-start.2
  26.8 1.2 %copy-done.2 = bf16[2,4,256,256]{3,2,1,0:T(8,128)(2,1)S(1)} copy-done((bf16[2,4,256,256]{3,2,1,0:T(8,128)(2,1)S(1)}, bf16[2,4,256,256]{3,2,1,0:T(8,128)(2,1)}, u32[]{:S(2)}) %copy-start.2) | copy-done | bytes 1048600
  28.0 2.1 %work.3 = (f32[2,2,64,256]{3,2,1,0:T(8,128)S(1)}, bf16[2,2,64,256]{3,2,1,0:T(8,128)(2,1)S(1)}, bf16[2,2,64,256]{3,2,1,0:T(8,128)(2,1)S(1)}, bf16[2,2,64,256]{3,2,1,0:T(8,128)(2,1)S(1)}) custom-call(s32[16]{0:T(128)S(1)} %copy-done.3, s32[2,16]{1,0:T(2,128)S(1)} %copy-done.4, bf16[4,2,256,256]{3,2,1,0:T(8,128)(2,1)S(1)} %copy-done, ...), custom_call_target="tpu_custom_call" | custom-call | tf_op jit(solution)/shard_map/work/pallas_call | solution.py:231
  30.1 0.0 collective-permute-done.6.rest_1_
  30.1 0.0 collective-permute-done.9.rest_5_
  30.1 0.0 collective-permute-done.8.rest_3_
  30.2 1.5 %work.4 = (f32[1,2,64,256]{3,2,1,0:T(8,128)S(1)}, bf16[1,2,64,256]{3,2,1,0:T(8,128)(2,1)S(1)}, bf16[1,2,64,256]{3,2,1,0:T(8,128)(2,1)S(1)}, bf16[1,2,64,256]{3,2,1,0:T(8,128)(2,1)S(1)}) custom-call(s32[16]{0:T(128)S(1)} %copy-done.3, s32[2,16]{1,0:T(2,128)S(1)} %copy-done.4, bf16[4,2,256,256]{3,2,1,0:T(8,128)(2,1)S(1)} %copy-done, ...), custom_call_target="tpu_custom_call" | custom-call | tf_op jit(solution)/shard_map/work/pallas_call | solution.py:231
  31.7 6.2 %collective-permute-start.12 = (bf16[1,2,64,256]{3,2,1,0:T(8,128)(2,1)S(1)}, bf16[1,2,64,256]{3,2,1,0:T(8,128)(2,1)S(1)}, u32[]{:S(2)}, u32[]{:S(2)}) collective-permute-start(bf16[1,2,64,256]{3,2,1,0:T(8,128)(2,1)S(1)} %get-tuple-element.33), channel_id=1, source_target_pairs={{0,12},{4,8},{8,4},{12,0},{1,13},{5,9},{9,5},{13,1},{2,14},{6,10},... | collective-permute-start | bytes 196616 | tf_op jit(solution)/shard_map/ppermute | solution.py:180
  37.9 0.3 collective-permute-start.11
  38.2 0.2 collective-permute-start.10
  38.4 0.3 collective-permute-start.1
  38.7 0.0 collective-permute-done.13.rest_5_
  38.7 1.1 %collective-permute-start.3 = (bf16[2,2,64,256]{3,2,1,0:T(8,128)(2,1)S(1)}, bf16[2,2,64,256]{3,2,1,0:T(8,128)(2,1)S(1)}, u32[]{:S(2)}, u32[]{:S(2)}) collective-permute-start(bf16[2,2,64,256]{3,2,1,0:T(8,128)(2,1)S(1)} %get-tuple-element.26), channel_id=1, source_target_pairs={{0,12},{4,8},{8,4},{12,0},{1,13},{5,9},{9,5},{13,1},{2,14},{6,10},... | collective-permute-start | bytes 393224 | tf_op jit(solution)/shard_map/ppermute | solution.py:180
  39.8 1.5 %work.5 = (f32[1,2,64,256]{3,2,1,0:T(8,128)S(1)}, bf16[1,2,64,256]{3,2,1,0:T(8,128)(2,1)S(1)}, bf16[1,2,64,256]{3,2,1,0:T(8,128)(2,1)S(1)}, bf16[1,2,64,256]{3,2,1,0:T(8,128)(2,1)S(1)}) custom-call(s32[16]{0:T(128)S(1)} %copy-done.3, s32[2,16]{1,0:T(2,128)S(1)} %copy-done.4, bf16[4,2,256,256]{3,2,1,0:T(8,128)(2,1)S(1)} %copy-done, ...), custom_call_target="tpu_custom_call" | custom-call | tf_op jit(solution)/shard_map/work/pallas_call | solution.py:231
  41.3 0.0 collective-permute-done.12
  41.4 0.5 %collective-permute-start.2 = (bf16[2,2,64,256]{3,2,1,0:T(8,128)(2,1)S(1)}, bf16[2,2,64,256]{3,2,1,0:T(8,128)(2,1)S(1)}, u32[]{:S(2)}, u32[]{:S(2)}) collective-permute-start(bf16[2,2,64,256]{3,2,1,0:T(8,128)(2,1)S(1)} %get-tuple-element.25), channel_id=1, source_target_pairs={{0,8},{4,12},{8,0},{12,4},{1,9},{5,13},{9,1},{13,5},{2,10},{6,14},... | collective-permute-start | bytes 393224 | tf_op jit(solution)/shard_map/ppermute | solution.py:180
  41.9 0.3 collective-permute-done.11
  42.2 0.5 collective-permute-start.14
  42.7 0.0 collective-permute-done.10
  42.7 1.0 %collective-permute-start.15 = (bf16[1,2,64,256]{3,2,1,0:T(8,128)(2,1)S(1)}, bf16[1,2,64,256]{3,2,1,0:T(8,128)(2,1)S(1)}, u32[]{:S(2)}, u32[]{:S(2)}) collective-permute-start(bf16[1,2,64,256]{3,2,1,0:T(8,128)(2,1)S(1)} %get-tuple-element.37), channel_id=1, source_target_pairs={{0,8},{4,12},{8,0},{12,4},{1,9},{5,13},{9,1},{13,5},{2,10},{6,14},... | collective-permute-start | bytes 196616 | tf_op jit(solution)/shard_map/ppermute | solution.py:180
  43.7 1.3 %collective-permute-done.3 = bf16[2,2,64,256]{3,2,1,0:T(8,128)(2,1)S(1)} collective-permute-done((bf16[2,2,64,256]{3,2,1,0:T(8,128)(2,1)S(1)}, bf16[2,2,64,256]{3,2,1,0:T(8,128)(2,1)S(1)}, u32[]{:S(2)}, u32[]{:S(2)}) %collective-permute-start.3) | collective-permute-done | bytes 131104 | tf_op jit(solution)/shard_map/ppermute | solution.py:180
  45.0 0.3 collective-permute-start.16
  45.3 2.4 %collective-permute-done.2 = bf16[2,2,64,256]{3,2,1,0:T(8,128)(2,1)S(1)} collective-permute-done((bf16[2,2,64,256]{3,2,1,0:T(8,128)(2,1)S(1)}, bf16[2,2,64,256]{3,2,1,0:T(8,128)(2,1)S(1)}, u32[]{:S(2)}, u32[]{:S(2)}) %collective-permute-start.2) | collective-permute-done | bytes 131104 | tf_op jit(solution)/shard_map/ppermute | solution.py:180
  47.7 0.0 collective-permute-done.1
  47.7 0.1 add_convert_fusion.rest_0_
  47.8 0.0 collective-permute-done.14.rest_3_
  47.8 1.3 %collective-permute-done.15.rest_4_ = bf16[1,2,64,256]{3,2,1,0:T(8,128)(2,1)S(1)} collective-permute-done((bf16[1,2,64,256]{3,2,1,0:T(8,128)(2,1)S(1)}, bf16[1,2,64,256]{3,2,1,0:T(8,128)(2,1)S(1)}, u32[]{:S(2)}, u32[]{:S(2)}) %collective-permute-start.15) | collective-permute-done | bytes 65568 | tf_op jit(solution)/shard_map/ppermute | solution.py:180
  49.1 1.4 %collective-permute-done.16.rest_5_ = bf16[1,2,64,256]{3,2,1,0:T(8,128)(2,1)S(1)} collective-permute-done((bf16[1,2,64,256]{3,2,1,0:T(8,128)(2,1)S(1)}, bf16[1,2,64,256]{3,2,1,0:T(8,128)(2,1)S(1)}, u32[]{:S(2)}, u32[]{:S(2)}) %collective-permute-start.16) | collective-permute-done | bytes 65568 | tf_op jit(solution)/shard_map/ppermute | solution.py:180
  50.6 2.1 %final.1 = bf16[4,2,64,256]{3,2,1,0:T(8,128)(2,1)} custom-call(s32[16]{0:T(128)S(1)} %copy-done.3, bf16[2,2,64,256]{3,2,1,0:T(8,128)(2,1)S(1)} %add_convert_fusion.rest_0_, bf16[1,2,64,256]{3,2,1,0:T(8,128)(2,1)S(1)} %add_convert_fusion.1.rest_1_, f32[1,2,64,256]{3,2,1,0:T(8,128)S(1)} %get-tuple-element.35.rest_2_, ...), custom_call_target="tpu_custom_call" | custom-call | tf_op jit(solution)/shard_map/final/pallas_call | solution.py:257
  (1 shorter events, 0.0 us)
Async XLA Ops:
  0.0 26.7 %copy-start = (bf16[4,2,256,256]{3,2,1,0:T(8,128)(2,1)S(1)}, bf16[4,2,256,256]{3,2,1,0:T(8,128)(2,1)}, u32[]{:S(2)}) copy-start(bf16[4,2,256,256]{3,2,1,0:T(8,128)(2,1)} %psi.7) | copy-start | bytes 3145732
  0.0 26.7 %copy-start.1 = (bf16[2,4,256,256]{3,2,1,0:T(8,128)(2,1)S(1)}, bf16[2,4,256,256]{3,2,1,0:T(8,128)(2,1)}, u32[]{:S(2)}) copy-start(bf16[2,4,256,256]{3,2,1,0:T(8,128)(2,1)} %left_env.7) | copy-start | bytes 3145732
  3.1 16.8 %copy-start.5 = (bf16[2,256,256]{2,1,0:T(8,128)(2,1)S(1)}, bf16[2,256,256]{2,1,0:T(8,128)(2,1)}, u32[]{:S(2)}) copy-start(bf16[2,256,256]{2,1,0:T(8,128)(2,1)} %get-tuple-element.34) | copy-start | bytes 786436
  3.2 23.6 %collective-permute-start = (bf16[4,256,256]{2,1,0:T(8,128)(2,1)}, bf16[4,256,256]{2,1,0:T(8,128)(2,1)S(1)}, u32[]{:S(2)}, u32[]{:S(2)}) collective-permute-start(bf16[4,256,256]{2,1,0:T(8,128)(2,1)} %get-tuple-element.22), channel_id=1, source_target_pairs={{0,1},{1,0},{2,3},{3,2},{4,5},{5,4},{6,7},{7,6},{8,9},{9,8},{10,11... | collective-permute-start | bytes 1572872 | tf_op jit(solution)/shard_map/ppermute | solution.py:180
  3.4 12.3 %collective-permute-start.4 = (bf16[2,64,256]{2,1,0:T(8,128)(2,1)}, bf16[2,64,256]{2,1,0:T(8,128)(2,1)S(1)}, u32[]{:S(2)}, u32[]{:S(2)}) collective-permute-start(bf16[2,64,256]{2,1,0:T(8,128)(2,1)} %get-tuple-element.27), channel_id=1, source_target_pairs={{0,2},{1,3},{2,0},{3,1},{4,6},{5,7},{6,4},{7,5},{8,10},{9,11},{10,... | collective-permute-start | bytes 196616 | tf_op jit(solution)/shard_map/ppermute | solution.py:180
  3.4 15.1 %collective-permute-start.5 = (bf16[2,64,256]{2,1,0:T(8,128)(2,1)}, bf16[2,64,256]{2,1,0:T(8,128)(2,1)S(1)}, u32[]{:S(2)}, u32[]{:S(2)}) collective-permute-start(bf16[2,64,256]{2,1,0:T(8,128)(2,1)} %get-tuple-element.28), channel_id=1, source_target_pairs={{0,3},{1,2},{2,1},{3,0},{4,7},{5,6},{6,5},{7,4},{8,11},{9,10},{10,... | collective-permute-start | bytes 196616 | tf_op jit(solution)/shard_map/ppermute | solution.py:180
  6.8 23.4 %collective-permute-start.9 = (bf16[2,256,256]{2,1,0:T(8,128)(2,1)}, bf16[2,256,256]{2,1,0:T(8,128)(2,1)S(1)}, u32[]{:S(2)}, u32[]{:S(2)}) collective-permute-start(bf16[2,256,256]{2,1,0:T(8,128)(2,1)} %get-tuple-element.29), channel_id=1, source_target_pairs={{0,2},{1,3},{2,0},{3,1},{4,6},{5,7},{6,4},{7,5},{8,10},{9,11},{10,... | collective-permute-start | bytes 786440 | tf_op jit(solution)/shard_map/ppermute | solution.py:180
  18.7 8.1 %copy-start.3 = (s32[16]{0:T(128)S(1)}, s32[16]{0:T(128)}, u32[]{:S(2)}) copy-start(s32[16]{0:T(128)} %place.9) | copy-start | bytes 196
  18.7 8.1 %copy-start.4 = (s32[2,16]{1,0:T(2,128)S(1)}, s32[2,16]{1,0:T(2,128)}, u32[]{:S(2)}) copy-start(s32[2,16]{1,0:T(2,128)} %dims.5) | copy-start | bytes 388
  18.7 7.1 %collective-permute-start.7 = (bf16[2,2,64,256]{3,2,1,0:T(8,128)(2,1)S(1)}, bf16[2,2,64,256]{3,2,1,0:T(8,128)(2,1)S(1)}, u32[]{:S(2)}, u32[]{:S(2)}) collective-permute-start(bf16[2,2,64,256]{3,2,1,0:T(8,128)(2,1)S(1)} %stack.1.rest_0_), channel_id=1, source_target_pairs={{0,8},{4,12},{8,0},{12,4},{1,9},{5,13},{9,1},{13,5},{2,10},{6,14},... | collective-permute-start | bytes 393224 | tf_op jit(solution)/shard_map/ppermute | solution.py:180
  20.0 18.7 %collective-permute-start.13 = (bf16[2,256,256]{2,1,0:T(8,128)(2,1)S(1)}, bf16[2,256,256]{2,1,0:T(8,128)(2,1)S(1)}, u32[]{:S(2)}, u32[]{:S(2)}) collective-permute-start(bf16[2,256,256]{2,1,0:T(8,128)(2,1)S(1)} %copy-done.5), channel_id=1, source_target_pairs={{0,3},{1,2},{2,1},{3,0},{4,7},{5,6},{6,5},{7,4},{8,11},{9,10},{10,... | collective-permute-start | bytes 786440 | tf_op jit(solution)/shard_map/ppermute | solution.py:180
  22.2 8.0 %collective-permute-start.6 = (bf16[2,2,64,256]{3,2,1,0:T(8,128)(2,1)S(1)}, bf16[2,2,64,256]{3,2,1,0:T(8,128)(2,1)S(1)}, u32[]{:S(2)}, u32[]{:S(2)}) collective-permute-start(bf16[2,2,64,256]{3,2,1,0:T(8,128)(2,1)S(1)} %stack.1.rest_0_), channel_id=1, source_target_pairs={{0,4},{4,0},{8,12},{12,8},{1,5},{5,1},{9,13},{13,9},{2,6},{6,2},{1... | collective-permute-start | bytes 393224 | tf_op jit(solution)/shard_map/ppermute | solution.py:180
  25.8 4.3 %collective-permute-start.8 = (bf16[2,2,64,256]{3,2,1,0:T(8,128)(2,1)S(1)}, bf16[2,2,64,256]{3,2,1,0:T(8,128)(2,1)S(1)}, u32[]{:S(2)}, u32[]{:S(2)}) collective-permute-start(bf16[2,2,64,256]{3,2,1,0:T(8,128)(2,1)S(1)} %collective-permute-done.7.rest_2_), channel_id=1, source_target_pairs={{0,4},{4,0},{8,12},{12,8},{1,5},{5,1},{9,13},{13,9},{2,6},{6,2},{1... | collective-permute-start | bytes 393224 | tf_op jit(solution)/shard_map/ppermute | solution.py:180
  26.8 1.2 %copy-start.2 = (bf16[2,4,256,256]{3,2,1,0:T(8,128)(2,1)S(1)}, bf16[2,4,256,256]{3,2,1,0:T(8,128)(2,1)}, u32[]{:S(2)}) copy-start(bf16[2,4,256,256]{3,2,1,0:T(8,128)(2,1)} %right_env.5) | copy-start | bytes 3145732
  31.7 9.7 %collective-permute-start.12 = (bf16[1,2,64,256]{3,2,1,0:T(8,128)(2,1)S(1)}, bf16[1,2,64,256]{3,2,1,0:T(8,128)(2,1)S(1)}, u32[]{:S(2)}, u32[]{:S(2)}) collective-permute-start(bf16[1,2,64,256]{3,2,1,0:T(8,128)(2,1)S(1)} %get-tuple-element.33), channel_id=1, source_target_pairs={{0,12},{4,8},{8,4},{12,0},{1,13},{5,9},{9,5},{13,1},{2,14},{6,10},... | collective-permute-start | bytes 196616 | tf_op jit(solution)/shard_map/ppermute | solution.py:180
  37.9 4.3 %collective-permute-start.11 = (bf16[1,2,64,256]{3,2,1,0:T(8,128)(2,1)S(1)}, bf16[1,2,64,256]{3,2,1,0:T(8,128)(2,1)S(1)}, u32[]{:S(2)}, u32[]{:S(2)}) collective-permute-start(bf16[1,2,64,256]{3,2,1,0:T(8,128)(2,1)S(1)} %get-tuple-element.32), channel_id=1, source_target_pairs={{0,8},{4,12},{8,0},{12,4},{1,9},{5,13},{9,1},{13,5},{2,10},{6,14},... | collective-permute-start | bytes 196616 | tf_op jit(solution)/shard_map/ppermute | solution.py:180
  38.2 4.5 %collective-permute-start.10 = (bf16[1,2,64,256]{3,2,1,0:T(8,128)(2,1)S(1)}, bf16[1,2,64,256]{3,2,1,0:T(8,128)(2,1)S(1)}, u32[]{:S(2)}, u32[]{:S(2)}) collective-permute-start(bf16[1,2,64,256]{3,2,1,0:T(8,128)(2,1)S(1)} %get-tuple-element.31.rest_4_), channel_id=1, source_target_pairs={{0,4},{4,0},{8,12},{12,8},{1,5},{5,1},{9,13},{13,9},{2,6},{6,2},{1... | collective-permute-start | bytes 196616 | tf_op jit(solution)/shard_map/ppermute | solution.py:180
  38.4 9.3 %collective-permute-start.1 = (bf16[2,2,64,256]{3,2,1,0:T(8,128)(2,1)S(1)}, bf16[2,2,64,256]{3,2,1,0:T(8,128)(2,1)S(1)}, u32[]{:S(2)}, u32[]{:S(2)}) collective-permute-start(bf16[2,2,64,256]{3,2,1,0:T(8,128)(2,1)S(1)} %get-tuple-element.24.rest_4_), channel_id=1, source_target_pairs={{0,4},{4,0},{8,12},{12,8},{1,5},{5,1},{9,13},{13,9},{2,6},{6,2},{1... | collective-permute-start | bytes 393224 | tf_op jit(solution)/shard_map/ppermute | solution.py:180
  38.7 6.3 %collective-permute-start.3 = (bf16[2,2,64,256]{3,2,1,0:T(8,128)(2,1)S(1)}, bf16[2,2,64,256]{3,2,1,0:T(8,128)(2,1)S(1)}, u32[]{:S(2)}, u32[]{:S(2)}) collective-permute-start(bf16[2,2,64,256]{3,2,1,0:T(8,128)(2,1)S(1)} %get-tuple-element.26), channel_id=1, source_target_pairs={{0,12},{4,8},{8,4},{12,0},{1,13},{5,9},{9,5},{13,1},{2,14},{6,10},... | collective-permute-start | bytes 393224 | tf_op jit(solution)/shard_map/ppermute | solution.py:180
  41.4 6.4 %collective-permute-start.2 = (bf16[2,2,64,256]{3,2,1,0:T(8,128)(2,1)S(1)}, bf16[2,2,64,256]{3,2,1,0:T(8,128)(2,1)S(1)}, u32[]{:S(2)}, u32[]{:S(2)}) collective-permute-start(bf16[2,2,64,256]{3,2,1,0:T(8,128)(2,1)S(1)} %get-tuple-element.25), channel_id=1, source_target_pairs={{0,8},{4,12},{8,0},{12,4},{1,9},{5,13},{9,1},{13,5},{2,10},{6,14},... | collective-permute-start | bytes 393224 | tf_op jit(solution)/shard_map/ppermute | solution.py:180
  42.2 5.6 %collective-permute-start.14 = (bf16[1,2,64,256]{3,2,1,0:T(8,128)(2,1)S(1)}, bf16[1,2,64,256]{3,2,1,0:T(8,128)(2,1)S(1)}, u32[]{:S(2)}, u32[]{:S(2)}) collective-permute-start(bf16[1,2,64,256]{3,2,1,0:T(8,128)(2,1)S(1)} %get-tuple-element.36), channel_id=1, source_target_pairs={{0,4},{4,0},{8,12},{12,8},{1,5},{5,1},{9,13},{13,9},{2,6},{6,2},{1... | collective-permute-start | bytes 196616 | tf_op jit(solution)/shard_map/ppermute | solution.py:180
  42.7 6.5 %collective-permute-start.15 = (bf16[1,2,64,256]{3,2,1,0:T(8,128)(2,1)S(1)}, bf16[1,2,64,256]{3,2,1,0:T(8,128)(2,1)S(1)}, u32[]{:S(2)}, u32[]{:S(2)}) collective-permute-start(bf16[1,2,64,256]{3,2,1,0:T(8,128)(2,1)S(1)} %get-tuple-element.37), channel_id=1, source_target_pairs={{0,8},{4,12},{8,0},{12,4},{1,9},{5,13},{9,1},{13,5},{2,10},{6,14},... | collective-permute-start | bytes 196616 | tf_op jit(solution)/shard_map/ppermute | solution.py:180
  45.0 5.6 %collective-permute-start.16 = (bf16[1,2,64,256]{3,2,1,0:T(8,128)(2,1)S(1)}, bf16[1,2,64,256]{3,2,1,0:T(8,128)(2,1)S(1)}, u32[]{:S(2)}, u32[]{:S(2)}) collective-permute-start(bf16[1,2,64,256]{3,2,1,0:T(8,128)(2,1)S(1)} %get-tuple-element.38), channel_id=1, source_target_pairs={{0,12},{4,8},{8,4},{12,0},{1,13},{5,9},{9,5},{13,1},{2,14},{6,10},... | collective-permute-start | bytes 196616 | tf_op jit(solution)/shard_map/ppermute | solution.py:180

commit v4 on v3

v4 whole, which is shorter than its diff:
```python
import functools

import jax
import jax.numpy as jnp
from jax import lax
from jax.experimental import pallas as pl
from jax.experimental.pallas import tpu as pltpu
from jax.sharding import PartitionSpec as P

ANY = pl.BlockSpec(memory_space=pl.ANY)
HBM = pl.BlockSpec(memory_space=pltpu.HBM)
SMEM = pl.BlockSpec(memory_space=pltpu.SMEM)
VMEM = pl.BlockSpec(memory_space=pltpu.VMEM)
F32 = jnp.float32
BF16 = jnp.bfloat16
EVERY = slice(None)
LONG = 10**11


def find(place, nb, left, right):
    block, slot, found = jnp.int32(0), jnp.int32(0), jnp.bool_(False)
    for i in range(nb):
        at = place[left * nb + i]
        hit = lax.div(at, jnp.int32(nb)) == right
        block = jnp.where(hit, jnp.int32(i), block)
        slot = jnp.where(hit, lax.rem(at, jnp.int32(nb)), slot)
        found = found | hit
    return block, slot, found


def chunk(ref, lead, index, rows):
    return ref.at[(*lead, pl.ds(pl.multiple_of(index * rows, rows), rows))]


class Copies:
    def __init__(self, sems):
        self.sems, self.used, self.groups = sems, 0, {}

    def add(self, group, src, dst):
        copy = pltpu.make_async_copy(src, dst, self.sems.at[self.used])
        self.used += 1
        copy.start()
        self.groups.setdefault(group, []).append(copy)

    def wait(self, group):
        for copy in self.groups.pop(group):
            copy.wait()


def pick_kernel(nsec, nop, nb, place, psi, left_env, *rest):
    outs, copies = rest[:-1], Copies(rest[-1])
    me, mine = lax.axis_index("sec"), lax.axis_index("op")
    found = [find(place, nb, me, me ^ d)[0] for d in range(1, nsec)]
    for n, block in enumerate(found):
        copies.add(0, left_env.at[:, block], outs[nsec - 1 + n])
    for n, block in enumerate(found):
        copies.add(0, chunk(psi, (block, EVERY), mine, psi.shape[-2] // nop), outs[n])
    copies.wait(0)


def stack_kernel(*refs):
    pieces, out, copies = refs[:-2], refs[-2], Copies(refs[-1])
    for n, piece in enumerate(pieces):
        copies.add(0, piece, out.at[n])
    copies.wait(0)


def work_kernel(rounds, waits, nsec, nop, nb, place, dims, psi, left_env, right_env, *rest):
    count = len(rounds)
    far = [d for d in rounds if d]
    rest = rest[waits:]
    pieces, rest = (rest[:nop], rest[nop:]) if far else ((), rest)
    lefts, rest = rest[: len(far)], rest[len(far) :]
    keep, send, psi_v, left_v, right_v, total, sems = rest
    copies = Copies(sems)
    me, mine = lax.axis_index("sec"), lax.axis_index("op")
    terms, vecs, width = left_v.shape[1], psi_v.shape[1], psi_v.shape[-1]
    rows = width // nop
    found = [find(place, nb, me ^ d, me) for d in rounds]
    for e, d in enumerate(rounds):
        block, slot, _ = found[e]
        if d == 0:
            copies.add((e, 0), psi.at[block], psi_v.at[e])
            copies.add((e, 0), left_env.at[:, block], left_v.at[e])
        else:
            for o in range(nop):
                copies.add((e, 0), pieces[o].at[d - 1], chunk(psi_v, (e, EVERY), mine ^ o, rows))
            copies.add((e, 0), lefts[far.index(d)], left_v.at[e])
        copies.add((e, 1), right_env.at[:, slot], right_v.at[e])
    row = lax.broadcasted_iota(jnp.int32, (width, width), 0)
    col = lax.broadcasted_iota(jnp.int32, (width, width), 1)
    for e, d in enumerate(rounds):
        block, _, there = found[e]
        source = me ^ d
        live_rows = jnp.where(there, dims[0, source * nb + block], 0)
        live_cols = jnp.where(there, dims[1, source * nb + block], 0)
        alive = (row < live_rows) & (col < live_cols)
        copies.wait((e, 0))
        left = left_v[e].reshape(terms * width, width)
        trans = []
        for v in range(vecs):
            masked = jnp.where(alive, psi_v[e, v], jnp.zeros_like(psi_v[e, v]))
            trans.append(jnp.dot(left, masked, preferred_element_type=F32).astype(BF16))
        copies.wait((e, 1))
        for v in range(vecs):
            value = None
            for k in range(terms):
                term = jnp.dot(trans[v][k * width : (k + 1) * width], right_v[e, k], preferred_element_type=F32)
                value = term if value is None else value + term
            total[v] = jnp.where(alive, value, 0.0)
        for o in range(nop):
            start = pl.multiple_of((mine ^ o) * rows, rows)
            part = total[:, pl.ds(start, rows), :]
            if o % 2:
                send[o // 2, e] = part.astype(BF16)
            else:
                keep[o // 2, e] = part


def local(psi, left_env, right_env, sector_dims, right_place):
    nsec, nop = lax.axis_size("sec"), lax.axis_size("op")
    nb, vecs, width, _ = psi.shape
    terms = left_env.shape[0]
    rows = width // nop
    away = nsec - 1
    params = pltpu.CompilerParams(vmem_limit_bytes=40 * 2**20)
    shape = lambda *dims: jax.ShapeDtypeStruct(dims, BF16)
    dma = lambda *dims: pltpu.SemaphoreType.DMA(dims)

    def ship(x, axis, d):
        n = lax.axis_size(axis)
        return lax.ppermute(x, axis, [(i, i ^ d) for i in range(n)])

    def cost(flops, values):
        return pl.CostEstimate(flops=flops, bytes_accessed=2 * values, transcendentals=0)

    picked = pl.pallas_call(
        functools.partial(pick_kernel, nsec, nop, nb),
        in_specs=[SMEM, HBM, HBM],
        out_specs=[VMEM] * (2 * away),
        out_shape=[shape(vecs, rows, width)] * away + [shape(terms, width, width)] * away,
        scratch_shapes=[dma(2 * away)],
        compiler_params=pltpu.CompilerParams(vmem_limit_bytes=61 * 2**20),
        cost_estimate=cost(0, 0),
        name="pick",
    )(right_place, psi, left_env)
    pieces = [ship(picked[d - 1], "sec", d) for d in range(1, nsec)]
    lefts = {d: ship(picked[away + d - 1], "sec", d) for d in range(1, nsec)}

    def gather(pieces):
        stacked = pl.pallas_call(
            stack_kernel,
            in_specs=[ANY] * away,
            out_specs=VMEM,
            out_shape=shape(away, vecs, rows, width),
            scratch_shapes=[dma(away)],
            compiler_params=params,
            cost_estimate=cost(LONG, 0),
            name="stack",
        )(*pieces)
        gathered = {0: stacked}
        bit = nop // 2
        while bit:
            for o in sorted(gathered):
                gathered[o ^ bit] = ship(gathered[o], "op", bit)
            bit //= 2
        return [gathered[o] for o in range(nop)]

    def group(rounds, gathered, lefts, after):
        count = len(rounds)
        given = list(after) + (list(gathered) + [lefts[d] for d in rounds if d] if any(rounds) else [])
        value, send = pl.pallas_call(
            functools.partial(work_kernel, rounds, len(after), nsec, nop, nb),
            in_specs=[SMEM, SMEM, HBM, HBM, HBM] + [ANY] * len(given),
            out_specs=[VMEM] * 2,
            out_shape=[
                jax.ShapeDtypeStruct((nop // 2, count, vecs, rows, width), F32),
                shape(nop // 2, count, vecs, rows, width),
            ],
            scratch_shapes=[
                pltpu.VMEM((count, vecs, width, width), BF16),
                pltpu.VMEM((count, terms, width, width), BF16),
                pltpu.VMEM((count, terms, width, width), BF16),
                pltpu.VMEM((vecs, width, width), F32),
                dma(count * (nop + 2)),
            ],
            compiler_params=params,
            cost_estimate=cost(0, 0),
            name="work",
        )(right_place, sector_dims, psi, left_env, right_env, *given)
        bit = 1
        while True:
            value = value + ship(send, "op", bit).astype(F32)
            bit *= 2
            if bit == nop:
                break
            value, send = value[0::2], value[1::2].astype(BF16)
        return list(value[0].astype(BF16))

    def region(fn, *operands):
        like = jax.eval_shape(fn, *operands)
        none = lambda *operands: jax.tree.map(lambda x: jnp.zeros(x.shape, x.dtype), like)
        return lax.cond(right_place[0] >= 0, fn, none, *operands)

    gathered = gather(pieces)
    half = nsec // 2 + 1
    groups = [([0, 1], True, []), (list(range(2, half)), False, [0]), (list(range(half, nsec)), False, [0])]
    ready = {}
    for rounds, apart, waits in groups:
        arrived = {d: lefts[d] for d in rounds if d}
        after = [ready[d] for d in waits]
        if apart:
            values = region(functools.partial(group, rounds), gathered, arrived, after)
        else:
            values = group(rounds, gathered, arrived, after)
        for d, value in zip(rounds, values):
            ready[d] = value

    slots = lax.axis_index("sec") * nb + jnp.arange(nb, dtype=jnp.int32)
    blocks = jnp.arange(right_place.shape[0], dtype=jnp.int32)
    block = jnp.sum(jnp.where(right_place[None, :] == slots[:, None], blocks[None, :], 0), axis=1)
    round_of = (block // nb) ^ lax.axis_index("sec")
    sigma = ready[0][None]
    for d in range(1, nsec):
        sigma = jnp.where((round_of == d)[:, None, None, None], ready[d][None], sigma)
    return sigma


def solution(mesh):
    return jax.shard_map(
        local,
        mesh=mesh,
        in_specs=(
            P(("grp", "sec"), None, None, None),
            P("op", ("grp", "sec"), None, None),
            P("op", ("grp", "sec"), None, None),
            P(None, "grp"),
            P("grp"),
        ),
        out_specs=P(("grp", "sec"), None, "op", None),
        check_vma=False,
    )
```

time: 52.8 us -> 45.9 us (0.87)
  the two profiles are of different devices: /device:TPU:25 before, /device:TPU:0 now
where the time goes in v4:
time: 45.9 us; the launch traced here: 45.7 us
  waiting for transfers between devices  18.4 us (40%)
  starting transfers between devices  16.5 us (36%)
  Pallas kernels  9.22 us (20%)
  other arithmetic  1.19 us (3%)
    ppermute x15, waiting for transfers between devices, ship(): return lax.ppermute(x, axis, [(i, i ^ d) for i in range(n)])  18.4 us
    ppermute x15, starting transfers between devices, ship(): return lax.ppermute(x, axis, [(i, i ^ d) for i in range(n)])  16.5 us
    pallas_call x3, Pallas kernels, group(): pl.pallas_call(functools.partial(work_kernel, rounds, len(after), nsec, n...  6.17 us
    pallas_call x1, Pallas kernels, local(): pl.pallas_call(functools.partial(pick_kernel, nsec, nop, nb), in_specs=[S...  2.79 us
  transfers between devices with their start and end apart: 15, of which 9 were waited for; matrix products, arithmetic and copies ran while one was open for 1% of the time, Pallas kernels for 14%

profile of v4, /device:TPU:0, one launch (start us, length us, event | category | flops | bytes accessed | tf_op | source)
XLA Modules:
  0.0 45.7 jit_solution(4788212500378365044)
XLA Ops:
  0.0 2.8 %pick.1 = (bf16[2,64,256]{2,1,0:T(8,128)(2,1)}, bf16[2,64,256]{2,1,0:T(8,128)(2,1)}, bf16[2,64,256]{2,1,0:T(8,128)(2,1)}, bf16[2,256,256]{2,1,0:T(8,128)(2,1)}, ...) custom-call(s32[16]{0:T(128)} %place.5, bf16[4,2,256,256]{3,2,1,0:T(8,128)(2,1)} %psi.5, ...), custom_call_target="tpu_custom_call" | custom-call | tf_op jit(solution)/shard_map/pick/pallas_call | solution.py:137
  2.8 3.1 %collective-permute-start.2 = (bf16[2,64,256]{2,1,0:T(8,128)(2,1)}, bf16[2,64,256]{2,1,0:T(8,128)(2,1)S(1)}, u32[]{:S(2)}, u32[]{:S(2)}) collective-permute-start(bf16[2,64,256]{2,1,0:T(8,128)(2,1)} %get-tuple-element.49), channel_id=1, source_target_pairs={{0,1},{1,0},{2,3},{3,2},{4,5},{5,4},{6,7},{7,6},{8,9},{9,8},{10,11... | collective-permute-start | bytes 196616 | tf_op jit(solution)/shard_map/ppermute | solution.py:132
  5.9 2.6 %collective-permute-start.3 = (bf16[2,64,256]{2,1,0:T(8,128)(2,1)}, bf16[2,64,256]{2,1,0:T(8,128)(2,1)S(1)}, u32[]{:S(2)}, u32[]{:S(2)}) collective-permute-start(bf16[2,64,256]{2,1,0:T(8,128)(2,1)} %get-tuple-element.50), channel_id=1, source_target_pairs={{0,2},{1,3},{2,0},{3,1},{4,6},{5,7},{6,4},{7,5},{8,10},{9,11},{10,... | collective-permute-start | bytes 196616 | tf_op jit(solution)/shard_map/ppermute | solution.py:132
  8.5 0.0 collective-permute-start.4
  8.5 0.9 %collective-permute-start.8 = (bf16[2,256,256]{2,1,0:T(8,128)(2,1)}, bf16[2,256,256]{2,1,0:T(8,128)(2,1)}, u32[]{:S(2)}, u32[]{:S(2)}) collective-permute-start(bf16[2,256,256]{2,1,0:T(8,128)(2,1)} %get-tuple-element.52), channel_id=1, source_target_pairs={{0,1},{1,0},{2,3},{3,2},{4,5},{5,4},{6,7},{7,6},{8,9},{9,8},{10,11... | collective-permute-start | bytes 786440 | tf_op jit(solution)/shard_map/ppermute | solution.py:132
  9.4 2.9 %collective-permute-start.9 = (bf16[2,256,256]{2,1,0:T(8,128)(2,1)}, bf16[2,256,256]{2,1,0:T(8,128)(2,1)S(1)}, u32[]{:S(2)}, u32[]{:S(2)}) collective-permute-start(bf16[2,256,256]{2,1,0:T(8,128)(2,1)} %get-tuple-element.54), channel_id=1, source_target_pairs={{0,3},{1,2},{2,1},{3,0},{4,7},{5,6},{6,5},{7,4},{8,11},{9,10},{10,... | collective-permute-start | bytes 786440 | tf_op jit(solution)/shard_map/ppermute | solution.py:132
  12.3 0.0 collective-permute-done.2.refs_0_
  12.3 0.0 copy-start
  12.3 0.0 copy-start.1
  12.3 0.0 copy-start.2
  12.3 0.6 %collective-permute-start.12 = (bf16[2,256,256]{2,1,0:T(8,128)(2,1)}, bf16[2,256,256]{2,1,0:T(8,128)(2,1)S(1)}, u32[]{:S(2)}, u32[]{:S(2)}) collective-permute-start(bf16[2,256,256]{2,1,0:T(8,128)(2,1)} %get-tuple-element.57), channel_id=1, source_target_pairs={{0,2},{1,3},{2,0},{3,1},{4,6},{5,7},{6,4},{7,5},{8,10},{9,11},{10,... | collective-permute-start | bytes 786440 | tf_op jit(solution)/shard_map/ppermute | solution.py:132
  13.0 0.5 %collective-permute-done.3.refs_1_ = bf16[2,64,256]{2,1,0:T(8,128)(2,1)S(1)} collective-permute-done((bf16[2,64,256]{2,1,0:T(8,128)(2,1)}, bf16[2,64,256]{2,1,0:T(8,128)(2,1)S(1)}, u32[]{:S(2)}, u32[]{:S(2)}) %collective-permute-start.3) | collective-permute-done | bytes 65568 | tf_op jit(solution)/shard_map/ppermute | solution.py:132
  13.5 2.1 %collective-permute-done.4.refs_2_ = bf16[2,64,256]{2,1,0:T(8,128)(2,1)S(1)} collective-permute-done((bf16[2,64,256]{2,1,0:T(8,128)(2,1)}, bf16[2,64,256]{2,1,0:T(8,128)(2,1)S(1)}, u32[]{:S(2)}, u32[]{:S(2)}) %collective-permute-start.4) | collective-permute-done | bytes 65568 | tf_op jit(solution)/shard_map/ppermute | solution.py:132
  15.5 0.3 stack.1.rest_1_
  15.8 0.0 copy-start.5
  15.8 1.6 %collective-permute-start.6 = (bf16[3,2,64,256]{3,2,1,0:T(8,128)(2,1)S(1)}, bf16[3,2,64,256]{3,2,1,0:T(8,128)(2,1)S(1)}, u32[]{:S(2)}, u32[]{:S(2)}) collective-permute-start(bf16[3,2,64,256]{3,2,1,0:T(8,128)(2,1)S(1)} %stack.1.rest_1_), channel_id=1, source_target_pairs={{0,8},{4,12},{8,0},{12,4},{1,9},{5,13},{9,1},{13,5},{2,10},{6,14},... | collective-permute-start | bytes 589832 | tf_op jit(solution)/shard_map/ppermute | solution.py:132
  17.4 0.0 copy-done.5
  17.4 0.2 select_reduce_fusion
  17.5 0.1 collective-permute-start.5
  17.6 3.9 %collective-permute-done.6.rest_3_ = bf16[3,2,64,256]{3,2,1,0:T(8,128)(2,1)S(1)} collective-permute-done((bf16[3,2,64,256]{3,2,1,0:T(8,128)(2,1)S(1)}, bf16[3,2,64,256]{3,2,1,0:T(8,128)(2,1)S(1)}, u32[]{:S(2)}, u32[]{:S(2)}) %collective-permute-start.6) | collective-permute-done | bytes 196640 | tf_op jit(solution)/shard_map/ppermute | solution.py:132
  21.5 0.0 collective-permute-start.7
  21.6 0.0 copy-start.4
  21.6 0.0 collective-permute-done.5.rest_2_
  21.6 0.0 collective-permute-done.8
  21.6 1.3 %collective-permute-done.7.rest_4_ = bf16[3,2,64,256]{3,2,1,0:T(8,128)(2,1)S(1)} collective-permute-done((bf16[3,2,64,256]{3,2,1,0:T(8,128)(2,1)S(1)}, bf16[3,2,64,256]{3,2,1,0:T(8,128)(2,1)S(1)}, u32[]{:S(2)}, u32[]{:S(2)}) %collective-permute-start.7) | collective-permute-done | bytes 196640 | tf_op jit(solution)/shard_map/ppermute | solution.py:132
  23.0 0.0 copy-done
  23.0 0.0 copy-done.1
  23.0 0.0 copy-done.2
  23.0 0.0 copy-done.4
  23.0 9.9 %conditional.1 = (bf16[2,64,256]{2,1,0:T(8,128)(2,1)S(1)}, bf16[2,64,256]{2,1,0:T(8,128)(2,1)S(1)}) conditional(s32[]{:T(128)} %bitcast.2, () %tuple.13, (s32[16]{0:T(128)S(1)}, s32[2,16]{1,0:T(2,128)S(1)}, bf16[4,2,256,256]{3,2,1,0:T(8,128)(2,1)S(1)}, bf16[2,4,256,256]{3,2,1,0:T(8,128)(2,1)S(1)}, bf16[2,4,256,256]{3,2,1,0:T(8,128)(2,1)S(1)}, ...), branch_computations={%region_1.0_spmd, %region_2.3_spmd} | conditional | flops 458752 | bytes 3932256 | solution.py:203
  23.0 2.5 %work.3 = (f32[2,2,2,64,256]{4,3,2,1,0:T(8,128)S(1)}, bf16[2,2,2,64,256]{4,3,2,1,0:T(8,128)(2,1)S(1)}) custom-call(s32[16]{0:T(128)S(1)} %get-tuple-element.25.place, s32[2,16]{1,0:T(2,128)S(1)} %get-tuple-element.26.dims, bf16[4,2,256,256]{3,2,1,0:T(8,128)(2,1)S(1)} %get-tuple-element.27.psi, bf16[2,4,256,256]{3,2,1,0:T(8,128)(2,1)S(1)} %get-tuple-element.28.left_env, ...), custom_call_target="tpu_custom_call" | custom-call | tf_op jit(solution)/shard_map/cond/branch_1_fun/work/pallas_call | solution.py:172
  25.5 0.2 collective-permute-start
  25.7 1.4 %collective-permute-done = bf16[2,2,2,64,256]{4,3,2,1,0:T(8,128)(2,1)S(1)} collective-permute-done((bf16[2,2,2,64,256]{4,3,2,1,0:T(8,128)(2,1)S(1)}, bf16[2,2,2,64,256]{4,3,2,1,0:T(8,128)(2,1)S(1)}, u32[]{:S(2)}, u32[]{:S(2)}) %collective-permute-start) | collective-permute-done | bytes 262176 | tf_op jit(solution)/shard_map/cond/branch_1_fun/ppermute | solution.py:132
  27.2 0.1 convert_add_fusion
  27.2 1.6 %collective-permute-start.1 = (bf16[1,2,2,64,256]{4,3,2,1,0:T(8,128)(2,1)S(1)}, bf16[1,2,2,64,256]{4,3,2,1,0:T(8,128)(2,1)S(1)}, u32[]{:S(2)}, u32[]{:S(2)}) collective-permute-start(bf16[1,2,2,64,256]{4,3,2,1,0:T(8,128)(2,1)S(1)} %slice.59), channel_id=1, source_target_pairs={{0,8},{4,12},{8,0},{12,4},{1,9},{5,13},{9,1},{13,5},{2,10},{6,14},... | collective-permute-start | bytes 393224 | tf_op jit(solution)/shard_map/cond/branch_1_fun/ppermute | solution.py:132
  28.8 4.1 %collective-permute-done.1 = bf16[1,2,2,64,256]{4,3,2,1,0:T(8,128)(2,1)S(1)} collective-permute-done((bf16[1,2,2,64,256]{4,3,2,1,0:T(8,128)(2,1)S(1)}, bf16[1,2,2,64,256]{4,3,2,1,0:T(8,128)(2,1)S(1)}, u32[]{:S(2)}, u32[]{:S(2)}) %collective-permute-start.1) | collective-permute-done | bytes 131104 | tf_op jit(solution)/shard_map/cond/branch_1_fun/ppermute | solution.py:132
  32.9 0.0 collective-permute-done.9.rest_5_
  32.9 0.0 copy-start.3
  32.9 2.1 %work.4 = (f32[2,1,2,64,256]{4,3,2,1,0:T(8,128)S(1)}, bf16[2,1,2,64,256]{4,3,2,1,0:T(8,128)(2,1)S(1)}) custom-call(s32[16]{0:T(128)S(1)} %copy-done.5, s32[2,16]{1,0:T(2,128)S(1)} %copy-done.4, bf16[4,2,256,256]{3,2,1,0:T(8,128)(2,1)S(1)} %copy-done, bf16[2,4,256,256]{3,2,1,0:T(8,128)(2,1)S(1)} %copy-done.1, bf16[2,4,256,256]{3,2,1,0:T(8,128)(2,1)} %right_env.3, ...), custom_call_target="tpu_custom_call" | custom-call | tf_op jit(solution)/shard_map/work/pallas_call | solution.py:172
  35.0 0.1 collective-permute-start.10
  35.1 2.1 %collective-permute-done.12.rest_5_ = bf16[2,256,256]{2,1,0:T(8,128)(2,1)S(1)} collective-permute-done((bf16[2,256,256]{2,1,0:T(8,128)(2,1)}, bf16[2,256,256]{2,1,0:T(8,128)(2,1)S(1)}, u32[]{:S(2)}, u32[]{:S(2)}) %collective-permute-start.12) | collective-permute-done | bytes 262176 | tf_op jit(solution)/shard_map/ppermute | solution.py:132
  37.2 0.0 copy-done.3
  37.2 1.5 %work.5 = (f32[2,1,2,64,256]{4,3,2,1,0:T(8,128)S(1)}, bf16[2,1,2,64,256]{4,3,2,1,0:T(8,128)(2,1)S(1)}) custom-call(s32[16]{0:T(128)S(1)} %copy-done.5, s32[2,16]{1,0:T(2,128)S(1)} %copy-done.4, bf16[4,2,256,256]{3,2,1,0:T(8,128)(2,1)S(1)} %copy-done, bf16[2,4,256,256]{3,2,1,0:T(8,128)(2,1)S(1)} %copy-done.1, bf16[2,4,256,256]{3,2,1,0:T(8,128)(2,1)S(1)} %copy-done.3, ...), custom_call_target="tpu_custom_call" | custom-call | tf_op jit(solution)/shard_map/work/pallas_call | solution.py:172
  38.8 0.1 collective-permute-start.13
  38.9 0.0 collective-permute-done.10
  38.9 1.6 %collective-permute-start.11 = (bf16[1,1,2,64,256]{4,3,2,1,0:T(8,128)(2,1)S(1)}, bf16[1,1,2,64,256]{4,3,2,1,0:T(8,128)(2,1)S(1)}, u32[]{:S(2)}, u32[]{:S(2)}) collective-permute-start(bf16[1,1,2,64,256]{4,3,2,1,0:T(8,128)(2,1)S(1)} %slice.61), channel_id=1, source_target_pairs={{0,8},{4,12},{8,0},{12,4},{1,9},{5,13},{9,1},{13,5},{2,10},{6,14},... | collective-permute-start | bytes 196616 | tf_op jit(solution)/shard_map/ppermute | solution.py:132
  40.5 0.0 collective-permute-done.13
  40.5 1.3 %collective-permute-start.14 = (bf16[1,1,2,64,256]{4,3,2,1,0:T(8,128)(2,1)S(1)}, bf16[1,1,2,64,256]{4,3,2,1,0:T(8,128)(2,1)S(1)}, u32[]{:S(2)}, u32[]{:S(2)}) collective-permute-start(bf16[1,1,2,64,256]{4,3,2,1,0:T(8,128)(2,1)S(1)} %slice.60), channel_id=1, source_target_pairs={{0,8},{4,12},{8,0},{12,4},{1,9},{5,13},{9,1},{13,5},{2,10},{6,14},... | collective-permute-start | bytes 196616 | tf_op jit(solution)/shard_map/ppermute | solution.py:132
  41.8 1.8 %collective-permute-done.11 = bf16[1,1,2,64,256]{4,3,2,1,0:T(8,128)(2,1)S(1)} collective-permute-done((bf16[1,1,2,64,256]{4,3,2,1,0:T(8,128)(2,1)S(1)}, bf16[1,1,2,64,256]{4,3,2,1,0:T(8,128)(2,1)S(1)}, u32[]{:S(2)}, u32[]{:S(2)}) %collective-permute-start.11) | collective-permute-done | bytes 65568 | tf_op jit(solution)/shard_map/ppermute | solution.py:132
  43.6 1.3 %collective-permute-done.14 = bf16[1,1,2,64,256]{4,3,2,1,0:T(8,128)(2,1)S(1)} collective-permute-done((bf16[1,1,2,64,256]{4,3,2,1,0:T(8,128)(2,1)S(1)}, bf16[1,1,2,64,256]{4,3,2,1,0:T(8,128)(2,1)S(1)}, u32[]{:S(2)}, u32[]{:S(2)}) %collective-permute-start.14) | collective-permute-done | bytes 65568 | tf_op jit(solution)/shard_map/ppermute | solution.py:132
  44.9 0.8 %select_select_fusion = bf16[4,2,64,256]{3,2,1,0:T(8,128)(2,1)} fusion(pred[4]{0:T(512)(128)(4,1)S(1)} %get-tuple-element.66, pred[4]{0:T(512)(128)(4,1)S(1)} %get-tuple-element.65, pred[4]{0:T(512)(128)(4,1)S(1)} %get-tuple-element.61, bf16[2,64,256]{2,1,0:T(8,128)(2,1)S(1)} %get-tuple-element.53.rest_0_, bf16[2,64,256]{2,1,0:T(8,128)(2,1)S(1)} %get-tuple-element.60, ...), kind=kLoop, calls=%fused_computation.6 | loop fusion | flops 393216 | bytes 524300 | tf_op jit(solution)/shard_map/jit(_where)/select_n | solution.py:225
  (12 shorter events, 0.2 us)
Async XLA Ops:
  2.8 9.5 %collective-permute-start.2 = (bf16[2,64,256]{2,1,0:T(8,128)(2,1)}, bf16[2,64,256]{2,1,0:T(8,128)(2,1)S(1)}, u32[]{:S(2)}, u32[]{:S(2)}) collective-permute-start(bf16[2,64,256]{2,1,0:T(8,128)(2,1)} %get-tuple-element.49), channel_id=1, source_target_pairs={{0,1},{1,0},{2,3},{3,2},{4,5},{5,4},{6,7},{7,6},{8,9},{9,8},{10,11... | collective-permute-start | bytes 196616 | tf_op jit(solution)/shard_map/ppermute | solution.py:132
  5.9 7.6 %collective-permute-start.3 = (bf16[2,64,256]{2,1,0:T(8,128)(2,1)}, bf16[2,64,256]{2,1,0:T(8,128)(2,1)S(1)}, u32[]{:S(2)}, u32[]{:S(2)}) collective-permute-start(bf16[2,64,256]{2,1,0:T(8,128)(2,1)} %get-tuple-element.50), channel_id=1, source_target_pairs={{0,2},{1,3},{2,0},{3,1},{4,6},{5,7},{6,4},{7,5},{8,10},{9,11},{10,... | collective-permute-start | bytes 196616 | tf_op jit(solution)/shard_map/ppermute | solution.py:132
  8.5 7.0 %collective-permute-start.4 = (bf16[2,64,256]{2,1,0:T(8,128)(2,1)}, bf16[2,64,256]{2,1,0:T(8,128)(2,1)S(1)}, u32[]{:S(2)}, u32[]{:S(2)}) collective-permute-start(bf16[2,64,256]{2,1,0:T(8,128)(2,1)} %get-tuple-element.51), channel_id=1, source_target_pairs={{0,3},{1,2},{2,1},{3,0},{4,7},{5,6},{6,5},{7,4},{8,11},{9,10},{10,... | collective-permute-start | bytes 196616 | tf_op jit(solution)/shard_map/ppermute | solution.py:132
  8.5 13.1 %collective-permute-start.8 = (bf16[2,256,256]{2,1,0:T(8,128)(2,1)}, bf16[2,256,256]{2,1,0:T(8,128)(2,1)}, u32[]{:S(2)}, u32[]{:S(2)}) collective-permute-start(bf16[2,256,256]{2,1,0:T(8,128)(2,1)} %get-tuple-element.52), channel_id=1, source_target_pairs={{0,1},{1,0},{2,3},{3,2},{4,5},{5,4},{6,7},{7,6},{8,9},{9,8},{10,11... | collective-permute-start | bytes 786440 | tf_op jit(solution)/shard_map/ppermute | solution.py:132
  9.4 23.5 %collective-permute-start.9 = (bf16[2,256,256]{2,1,0:T(8,128)(2,1)}, bf16[2,256,256]{2,1,0:T(8,128)(2,1)S(1)}, u32[]{:S(2)}, u32[]{:S(2)}) collective-permute-start(bf16[2,256,256]{2,1,0:T(8,128)(2,1)} %get-tuple-element.54), channel_id=1, source_target_pairs={{0,3},{1,2},{2,1},{3,0},{4,7},{5,6},{6,5},{7,4},{8,11},{9,10},{10,... | collective-permute-start | bytes 786440 | tf_op jit(solution)/shard_map/ppermute | solution.py:132
  12.3 10.7 %copy-start = (bf16[4,2,256,256]{3,2,1,0:T(8,128)(2,1)S(1)}, bf16[4,2,256,256]{3,2,1,0:T(8,128)(2,1)}, u32[]{:S(2)}) copy-start(bf16[4,2,256,256]{3,2,1,0:T(8,128)(2,1)} %psi.5) | copy-start | bytes 3145732
  12.3 10.7 %copy-start.1 = (bf16[2,4,256,256]{3,2,1,0:T(8,128)(2,1)S(1)}, bf16[2,4,256,256]{3,2,1,0:T(8,128)(2,1)}, u32[]{:S(2)}) copy-start(bf16[2,4,256,256]{3,2,1,0:T(8,128)(2,1)} %left_env.5) | copy-start | bytes 3145732
  12.3 10.7 %copy-start.2 = (bf16[2,4,256,256]{3,2,1,0:T(8,128)(2,1)S(1)}, bf16[2,4,256,256]{3,2,1,0:T(8,128)(2,1)}, u32[]{:S(2)}) copy-start(bf16[2,4,256,256]{3,2,1,0:T(8,128)(2,1)} %right_env.3) | copy-start | bytes 3145732
  12.3 24.9 %collective-permute-start.12 = (bf16[2,256,256]{2,1,0:T(8,128)(2,1)}, bf16[2,256,256]{2,1,0:T(8,128)(2,1)S(1)}, u32[]{:S(2)}, u32[]{:S(2)}) collective-permute-start(bf16[2,256,256]{2,1,0:T(8,128)(2,1)} %get-tuple-element.57), channel_id=1, source_target_pairs={{0,2},{1,3},{2,0},{3,1},{4,6},{5,7},{6,4},{7,5},{8,10},{9,11},{10,... | collective-permute-start | bytes 786440 | tf_op jit(solution)/shard_map/ppermute | solution.py:132
  15.8 1.6 %copy-start.5 = (s32[16]{0:T(128)S(1)}, s32[16]{0:T(128)}, u32[]{:S(2)}) copy-start(s32[16]{0:T(128)} %place.5) | copy-start | bytes 196
  15.8 5.7 %collective-permute-start.6 = (bf16[3,2,64,256]{3,2,1,0:T(8,128)(2,1)S(1)}, bf16[3,2,64,256]{3,2,1,0:T(8,128)(2,1)S(1)}, u32[]{:S(2)}, u32[]{:S(2)}) collective-permute-start(bf16[3,2,64,256]{3,2,1,0:T(8,128)(2,1)S(1)} %stack.1.rest_1_), channel_id=1, source_target_pairs={{0,8},{4,12},{8,0},{12,4},{1,9},{5,13},{9,1},{13,5},{2,10},{6,14},... | collective-permute-start | bytes 589832 | tf_op jit(solution)/shard_map/ppermute | solution.py:132
  17.5 4.1 %collective-permute-start.5 = (bf16[3,2,64,256]{3,2,1,0:T(8,128)(2,1)S(1)}, bf16[3,2,64,256]{3,2,1,0:T(8,128)(2,1)S(1)}, u32[]{:S(2)}, u32[]{:S(2)}) collective-permute-start(bf16[3,2,64,256]{3,2,1,0:T(8,128)(2,1)S(1)} %stack.1.rest_1_), channel_id=1, source_target_pairs={{0,4},{4,0},{8,12},{12,8},{1,5},{5,1},{9,13},{13,9},{2,6},{6,2},{1... | collective-permute-start | bytes 589832 | tf_op jit(solution)/shard_map/ppermute | solution.py:132
  21.5 1.4 %collective-permute-start.7 = (bf16[3,2,64,256]{3,2,1,0:T(8,128)(2,1)S(1)}, bf16[3,2,64,256]{3,2,1,0:T(8,128)(2,1)S(1)}, u32[]{:S(2)}, u32[]{:S(2)}) collective-permute-start(bf16[3,2,64,256]{3,2,1,0:T(8,128)(2,1)S(1)} %collective-permute-done.6.rest_3_), channel_id=1, source_target_pairs={{0,4},{4,0},{8,12},{12,8},{1,5},{5,1},{9,13},{13,9},{2,6},{6,2},{1... | collective-permute-start | bytes 589832 | tf_op jit(solution)/shard_map/ppermute | solution.py:132
  21.6 1.4 %copy-start.4 = (s32[2,16]{1,0:T(2,128)S(1)}, s32[2,16]{1,0:T(2,128)}, u32[]{:S(2)}) copy-start(s32[2,16]{1,0:T(2,128)} %dims.3) | copy-start | bytes 388
  25.5 1.6 %collective-permute-start = (bf16[2,2,2,64,256]{4,3,2,1,0:T(8,128)(2,1)S(1)}, bf16[2,2,2,64,256]{4,3,2,1,0:T(8,128)(2,1)S(1)}, u32[]{:S(2)}, u32[]{:S(2)}) collective-permute-start(bf16[2,2,2,64,256]{4,3,2,1,0:T(8,128)(2,1)S(1)} %get-tuple-element.36), channel_id=1, source_target_pairs={{0,4},{4,0},{8,12},{12,8},{1,5},{5,1},{9,13},{13,9},{2,6},{6,2},{1... | collective-permute-start | bytes 786440 | tf_op jit(solution)/shard_map/cond/branch_1_fun/ppermute | solution.py:132
  27.2 5.6 %collective-permute-start.1 = (bf16[1,2,2,64,256]{4,3,2,1,0:T(8,128)(2,1)S(1)}, bf16[1,2,2,64,256]{4,3,2,1,0:T(8,128)(2,1)S(1)}, u32[]{:S(2)}, u32[]{:S(2)}) collective-permute-start(bf16[1,2,2,64,256]{4,3,2,1,0:T(8,128)(2,1)S(1)} %slice.59), channel_id=1, source_target_pairs={{0,8},{4,12},{8,0},{12,4},{1,9},{5,13},{9,1},{13,5},{2,10},{6,14},... | collective-permute-start | bytes 393224 | tf_op jit(solution)/shard_map/cond/branch_1_fun/ppermute | solution.py:132
  32.9 4.3 %copy-start.3 = (bf16[2,4,256,256]{3,2,1,0:T(8,128)(2,1)S(1)}, bf16[2,4,256,256]{3,2,1,0:T(8,128)(2,1)}, u32[]{:S(2)}) copy-start(bf16[2,4,256,256]{3,2,1,0:T(8,128)(2,1)} %right_env.3) | copy-start | bytes 3145732
  35.0 3.8 %collective-permute-start.10 = (bf16[2,1,2,64,256]{4,3,2,1,0:T(8,128)(2,1)S(1)}, bf16[2,1,2,64,256]{4,3,2,1,0:T(8,128)(2,1)S(1)}, u32[]{:S(2)}, u32[]{:S(2)}) collective-permute-start(bf16[2,1,2,64,256]{4,3,2,1,0:T(8,128)(2,1)S(1)} %get-tuple-element.56), channel_id=1, source_target_pairs={{0,4},{4,0},{8,12},{12,8},{1,5},{5,1},{9,13},{13,9},{2,6},{6,2},{1... | collective-permute-start | bytes 393224 | tf_op jit(solution)/shard_map/ppermute | solution.py:132
  38.8 1.7 %collective-permute-start.13 = (bf16[2,1,2,64,256]{4,3,2,1,0:T(8,128)(2,1)S(1)}, bf16[2,1,2,64,256]{4,3,2,1,0:T(8,128)(2,1)S(1)}, u32[]{:S(2)}, u32[]{:S(2)}) collective-permute-start(bf16[2,1,2,64,256]{4,3,2,1,0:T(8,128)(2,1)S(1)} %get-tuple-element.59), channel_id=1, source_target_pairs={{0,4},{4,0},{8,12},{12,8},{1,5},{5,1},{9,13},{13,9},{2,6},{6,2},{1... | collective-permute-start | bytes 393224 | tf_op jit(solution)/shard_map/ppermute | solution.py:132
  38.9 4.6 %collective-permute-start.11 = (bf16[1,1,2,64,256]{4,3,2,1,0:T(8,128)(2,1)S(1)}, bf16[1,1,2,64,256]{4,3,2,1,0:T(8,128)(2,1)S(1)}, u32[]{:S(2)}, u32[]{:S(2)}) collective-permute-start(bf16[1,1,2,64,256]{4,3,2,1,0:T(8,128)(2,1)S(1)} %slice.61), channel_id=1, source_target_pairs={{0,8},{4,12},{8,0},{12,4},{1,9},{5,13},{9,1},{13,5},{2,10},{6,14},... | collective-permute-start | bytes 196616 | tf_op jit(solution)/shard_map/ppermute | solution.py:132
  40.5 4.3 %collective-permute-start.14 = (bf16[1,1,2,64,256]{4,3,2,1,0:T(8,128)(2,1)S(1)}, bf16[1,1,2,64,256]{4,3,2,1,0:T(8,128)(2,1)S(1)}, u32[]{:S(2)}, u32[]{:S(2)}) collective-permute-start(bf16[1,1,2,64,256]{4,3,2,1,0:T(8,128)(2,1)S(1)} %slice.60), channel_id=1, source_target_pairs={{0,8},{4,12},{8,0},{12,4},{1,9},{5,13},{9,1},{13,5},{2,10},{6,14},... | collective-permute-start | bytes 196616 | tf_op jit(solution)/shard_map/ppermute | solution.py:132

commit v5 on v4

--- a/solution.py
+++ b/solution.py
@@ -14,7 +14,6 @@
 F32 = jnp.float32
 BF16 = jnp.bfloat16
 EVERY = slice(None)
-LONG = 10**11
 
 
 def find(place, nb, left, right):
@@ -140,7 +139,7 @@
         out_specs=[VMEM] * (2 * away),
         out_shape=[shape(vecs, rows, width)] * away + [shape(terms, width, width)] * away,
         scratch_shapes=[dma(2 * away)],
-        compiler_params=pltpu.CompilerParams(vmem_limit_bytes=61 * 2**20),
+        compiler_params=pltpu.CompilerParams(vmem_limit_bytes=40 * 2**20),
         cost_estimate=cost(0, 0),
         name="pick",
     )(right_place, psi, left_env)
@@ -155,7 +154,7 @@
             out_shape=shape(away, vecs, rows, width),
             scratch_shapes=[dma(away)],
             compiler_params=params,
-            cost_estimate=cost(LONG, 0),
+            cost_estimate=cost(0, 0),
             name="stack",
         )(*pieces)
         gathered = {0: stacked}
@@ -204,7 +203,7 @@
 
     gathered = gather(pieces)
     half = nsec // 2 + 1
-    groups = [([0, 1], True, []), (list(range(2, half)), False, [0]), (list(range(half, nsec)), False, [0])]
+    groups = [([1], True, []), (list(range(2, half)), False, [1]), ([0, *range(half, nsec)], False, [1])]
     ready = {}
     for rounds, apart, waits in groups:
         arrived = {d: lefts[d] for d in rounds if d}

time: 45.9 us -> 44.8 us (0.976)
  waiting for transfers between devices: 18.4 us -> 17.5 us
    ppermute x15, waiting for transfers between devices: 18.4 us -> 17.5 us  [ship(): return lax.ppermute(x, axis, [(i, i ^ d) for i in range(n)])]
    pallas_call x1, Pallas kernels: 2.79 us -> 1.98 us  [local(): pl.pallas_call(functools.partial(pick_kernel, nsec, nop, nb), in_specs=[S...]
  transfers between devices with their start and end apart: 15 -> 15, of which waited for: 9 -> 9; matrix products, arithmetic and copies ran while one was open for 1% -> 1% of each run, Pallas kernels for 14% -> 15%
where the time goes in v5:
time: 44.8 us; the launch traced here: 44.6 us
  waiting for transfers between devices  17.5 us (39%)
  starting transfers between devices  16.7 us (37%)
  Pallas kernels  8.77 us (20%)
  other arithmetic  1.19 us (3%)
    ppermute x15, waiting for transfers between devices, ship(): return lax.ppermute(x, axis, [(i, i ^ d) for i in range(n)])  17.5 us
    ppermute x15, starting transfers between devices, ship(): return lax.ppermute(x, axis, [(i, i ^ d) for i in range(n)])  16.7 us
    pallas_call x3, Pallas kernels, group(): pl.pallas_call(functools.partial(work_kernel, rounds, len(after), nsec, n...  6.54 us
    pallas_call x1, Pallas kernels, local(): pl.pallas_call(functools.partial(pick_kernel, nsec, nop, nb), in_specs=[S...  1.98 us
  transfers between devices with their start and end apart: 15, of which 9 were waited for; matrix products, arithmetic and copies ran while one was open for 1% of the time, Pallas kernels for 15%

profile of v5, /device:TPU:0, one launch (start us, length us, event | category | flops | bytes accessed | tf_op | source)
XLA Modules:
  0.0 44.6 jit_solution(17570484187081144857)
XLA Ops:
  0.0 0.0 copy-start
  0.0 2.0 %pick.1 = (bf16[2,64,256]{2,1,0:T(8,128)(2,1)S(1)}, bf16[2,64,256]{2,1,0:T(8,128)(2,1)S(1)}, bf16[2,64,256]{2,1,0:T(8,128)(2,1)S(1)}, bf16[2,256,256]{2,1,0:T(8,...) custom-call(s32[16]{0:T(128)} %place.5, bf16[4,2,256,256]{3,2,1,0:T(8,128)(2,1)} %psi.5, ...), custom_call_target="tpu_custom_call" | custom-call | tf_op jit(solution)/shard_map/pick/pallas_call | solution.py:136
  2.0 3.1 %collective-permute-start.2 = (bf16[2,64,256]{2,1,0:T(8,128)(2,1)S(1)}, bf16[2,64,256]{2,1,0:T(8,128)(2,1)S(1)}, u32[]{:S(2)}, u32[]{:S(2)}) collective-permute-start(bf16[2,64,256]{2,1,0:T(8,128)(2,1)S(1)} %get-tuple-element.50), channel_id=1, source_target_pairs={{0,1},{1,0},{2,3},{3,2},{4,5},{5,4},{6,7},{7,6},{8,9},{9,8},{10,11... | collective-permute-start | bytes 196616 | tf_op jit(solution)/shard_map/ppermute | solution.py:131
  5.1 2.6 %collective-permute-start.3 = (bf16[2,64,256]{2,1,0:T(8,128)(2,1)S(1)}, bf16[2,64,256]{2,1,0:T(8,128)(2,1)S(1)}, u32[]{:S(2)}, u32[]{:S(2)}) collective-permute-start(bf16[2,64,256]{2,1,0:T(8,128)(2,1)S(1)} %get-tuple-element.51), channel_id=1, source_target_pairs={{0,2},{1,3},{2,0},{3,1},{4,6},{5,7},{6,4},{7,5},{8,10},{9,11},{10,... | collective-permute-start | bytes 196616 | tf_op jit(solution)/shard_map/ppermute | solution.py:131
  7.7 0.0 collective-permute-start.4
  7.7 0.9 %collective-permute-start.8 = (bf16[2,256,256]{2,1,0:T(8,128)(2,1)S(1)}, bf16[2,256,256]{2,1,0:T(8,128)(2,1)S(1)}, u32[]{:S(2)}, u32[]{:S(2)}) collective-permute-start(bf16[2,256,256]{2,1,0:T(8,128)(2,1)S(1)} %get-tuple-element.53), channel_id=1, source_target_pairs={{0,1},{1,0},{2,3},{3,2},{4,5},{5,4},{6,7},{7,6},{8,9},{9,8},{10,11... | collective-permute-start | bytes 786440 | tf_op jit(solution)/shard_map/ppermute | solution.py:131
  8.6 3.5 %collective-permute-start.12 = (bf16[2,256,256]{2,1,0:T(8,128)(2,1)S(1)}, bf16[2,256,256]{2,1,0:T(8,128)(2,1)S(1)}, u32[]{:S(2)}, u32[]{:S(2)}) collective-permute-start(bf16[2,256,256]{2,1,0:T(8,128)(2,1)S(1)} %get-tuple-element.57), channel_id=1, source_target_pairs={{0,2},{1,3},{2,0},{3,1},{4,6},{5,7},{6,4},{7,5},{8,10},{9,11},{10,... | collective-permute-start | bytes 786440 | tf_op jit(solution)/shard_map/ppermute | solution.py:131
  12.1 0.0 collective-permute-done.2.refs_0_
  12.1 0.0 collective-permute-start.9
  12.1 0.4 collective-permute-done.3.refs_1_
  12.5 2.0 %collective-permute-done.4.refs_2_ = bf16[2,64,256]{2,1,0:T(8,128)(2,1)S(1)} collective-permute-done((bf16[2,64,256]{2,1,0:T(8,128)(2,1)S(1)}, bf16[2,64,256]{2,1,0:T(8,128)(2,1)S(1)}, u32[]{:S(2)}, u32[]{:S(2)}) %collective-permute-start.4) | collective-permute-done | bytes 65568 | tf_op jit(solution)/shard_map/ppermute | solution.py:131
  14.5 0.3 stack.1.rest_1_
  14.8 0.0 copy-start.4
  14.8 1.6 %collective-permute-start.6 = (bf16[3,2,64,256]{3,2,1,0:T(8,128)(2,1)S(1)}, bf16[3,2,64,256]{3,2,1,0:T(8,128)(2,1)S(1)}, u32[]{:S(2)}, u32[]{:S(2)}) collective-permute-start(bf16[3,2,64,256]{3,2,1,0:T(8,128)(2,1)S(1)} %stack.1.rest_1_), channel_id=1, source_target_pairs={{0,8},{4,12},{8,0},{12,4},{1,9},{5,13},{9,1},{13,5},{2,10},{6,14},... | collective-permute-start | bytes 589832 | tf_op jit(solution)/shard_map/ppermute | solution.py:131
  16.3 0.0 copy-done.4
  16.3 0.2 select_reduce_fusion
  16.6 0.1 collective-permute-start.5
  16.7 3.9 %collective-permute-done.6.rest_3_ = bf16[3,2,64,256]{3,2,1,0:T(8,128)(2,1)S(1)} collective-permute-done((bf16[3,2,64,256]{3,2,1,0:T(8,128)(2,1)S(1)}, bf16[3,2,64,256]{3,2,1,0:T(8,128)(2,1)S(1)}, u32[]{:S(2)}, u32[]{:S(2)}) %collective-permute-start.6) | collective-permute-done | bytes 196640 | tf_op jit(solution)/shard_map/ppermute | solution.py:131
  20.5 0.0 collective-permute-start.7
  20.5 0.0 copy-start.3
  20.5 0.0 collective-permute-done.5.rest_2_
  20.6 1.4 %collective-permute-done.8 = bf16[2,256,256]{2,1,0:T(8,128)(2,1)S(1)} collective-permute-done((bf16[2,256,256]{2,1,0:T(8,128)(2,1)S(1)}, bf16[2,256,256]{2,1,0:T(8,128)(2,1)S(1)}, u32[]{:S(2)}, u32[]{:S(2)}) %collective-permute-start.8) | collective-permute-done | bytes 262176 | tf_op jit(solution)/shard_map/ppermute | solution.py:131
  22.0 0.0 collective-permute-done.7.rest_4_
  22.0 0.0 copy-done
  22.0 0.0 copy-done.3
  22.0 8.0 %conditional.1 = (bf16[2,64,256]{2,1,0:T(8,128)(2,1)S(1)}) conditional(s32[]{:T(128)} %bitcast.1, () %tuple.11, (s32[16]{0:T(128)S(1)}, s32[2,16]{1,0:T(2,128)S(1)}, bf16[4,2,256,256]{3,2,1,0:T(8,128)(2,1)S(1)}, bf16[2,4,256,256]{3,2,1,0:T(8,128)(2,1)}, bf16[2,4,256,256]{3,2,1,0:T(8,128)(2,1)}, /*index=5*/bf16[3,2,64,256]{3,2,1,0:T(8,128)(2,1)S(1)}, ...), branch_computations={%region_1.0_spmd, %region_2.3_spmd} | conditional | flops 229376 | bytes 1835096 | solution.py:202
  22.0 2.1 %work.3 = (f32[2,1,2,64,256]{4,3,2,1,0:T(8,128)S(1)}, bf16[2,1,2,64,256]{4,3,2,1,0:T(8,128)(2,1)S(1)}) custom-call(s32[16]{0:T(128)S(1)} %get-tuple-element.28.place, s32[2,16]{1,0:T(2,128)S(1)} %get-tuple-element.29.dims, bf16[4,2,256,256]{3,2,1,0:T(8,128)(2,1)S(1)} %get-tuple-element.30.psi, bf16[2,4,256,256]{3,2,1,0:T(8,128)(2,1)} %get-tuple-element.31.left_env, ...), custom_call_target="tpu_custom_call" | custom-call | tf_op jit(solution)/shard_map/cond/branch_1_fun/work/pallas_call | solution.py:171
  24.1 0.2 collective-permute-start
  24.3 1.3 %collective-permute-done = bf16[2,1,2,64,256]{4,3,2,1,0:T(8,128)(2,1)S(1)} collective-permute-done((bf16[2,1,2,64,256]{4,3,2,1,0:T(8,128)(2,1)S(1)}, bf16[2,1,2,64,256]{4,3,2,1,0:T(8,128)(2,1)S(1)}, u32[]{:S(2)}, u32[]{:S(2)}) %collective-permute-start) | collective-permute-done | bytes 131104 | tf_op jit(solution)/shard_map/cond/branch_1_fun/ppermute | solution.py:131
  25.6 1.6 %collective-permute-start.1 = (bf16[1,1,2,64,256]{4,3,2,1,0:T(8,128)(2,1)S(1)}, bf16[1,1,2,64,256]{4,3,2,1,0:T(8,128)(2,1)S(1)}, u32[]{:S(2)}, u32[]{:S(2)}) collective-permute-start(bf16[1,1,2,64,256]{4,3,2,1,0:T(8,128)(2,1)S(1)} %slice.59), channel_id=1, source_target_pairs={{0,8},{4,12},{8,0},{12,4},{1,9},{5,13},{9,1},{13,5},{2,10},{6,14},... | collective-permute-start | bytes 196616 | tf_op jit(solution)/shard_map/cond/branch_1_fun/ppermute | solution.py:131
  27.2 2.8 %collective-permute-done.1 = bf16[1,1,2,64,256]{4,3,2,1,0:T(8,128)(2,1)S(1)} collective-permute-done((bf16[1,1,2,64,256]{4,3,2,1,0:T(8,128)(2,1)S(1)}, bf16[1,1,2,64,256]{4,3,2,1,0:T(8,128)(2,1)S(1)}, u32[]{:S(2)}, u32[]{:S(2)}) %collective-permute-start.1) | collective-permute-done | bytes 65568 | tf_op jit(solution)/shard_map/cond/branch_1_fun/ppermute | solution.py:131
  29.9 0.0 copy-start.1
  30.0 0.0 copy-start.2
  30.0 1.4 %collective-permute-done.12.rest_5_ = bf16[2,256,256]{2,1,0:T(8,128)(2,1)S(1)} collective-permute-done((bf16[2,256,256]{2,1,0:T(8,128)(2,1)S(1)}, bf16[2,256,256]{2,1,0:T(8,128)(2,1)S(1)}, u32[]{:S(2)}, u32[]{:S(2)}) %collective-permute-start.12) | collective-permute-done | bytes 262176 | tf_op jit(solution)/shard_map/ppermute | solution.py:131
  31.4 2.1 %work.5 = (f32[2,1,2,64,256]{4,3,2,1,0:T(8,128)S(1)}, bf16[2,1,2,64,256]{4,3,2,1,0:T(8,128)(2,1)S(1)}) custom-call(s32[16]{0:T(128)S(1)} %copy-done.4, s32[2,16]{1,0:T(2,128)S(1)} %copy-done.3, bf16[4,2,256,256]{3,2,1,0:T(8,128)(2,1)S(1)} %copy-done, bf16[2,4,256,256]{3,2,1,0:T(8,128)(2,1)} %left_env.5, bf16[2,4,256,256]{3,2,1,0:T(8,128)(2,1)} %right_env.3, ...), custom_call_target="tpu_custom_call" | custom-call | tf_op jit(solution)/shard_map/work/pallas_call | solution.py:171
  33.5 0.1 collective-permute-start.13
  33.6 0.0 collective-permute-done.9.rest_5_
  33.6 0.0 copy-done.1
  33.6 0.0 copy-done.2
  33.6 2.3 %work.4 = (f32[2,2,2,64,256]{4,3,2,1,0:T(8,128)S(1)}, bf16[2,2,2,64,256]{4,3,2,1,0:T(8,128)(2,1)S(1)}) custom-call(s32[16]{0:T(128)S(1)} %copy-done.4, s32[2,16]{1,0:T(2,128)S(1)} %copy-done.3, bf16[4,2,256,256]{3,2,1,0:T(8,128)(2,1)S(1)} %copy-done, bf16[2,4,256,256]{3,2,1,0:T(8,128)(2,1)S(1)} %copy-done.1, bf16[2,4,256,256]{3,2,1,0:T(8,128)(2,1)S(1)} %copy-done.2, ...), custom_call_target="tpu_custom_call" | custom-call | tf_op jit(solution)/shard_map/work/pallas_call | solution.py:171
  35.9 0.5 %collective-permute-start.10 = (bf16[2,2,2,64,256]{4,3,2,1,0:T(8,128)(2,1)S(1)}, bf16[2,2,2,64,256]{4,3,2,1,0:T(8,128)(2,1)S(1)}, u32[]{:S(2)}, u32[]{:S(2)}) collective-permute-start(bf16[2,2,2,64,256]{4,3,2,1,0:T(8,128)(2,1)S(1)} %get-tuple-element.56), channel_id=1, source_target_pairs={{0,4},{4,0},{8,12},{12,8},{1,5},{5,1},{9,13},{13,9},{2,6},{6,2},{1... | collective-permute-start | bytes 786440 | tf_op jit(solution)/shard_map/ppermute | solution.py:131
  36.5 0.0 collective-permute-done.13
  36.5 1.6 %collective-permute-start.14 = (bf16[1,1,2,64,256]{4,3,2,1,0:T(8,128)(2,1)S(1)}, bf16[1,1,2,64,256]{4,3,2,1,0:T(8,128)(2,1)S(1)}, u32[]{:S(2)}, u32[]{:S(2)}) collective-permute-start(bf16[1,1,2,64,256]{4,3,2,1,0:T(8,128)(2,1)S(1)} %slice.61), channel_id=1, source_target_pairs={{0,8},{4,12},{8,0},{12,4},{1,9},{5,13},{9,1},{13,5},{2,10},{6,14},... | collective-permute-start | bytes 196616 | tf_op jit(solution)/shard_map/ppermute | solution.py:131
  38.1 0.0 collective-permute-done.10
  38.1 0.1 convert_add_fusion.1
  38.2 1.1 %collective-permute-start.11 = (bf16[1,2,2,64,256]{4,3,2,1,0:T(8,128)(2,1)S(1)}, bf16[1,2,2,64,256]{4,3,2,1,0:T(8,128)(2,1)S(1)}, u32[]{:S(2)}, u32[]{:S(2)}) collective-permute-start(bf16[1,2,2,64,256]{4,3,2,1,0:T(8,128)(2,1)S(1)} %slice.60), channel_id=1, source_target_pairs={{0,8},{4,12},{8,0},{12,4},{1,9},{5,13},{9,1},{13,5},{2,10},{6,14},... | collective-permute-start | bytes 393224 | tf_op jit(solution)/shard_map/ppermute | solution.py:131
  39.3 1.7 %collective-permute-done.14 = bf16[1,1,2,64,256]{4,3,2,1,0:T(8,128)(2,1)S(1)} collective-permute-done((bf16[1,1,2,64,256]{4,3,2,1,0:T(8,128)(2,1)S(1)}, bf16[1,1,2,64,256]{4,3,2,1,0:T(8,128)(2,1)S(1)}, u32[]{:S(2)}, u32[]{:S(2)}) %collective-permute-start.14) | collective-permute-done | bytes 65568 | tf_op jit(solution)/shard_map/ppermute | solution.py:131
  41.0 2.6 %collective-permute-done.11 = bf16[1,2,2,64,256]{4,3,2,1,0:T(8,128)(2,1)S(1)} collective-permute-done((bf16[1,2,2,64,256]{4,3,2,1,0:T(8,128)(2,1)S(1)}, bf16[1,2,2,64,256]{4,3,2,1,0:T(8,128)(2,1)S(1)}, u32[]{:S(2)}, u32[]{:S(2)}) %collective-permute-start.11) | collective-permute-done | bytes 131104 | tf_op jit(solution)/shard_map/ppermute | solution.py:131
  43.7 0.8 %select_select_fusion = bf16[4,2,64,256]{3,2,1,0:T(8,128)(2,1)} fusion(pred[4]{0:T(512)(128)(4,1)S(1)} %get-tuple-element.65, pred[4]{0:T(512)(128)(4,1)S(1)} %get-tuple-element.64, pred[4]{0:T(512)(128)(4,1)S(1)} %get-tuple-element.60, bf16[2,64,256]{2,1,0:T(8,128)(2,1)S(1)} %get-tuple-element.63, bf16[2,64,256]{2,1,0:T(8,128)(2,1)S(1)} %get-tuple-element.66.rest_0_, ...), kind=kLoop, calls=%fused_computation.9 | loop fusion | flops 393216 | bytes 524300 | tf_op jit(solution)/shard_map/jit(_where)/select_n | solution.py:224
  (12 shorter events, 0.2 us)
Async XLA Ops:
  0.0 22.0 %copy-start = (bf16[4,2,256,256]{3,2,1,0:T(8,128)(2,1)S(1)}, bf16[4,2,256,256]{3,2,1,0:T(8,128)(2,1)}, u32[]{:S(2)}) copy-start(bf16[4,2,256,256]{3,2,1,0:T(8,128)(2,1)} %psi.5) | copy-start | bytes 3145732
  2.0 10.1 %collective-permute-start.2 = (bf16[2,64,256]{2,1,0:T(8,128)(2,1)S(1)}, bf16[2,64,256]{2,1,0:T(8,128)(2,1)S(1)}, u32[]{:S(2)}, u32[]{:S(2)}) collective-permute-start(bf16[2,64,256]{2,1,0:T(8,128)(2,1)S(1)} %get-tuple-element.50), channel_id=1, source_target_pairs={{0,1},{1,0},{2,3},{3,2},{4,5},{5,4},{6,7},{7,6},{8,9},{9,8},{10,11... | collective-permute-start | bytes 196616 | tf_op jit(solution)/shard_map/ppermute | solution.py:131
  5.1 7.4 %collective-permute-start.3 = (bf16[2,64,256]{2,1,0:T(8,128)(2,1)S(1)}, bf16[2,64,256]{2,1,0:T(8,128)(2,1)S(1)}, u32[]{:S(2)}, u32[]{:S(2)}) collective-permute-start(bf16[2,64,256]{2,1,0:T(8,128)(2,1)S(1)} %get-tuple-element.51), channel_id=1, source_target_pairs={{0,2},{1,3},{2,0},{3,1},{4,6},{5,7},{6,4},{7,5},{8,10},{9,11},{10,... | collective-permute-start | bytes 196616 | tf_op jit(solution)/shard_map/ppermute | solution.py:131
  7.7 6.8 %collective-permute-start.4 = (bf16[2,64,256]{2,1,0:T(8,128)(2,1)S(1)}, bf16[2,64,256]{2,1,0:T(8,128)(2,1)S(1)}, u32[]{:S(2)}, u32[]{:S(2)}) collective-permute-start(bf16[2,64,256]{2,1,0:T(8,128)(2,1)S(1)} %get-tuple-element.52), channel_id=1, source_target_pairs={{0,3},{1,2},{2,1},{3,0},{4,7},{5,6},{6,5},{7,4},{8,11},{9,10},{10,... | collective-permute-start | bytes 196616 | tf_op jit(solution)/shard_map/ppermute | solution.py:131
  7.7 14.3 %collective-permute-start.8 = (bf16[2,256,256]{2,1,0:T(8,128)(2,1)S(1)}, bf16[2,256,256]{2,1,0:T(8,128)(2,1)S(1)}, u32[]{:S(2)}, u32[]{:S(2)}) collective-permute-start(bf16[2,256,256]{2,1,0:T(8,128)(2,1)S(1)} %get-tuple-element.53), channel_id=1, source_target_pairs={{0,1},{1,0},{2,3},{3,2},{4,5},{5,4},{6,7},{7,6},{8,9},{9,8},{10,11... | collective-permute-start | bytes 786440 | tf_op jit(solution)/shard_map/ppermute | solution.py:131
  8.6 22.8 %collective-permute-start.12 = (bf16[2,256,256]{2,1,0:T(8,128)(2,1)S(1)}, bf16[2,256,256]{2,1,0:T(8,128)(2,1)S(1)}, u32[]{:S(2)}, u32[]{:S(2)}) collective-permute-start(bf16[2,256,256]{2,1,0:T(8,128)(2,1)S(1)} %get-tuple-element.57), channel_id=1, source_target_pairs={{0,2},{1,3},{2,0},{3,1},{4,6},{5,7},{6,4},{7,5},{8,10},{9,11},{10,... | collective-permute-start | bytes 786440 | tf_op jit(solution)/shard_map/ppermute | solution.py:131
  12.1 21.5 %collective-permute-start.9 = (bf16[2,256,256]{2,1,0:T(8,128)(2,1)S(1)}, bf16[2,256,256]{2,1,0:T(8,128)(2,1)S(1)}, u32[]{:S(2)}, u32[]{:S(2)}) collective-permute-start(bf16[2,256,256]{2,1,0:T(8,128)(2,1)S(1)} %get-tuple-element.54), channel_id=1, source_target_pairs={{0,3},{1,2},{2,1},{3,0},{4,7},{5,6},{6,5},{7,4},{8,11},{9,10},{10,... | collective-permute-start | bytes 786440 | tf_op jit(solution)/shard_map/ppermute | solution.py:131
  14.8 1.6 %copy-start.4 = (s32[16]{0:T(128)S(1)}, s32[16]{0:T(128)}, u32[]{:S(2)}) copy-start(s32[16]{0:T(128)} %place.5) | copy-start | bytes 196
  14.8 5.7 %collective-permute-start.6 = (bf16[3,2,64,256]{3,2,1,0:T(8,128)(2,1)S(1)}, bf16[3,2,64,256]{3,2,1,0:T(8,128)(2,1)S(1)}, u32[]{:S(2)}, u32[]{:S(2)}) collective-permute-start(bf16[3,2,64,256]{3,2,1,0:T(8,128)(2,1)S(1)} %stack.1.rest_1_), channel_id=1, source_target_pairs={{0,8},{4,12},{8,0},{12,4},{1,9},{5,13},{9,1},{13,5},{2,10},{6,14},... | collective-permute-start | bytes 589832 | tf_op jit(solution)/shard_map/ppermute | solution.py:131
  16.6 4.0 %collective-permute-start.5 = (bf16[3,2,64,256]{3,2,1,0:T(8,128)(2,1)S(1)}, bf16[3,2,64,256]{3,2,1,0:T(8,128)(2,1)S(1)}, u32[]{:S(2)}, u32[]{:S(2)}) collective-permute-start(bf16[3,2,64,256]{3,2,1,0:T(8,128)(2,1)S(1)} %stack.1.rest_1_), channel_id=1, source_target_pairs={{0,4},{4,0},{8,12},{12,8},{1,5},{5,1},{9,13},{13,9},{2,6},{6,2},{1... | collective-permute-start | bytes 589832 | tf_op jit(solution)/shard_map/ppermute | solution.py:131
  20.5 1.5 %collective-permute-start.7 = (bf16[3,2,64,256]{3,2,1,0:T(8,128)(2,1)S(1)}, bf16[3,2,64,256]{3,2,1,0:T(8,128)(2,1)S(1)}, u32[]{:S(2)}, u32[]{:S(2)}) collective-permute-start(bf16[3,2,64,256]{3,2,1,0:T(8,128)(2,1)S(1)} %collective-permute-done.6.rest_3_), channel_id=1, source_target_pairs={{0,4},{4,0},{8,12},{12,8},{1,5},{5,1},{9,13},{13,9},{2,6},{6,2},{1... | collective-permute-start | bytes 589832 | tf_op jit(solution)/shard_map/ppermute | solution.py:131
  20.5 1.5 %copy-start.3 = (s32[2,16]{1,0:T(2,128)S(1)}, s32[2,16]{1,0:T(2,128)}, u32[]{:S(2)}) copy-start(s32[2,16]{1,0:T(2,128)} %dims.3) | copy-start | bytes 388
  24.1 1.4 %collective-permute-start = (bf16[2,1,2,64,256]{4,3,2,1,0:T(8,128)(2,1)S(1)}, bf16[2,1,2,64,256]{4,3,2,1,0:T(8,128)(2,1)S(1)}, u32[]{:S(2)}, u32[]{:S(2)}) collective-permute-start(bf16[2,1,2,64,256]{4,3,2,1,0:T(8,128)(2,1)S(1)} %get-tuple-element.39), channel_id=1, source_target_pairs={{0,4},{4,0},{8,12},{12,8},{1,5},{5,1},{9,13},{13,9},{2,6},{6,2},{1... | collective-permute-start | bytes 393224 | tf_op jit(solution)/shard_map/cond/branch_1_fun/ppermute | solution.py:131
  25.6 4.3 %collective-permute-start.1 = (bf16[1,1,2,64,256]{4,3,2,1,0:T(8,128)(2,1)S(1)}, bf16[1,1,2,64,256]{4,3,2,1,0:T(8,128)(2,1)S(1)}, u32[]{:S(2)}, u32[]{:S(2)}) collective-permute-start(bf16[1,1,2,64,256]{4,3,2,1,0:T(8,128)(2,1)S(1)} %slice.59), channel_id=1, source_target_pairs={{0,8},{4,12},{8,0},{12,4},{1,9},{5,13},{9,1},{13,5},{2,10},{6,14},... | collective-permute-start | bytes 196616 | tf_op jit(solution)/shard_map/cond/branch_1_fun/ppermute | solution.py:131
  29.9 3.7 %copy-start.1 = (bf16[2,4,256,256]{3,2,1,0:T(8,128)(2,1)S(1)}, bf16[2,4,256,256]{3,2,1,0:T(8,128)(2,1)}, u32[]{:S(2)}) copy-start(bf16[2,4,256,256]{3,2,1,0:T(8,128)(2,1)} %left_env.5) | copy-start | bytes 3145732
  30.0 3.7 %copy-start.2 = (bf16[2,4,256,256]{3,2,1,0:T(8,128)(2,1)S(1)}, bf16[2,4,256,256]{3,2,1,0:T(8,128)(2,1)}, u32[]{:S(2)}) copy-start(bf16[2,4,256,256]{3,2,1,0:T(8,128)(2,1)} %right_env.3) | copy-start | bytes 3145732
  33.5 3.0 %collective-permute-start.13 = (bf16[2,1,2,64,256]{4,3,2,1,0:T(8,128)(2,1)S(1)}, bf16[2,1,2,64,256]{4,3,2,1,0:T(8,128)(2,1)S(1)}, u32[]{:S(2)}, u32[]{:S(2)}) collective-permute-start(bf16[2,1,2,64,256]{4,3,2,1,0:T(8,128)(2,1)S(1)} %get-tuple-element.59), channel_id=1, source_target_pairs={{0,4},{4,0},{8,12},{12,8},{1,5},{5,1},{9,13},{13,9},{2,6},{6,2},{1... | collective-permute-start | bytes 393224 | tf_op jit(solution)/shard_map/ppermute | solution.py:131
  35.9 2.2 %collective-permute-start.10 = (bf16[2,2,2,64,256]{4,3,2,1,0:T(8,128)(2,1)S(1)}, bf16[2,2,2,64,256]{4,3,2,1,0:T(8,128)(2,1)S(1)}, u32[]{:S(2)}, u32[]{:S(2)}) collective-permute-start(bf16[2,2,2,64,256]{4,3,2,1,0:T(8,128)(2,1)S(1)} %get-tuple-element.56), channel_id=1, source_target_pairs={{0,4},{4,0},{8,12},{12,8},{1,5},{5,1},{9,13},{13,9},{2,6},{6,2},{1... | collective-permute-start | bytes 786440 | tf_op jit(solution)/shard_map/ppermute | solution.py:131
  36.5 4.5 %collective-permute-start.14 = (bf16[1,1,2,64,256]{4,3,2,1,0:T(8,128)(2,1)S(1)}, bf16[1,1,2,64,256]{4,3,2,1,0:T(8,128)(2,1)S(1)}, u32[]{:S(2)}, u32[]{:S(2)}) collective-permute-start(bf16[1,1,2,64,256]{4,3,2,1,0:T(8,128)(2,1)S(1)} %slice.61), channel_id=1, source_target_pairs={{0,8},{4,12},{8,0},{12,4},{1,9},{5,13},{9,1},{13,5},{2,10},{6,14},... | collective-permute-start | bytes 196616 | tf_op jit(solution)/shard_map/ppermute | solution.py:131
  38.2 5.5 %collective-permute-start.11 = (bf16[1,2,2,64,256]{4,3,2,1,0:T(8,128)(2,1)S(1)}, bf16[1,2,2,64,256]{4,3,2,1,0:T(8,128)(2,1)S(1)}, u32[]{:S(2)}, u32[]{:S(2)}) collective-permute-start(bf16[1,2,2,64,256]{4,3,2,1,0:T(8,128)(2,1)S(1)} %slice.60), channel_id=1, source_target_pairs={{0,8},{4,12},{8,0},{12,4},{1,9},{5,13},{9,1},{13,5},{2,10},{6,14},... | collective-permute-start | bytes 393224 | tf_op jit(solution)/shard_map/ppermute | solution.py:131

commit v6 on v5

--- a/solution.py
+++ b/solution.py
@@ -57,14 +57,23 @@
     copies.wait(0)
 
 
-def stack_kernel(*refs):
+def keep_kernel(nsec, nb, place, right_env, after, rights, sems):
+    copies = Copies(sems)
+    me = lax.axis_index("sec")
+    for d in range(nsec):
+        _, slot, _ = find(place, nb, me ^ d, me)
+        copies.add(0, right_env.at[:, slot], rights.at[d])
+    copies.wait(0)
+
+
+def stack_kernel(after, *refs):
     pieces, out, copies = refs[:-2], refs[-2], Copies(refs[-1])
     for n, piece in enumerate(pieces):
         copies.add(0, piece, out.at[n])
     copies.wait(0)
 
 
-def work_kernel(rounds, waits, nsec, nop, nb, place, dims, psi, left_env, right_env, *rest):
+def work_kernel(rounds, waits, nsec, nop, nb, place, dims, psi, left_env, rights, *rest):
     count = len(rounds)
     far = [d for d in rounds if d]
     rest = rest[waits:]
@@ -77,7 +86,7 @@
     rows = width // nop
     found = [find(place, nb, me ^ d, me) for d in rounds]
     for e, d in enumerate(rounds):
-        block, slot, _ = found[e]
+        block, _, _ = found[e]
         if d == 0:
             copies.add((e, 0), psi.at[block], psi_v.at[e])
             copies.add((e, 0), left_env.at[:, block], left_v.at[e])
@@ -85,7 +94,7 @@
             for o in range(nop):
                 copies.add((e, 0), pieces[o].at[d - 1], chunk(psi_v, (e, EVERY), mine ^ o, rows))
             copies.add((e, 0), lefts[far.index(d)], left_v.at[e])
-        copies.add((e, 1), right_env.at[:, slot], right_v.at[e])
+        copies.add((e, 1), rights.at[d], right_v.at[e])
     row = lax.broadcasted_iota(jnp.int32, (width, width), 0)
     col = lax.broadcasted_iota(jnp.int32, (width, width), 1)
     for e, d in enumerate(rounds):
@@ -146,17 +155,28 @@
     pieces = [ship(picked[d - 1], "sec", d) for d in range(1, nsec)]
     lefts = {d: ship(picked[away + d - 1], "sec", d) for d in range(1, nsec)}
 
+    rights = pl.pallas_call(
+        functools.partial(keep_kernel, nsec, nb),
+        in_specs=[SMEM, HBM, ANY],
+        out_specs=VMEM,
+        out_shape=shape(nsec, terms, width, width),
+        scratch_shapes=[dma(nsec)],
+        compiler_params=pltpu.CompilerParams(vmem_limit_bytes=40 * 2**20),
+        cost_estimate=cost(0, 0),
+        name="keep",
+    )(right_place, right_env, picked[0])
+
     def gather(pieces):
         stacked = pl.pallas_call(
             stack_kernel,
-            in_specs=[ANY] * away,
+            in_specs=[ANY] * nsec,
             out_specs=VMEM,
             out_shape=shape(away, vecs, rows, width),
             scratch_shapes=[dma(away)],
             compiler_params=params,
             cost_estimate=cost(0, 0),
             name="stack",
-        )(*pieces)
+        )(rights, *pieces)
         gathered = {0: stacked}
         bit = nop // 2
         while bit:
@@ -170,7 +190,7 @@
         given = list(after) + (list(gathered) + [lefts[d] for d in rounds if d] if any(rounds) else [])
         value, send = pl.pallas_call(
             functools.partial(work_kernel, rounds, len(after), nsec, nop, nb),
-            in_specs=[SMEM, SMEM, HBM, HBM, HBM] + [ANY] * len(given),
+            in_specs=[SMEM, SMEM, HBM, HBM, ANY] + [ANY] * len(given),
             out_specs=[VMEM] * 2,
             out_shape=[
                 jax.ShapeDtypeStruct((nop // 2, count, vecs, rows, width), F32),
@@ -186,7 +206,7 @@
             compiler_params=params,
             cost_estimate=cost(0, 0),
             name="work",
-        )(right_place, sector_dims, psi, left_env, right_env, *given)
+        )(right_place, sector_dims, psi, left_env, rights, *given)
         bit = 1
         while True:
             value = value + ship(send, "op", bit).astype(F32)

time: 44.8 us -> 44.6 us (level)
  Pallas kernels: 8.77 us -> 8.32 us
    pallas_call x3, Pallas kernels: 6.54 us -> 5.35 us  [group(): pl.pallas_call(functools.partial(work_kernel, rounds, len(after), nsec, n...]
    pallas_call x1 -> x2, Pallas kernels: 0.25 us -> 0.99 us  [the longest x1 0.73 us: local(): pl.pallas_call(functools.partial(keep_kernel, nsec, nb), in_specs=[SMEM,...]
  transfers between devices with their start and end apart: 15 -> 15, of which waited for: 9 -> 8; matrix products, arithmetic and copies ran while one was open for 1% -> 1% of each run, Pallas kernels for 15% -> 14%
where the time goes in v6:
time: 44.6 us; the launch traced here: 44 us
  waiting for transfers between devices  17.3 us (39%)
  starting transfers between devices  16.9 us (38%)
  Pallas kernels  8.32 us (19%)
  other arithmetic  1.2 us (3%)
    ppermute x15, waiting for transfers between devices, ship(): return lax.ppermute(x, axis, [(i, i ^ d) for i in range(n)])  17.3 us
    ppermute x15, starting transfers between devices, ship(): return lax.ppermute(x, axis, [(i, i ^ d) for i in range(n)])  16.9 us
    pallas_call x3, Pallas kernels, group(): pl.pallas_call(functools.partial(work_kernel, rounds, len(after), nsec, n...  5.35 us
    pallas_call x1, Pallas kernels, local(): pl.pallas_call(functools.partial(pick_kernel, nsec, nop, nb), in_specs=[S...  1.98 us
  transfers between devices with their start and end apart: 15, of which 8 were waited for; matrix products, arithmetic and copies ran while one was open for 1% of the time, Pallas kernels for 14%

profile of v6, /device:TPU:0, one launch (start us, length us, event | category | flops | bytes accessed | tf_op | source)
XLA Modules:
  0.0 44.0 jit_solution(17377834181517527426)
XLA Ops:
  0.0 0.0 copy-start
  0.0 2.0 %pick.1 = (bf16[2,64,256]{2,1,0:T(8,128)(2,1)S(1)}, bf16[2,64,256]{2,1,0:T(8,128)(2,1)S(1)}, bf16[2,64,256]{2,1,0:T(8,128)(2,1)S(1)}, bf16[2,256,256]{2,1,0:T(8,...) custom-call(s32[16]{0:T(128)} %place.7, bf16[4,2,256,256]{3,2,1,0:T(8,128)(2,1)} %psi.5, ...), custom_call_target="tpu_custom_call" | custom-call | tf_op jit(solution)/shard_map/pick/pallas_call | solution.py:145
  2.0 3.1 %collective-permute-start.2 = (bf16[2,64,256]{2,1,0:T(8,128)(2,1)S(1)}, bf16[2,64,256]{2,1,0:T(8,128)(2,1)S(1)}, u32[]{:S(2)}, u32[]{:S(2)}) collective-permute-start(bf16[2,64,256]{2,1,0:T(8,128)(2,1)S(1)} %get-tuple-element.50.after), channel_id=1, source_target_pairs={{0,1},{1,0},{2,3},{3,2},{4,5},{5,4},{6,7},{7,6},{8,9},{9,8},{10,11... | collective-permute-start | bytes 196616 | tf_op jit(solution)/shard_map/ppermute | solution.py:140
  5.1 2.6 %collective-permute-start.3 = (bf16[2,64,256]{2,1,0:T(8,128)(2,1)S(1)}, bf16[2,64,256]{2,1,0:T(8,128)(2,1)S(1)}, u32[]{:S(2)}, u32[]{:S(2)}) collective-permute-start(bf16[2,64,256]{2,1,0:T(8,128)(2,1)S(1)} %get-tuple-element.51), channel_id=1, source_target_pairs={{0,2},{1,3},{2,0},{3,1},{4,6},{5,7},{6,4},{7,5},{8,10},{9,11},{10,... | collective-permute-start | bytes 196616 | tf_op jit(solution)/shard_map/ppermute | solution.py:140
  7.7 0.0 collective-permute-start.4
  7.7 0.9 %collective-permute-start.8 = (bf16[2,256,256]{2,1,0:T(8,128)(2,1)S(1)}, bf16[2,256,256]{2,1,0:T(8,128)(2,1)S(1)}, u32[]{:S(2)}, u32[]{:S(2)}) collective-permute-start(bf16[2,256,256]{2,1,0:T(8,128)(2,1)S(1)} %get-tuple-element.53), channel_id=1, source_target_pairs={{0,1},{1,0},{2,3},{3,2},{4,5},{5,4},{6,7},{7,6},{8,9},{9,8},{10,11... | collective-permute-start | bytes 786440 | tf_op jit(solution)/shard_map/ppermute | solution.py:140
  8.6 0.0 copy-start.3
  8.6 3.5 %collective-permute-start.12 = (bf16[2,256,256]{2,1,0:T(8,128)(2,1)S(1)}, bf16[2,256,256]{2,1,0:T(8,128)(2,1)S(1)}, u32[]{:S(2)}, u32[]{:S(2)}) collective-permute-start(bf16[2,256,256]{2,1,0:T(8,128)(2,1)S(1)} %get-tuple-element.57), channel_id=1, source_target_pairs={{0,2},{1,3},{2,0},{3,1},{4,6},{5,7},{6,4},{7,5},{8,10},{9,11},{10,... | collective-permute-start | bytes 786440 | tf_op jit(solution)/shard_map/ppermute | solution.py:140
  12.1 0.0 copy-done
  12.1 0.0 copy-done.3
  12.1 0.7 %keep.1.after.rights = bf16[4,2,256,256]{3,2,1,0:T(8,128)(2,1)S(1)} custom-call(s32[16]{0:T(128)S(1)} %copy-done.3, bf16[2,4,256,256]{3,2,1,0:T(8,128)(2,1)S(1)} %copy-done, bf16[2,64,256]{2,1,0:T(8,128)(2,1)S(1)} %get-tuple-element.50.after), custom_call_target="tpu_custom_call" | custom-call | tf_op jit(solution)/shard_map/keep/pallas_call | solution.py:158
  12.8 0.0 collective-permute-done.2.refs_0_
  12.8 0.2 collective-permute-start.9
  13.0 0.0 collective-permute-done.3.refs_1_
  13.0 1.5 %collective-permute-done.4.refs_2_ = bf16[2,64,256]{2,1,0:T(8,128)(2,1)S(1)} collective-permute-done((bf16[2,64,256]{2,1,0:T(8,128)(2,1)S(1)}, bf16[2,64,256]{2,1,0:T(8,128)(2,1)S(1)}, u32[]{:S(2)}, u32[]{:S(2)}) %collective-permute-start.4) | collective-permute-done | bytes 65568 | tf_op jit(solution)/shard_map/ppermute | solution.py:140
  14.5 0.3 stack.1.rest_1_
  14.8 1.6 %collective-permute-start.6 = (bf16[3,2,64,256]{3,2,1,0:T(8,128)(2,1)S(1)}, bf16[3,2,64,256]{3,2,1,0:T(8,128)(2,1)S(1)}, u32[]{:S(2)}, u32[]{:S(2)}) collective-permute-start(bf16[3,2,64,256]{3,2,1,0:T(8,128)(2,1)S(1)} %stack.1.rest_1_), channel_id=1, source_target_pairs={{0,8},{4,12},{8,0},{12,4},{1,9},{5,13},{9,1},{13,5},{2,10},{6,14},... | collective-permute-start | bytes 589832 | tf_op jit(solution)/shard_map/ppermute | solution.py:140
  16.3 0.2 select_reduce_fusion
  16.6 0.1 collective-permute-start.5
  16.6 3.9 %collective-permute-done.6.rest_3_ = bf16[3,2,64,256]{3,2,1,0:T(8,128)(2,1)S(1)} collective-permute-done((bf16[3,2,64,256]{3,2,1,0:T(8,128)(2,1)S(1)}, bf16[3,2,64,256]{3,2,1,0:T(8,128)(2,1)S(1)}, u32[]{:S(2)}, u32[]{:S(2)}) %collective-permute-start.6) | collective-permute-done | bytes 196640 | tf_op jit(solution)/shard_map/ppermute | solution.py:140
  20.5 0.0 collective-permute-start.7
  20.5 0.0 copy-start.4
  20.5 0.0 collective-permute-done.5.rest_2_
  20.5 1.4 %collective-permute-done.8 = bf16[2,256,256]{2,1,0:T(8,128)(2,1)S(1)} collective-permute-done((bf16[2,256,256]{2,1,0:T(8,128)(2,1)S(1)}, bf16[2,256,256]{2,1,0:T(8,128)(2,1)S(1)}, u32[]{:S(2)}, u32[]{:S(2)}) %collective-permute-start.8) | collective-permute-done | bytes 262176 | tf_op jit(solution)/shard_map/ppermute | solution.py:140
  22.0 0.0 collective-permute-done.7.rest_4_
  22.0 0.0 copy-done.4
  22.0 7.3 %conditional.1 = (bf16[2,64,256]{2,1,0:T(8,128)(2,1)S(1)}) conditional(s32[]{:T(128)} %bitcast.1, () %tuple.11, (s32[16]{0:T(128)S(1)}, s32[2,16]{1,0:T(2,128)S(1)}, bf16[4,2,256,256]{3,2,1,0:T(8,128)(2,1)}, bf16[2,4,256,256]{3,2,1,0:T(8,128)(2,1)}, bf16[4,2,256,256]{3,2,1,0:T(8,128)(2,1)S(1)}, /*index=5*/bf16[3,2,64,256]{3,2,1,0:T(8,128)(2,1)S(1)}, ...), branch_computations={%region_1.0_spmd, %region_2.3_spmd} | conditional | flops 229376 | bytes 1835096 | solution.py:222
  22.0 1.5 %work.3 = (f32[2,1,2,64,256]{4,3,2,1,0:T(8,128)S(1)}, bf16[2,1,2,64,256]{4,3,2,1,0:T(8,128)(2,1)S(1)}) custom-call(s32[16]{0:T(128)S(1)} %get-tuple-element.28.place, s32[2,16]{1,0:T(2,128)S(1)} %get-tuple-element.29.dims, bf16[4,2,256,256]{3,2,1,0:T(8,128)(2,1)} %get-tuple-element.30.psi, bf16[2,4,256,256]{3,2,1,0:T(8,128)(2,1)} %get-tuple-element.31.left_env, ...), custom_call_target="tpu_custom_call" | custom-call | tf_op jit(solution)/shard_map/cond/branch_1_fun/work/pallas_call | solution.py:191
  23.5 0.2 collective-permute-start
  23.7 1.3 %collective-permute-done = bf16[2,1,2,64,256]{4,3,2,1,0:T(8,128)(2,1)S(1)} collective-permute-done((bf16[2,1,2,64,256]{4,3,2,1,0:T(8,128)(2,1)S(1)}, bf16[2,1,2,64,256]{4,3,2,1,0:T(8,128)(2,1)S(1)}, u32[]{:S(2)}, u32[]{:S(2)}) %collective-permute-start) | collective-permute-done | bytes 131104 | tf_op jit(solution)/shard_map/cond/branch_1_fun/ppermute | solution.py:140
  25.0 1.6 %collective-permute-start.1 = (bf16[1,1,2,64,256]{4,3,2,1,0:T(8,128)(2,1)S(1)}, bf16[1,1,2,64,256]{4,3,2,1,0:T(8,128)(2,1)S(1)}, u32[]{:S(2)}, u32[]{:S(2)}) collective-permute-start(bf16[1,1,2,64,256]{4,3,2,1,0:T(8,128)(2,1)S(1)} %slice.59), channel_id=1, source_target_pairs={{0,8},{4,12},{8,0},{12,4},{1,9},{5,13},{9,1},{13,5},{2,10},{6,14},... | collective-permute-start | bytes 196616 | tf_op jit(solution)/shard_map/cond/branch_1_fun/ppermute | solution.py:140
  26.5 2.8 %collective-permute-done.1 = bf16[1,1,2,64,256]{4,3,2,1,0:T(8,128)(2,1)S(1)} collective-permute-done((bf16[1,1,2,64,256]{4,3,2,1,0:T(8,128)(2,1)S(1)}, bf16[1,1,2,64,256]{4,3,2,1,0:T(8,128)(2,1)S(1)}, u32[]{:S(2)}, u32[]{:S(2)}) %collective-permute-start.1) | collective-permute-done | bytes 65568 | tf_op jit(solution)/shard_map/cond/branch_1_fun/ppermute | solution.py:140
  29.3 0.0 copy-start.1
  29.3 0.0 copy-start.2
  29.4 2.0 %collective-permute-done.12.rest_5_ = bf16[2,256,256]{2,1,0:T(8,128)(2,1)S(1)} collective-permute-done((bf16[2,256,256]{2,1,0:T(8,128)(2,1)S(1)}, bf16[2,256,256]{2,1,0:T(8,128)(2,1)S(1)}, u32[]{:S(2)}, u32[]{:S(2)}) %collective-permute-start.12) | collective-permute-done | bytes 262176 | tf_op jit(solution)/shard_map/ppermute | solution.py:140
  31.4 1.5 %work.5 = (f32[2,1,2,64,256]{4,3,2,1,0:T(8,128)S(1)}, bf16[2,1,2,64,256]{4,3,2,1,0:T(8,128)(2,1)S(1)}) custom-call(s32[16]{0:T(128)S(1)} %copy-done.3, s32[2,16]{1,0:T(2,128)S(1)} %copy-done.4, bf16[4,2,256,256]{3,2,1,0:T(8,128)(2,1)} %psi.5, bf16[2,4,256,256]{3,2,1,0:T(8,128)(2,1)} %left_env.5, bf16[4,2,256,256]{3,2,1,0:T(8,128)(2,1)S(1)} %keep.1.after.rights, ...), custom_call_target="tpu_custom_call" | custom-call | tf_op jit(solution)/shard_map/work/pallas_call | solution.py:191
  32.9 0.1 collective-permute-start.13
  33.0 0.0 collective-permute-done.9.rest_5_
  33.0 0.0 copy-done.1
  33.0 0.0 copy-done.2
  33.0 2.3 %work.4 = (f32[2,2,2,64,256]{4,3,2,1,0:T(8,128)S(1)}, bf16[2,2,2,64,256]{4,3,2,1,0:T(8,128)(2,1)S(1)}) custom-call(s32[16]{0:T(128)S(1)} %copy-done.3, s32[2,16]{1,0:T(2,128)S(1)} %copy-done.4, bf16[4,2,256,256]{3,2,1,0:T(8,128)(2,1)S(1)} %copy-done.1, bf16[2,4,256,256]{3,2,1,0:T(8,128)(2,1)S(1)} %copy-done.2, ...), custom_call_target="tpu_custom_call" | custom-call | tf_op jit(solution)/shard_map/work/pallas_call | solution.py:191
  35.4 0.6 %collective-permute-start.10 = (bf16[2,2,2,64,256]{4,3,2,1,0:T(8,128)(2,1)S(1)}, bf16[2,2,2,64,256]{4,3,2,1,0:T(8,128)(2,1)S(1)}, u32[]{:S(2)}, u32[]{:S(2)}) collective-permute-start(bf16[2,2,2,64,256]{4,3,2,1,0:T(8,128)(2,1)S(1)} %get-tuple-element.56), channel_id=1, source_target_pairs={{0,4},{4,0},{8,12},{12,8},{1,5},{5,1},{9,13},{13,9},{2,6},{6,2},{1... | collective-permute-start | bytes 786440 | tf_op jit(solution)/shard_map/ppermute | solution.py:140
  35.9 0.0 collective-permute-done.13
  36.0 1.6 %collective-permute-start.14 = (bf16[1,1,2,64,256]{4,3,2,1,0:T(8,128)(2,1)S(1)}, bf16[1,1,2,64,256]{4,3,2,1,0:T(8,128)(2,1)S(1)}, u32[]{:S(2)}, u32[]{:S(2)}) collective-permute-start(bf16[1,1,2,64,256]{4,3,2,1,0:T(8,128)(2,1)S(1)} %slice.61), channel_id=1, source_target_pairs={{0,8},{4,12},{8,0},{12,4},{1,9},{5,13},{9,1},{13,5},{2,10},{6,14},... | collective-permute-start | bytes 196616 | tf_op jit(solution)/shard_map/ppermute | solution.py:140
  37.5 0.0 collective-permute-done.10
  37.5 0.1 convert_add_fusion.1
  37.6 1.1 %collective-permute-start.11 = (bf16[1,2,2,64,256]{4,3,2,1,0:T(8,128)(2,1)S(1)}, bf16[1,2,2,64,256]{4,3,2,1,0:T(8,128)(2,1)S(1)}, u32[]{:S(2)}, u32[]{:S(2)}) collective-permute-start(bf16[1,2,2,64,256]{4,3,2,1,0:T(8,128)(2,1)S(1)} %slice.60), channel_id=1, source_target_pairs={{0,8},{4,12},{8,0},{12,4},{1,9},{5,13},{9,1},{13,5},{2,10},{6,14},... | collective-permute-start | bytes 393224 | tf_op jit(solution)/shard_map/ppermute | solution.py:140
  38.7 1.7 %collective-permute-done.14 = bf16[1,1,2,64,256]{4,3,2,1,0:T(8,128)(2,1)S(1)} collective-permute-done((bf16[1,1,2,64,256]{4,3,2,1,0:T(8,128)(2,1)S(1)}, bf16[1,1,2,64,256]{4,3,2,1,0:T(8,128)(2,1)S(1)}, u32[]{:S(2)}, u32[]{:S(2)}) %collective-permute-start.14) | collective-permute-done | bytes 65568 | tf_op jit(solution)/shard_map/ppermute | solution.py:140
  40.5 2.6 %collective-permute-done.11 = bf16[1,2,2,64,256]{4,3,2,1,0:T(8,128)(2,1)S(1)} collective-permute-done((bf16[1,2,2,64,256]{4,3,2,1,0:T(8,128)(2,1)S(1)}, bf16[1,2,2,64,256]{4,3,2,1,0:T(8,128)(2,1)S(1)}, u32[]{:S(2)}, u32[]{:S(2)}) %collective-permute-start.11) | collective-permute-done | bytes 131104 | tf_op jit(solution)/shard_map/ppermute | solution.py:140
  43.2 0.8 %select_select_fusion = bf16[4,2,64,256]{3,2,1,0:T(8,128)(2,1)} fusion(pred[4]{0:T(512)(128)(4,1)S(1)} %get-tuple-element.65, pred[4]{0:T(512)(128)(4,1)S(1)} %get-tuple-element.64, pred[4]{0:T(512)(128)(4,1)S(1)} %get-tuple-element.60, bf16[2,64,256]{2,1,0:T(8,128)(2,1)S(1)} %get-tuple-element.63, bf16[2,64,256]{2,1,0:T(8,128)(2,1)S(1)} %get-tuple-element.66.rest_0_, ...), kind=kLoop, calls=%fused_computation.9 | loop fusion | flops 393216 | bytes 524300 | tf_op jit(solution)/shard_map/jit(_where)/select_n | solution.py:244
  (12 shorter events, 0.2 us)
Async XLA Ops:
  0.0 12.1 %copy-start = (bf16[2,4,256,256]{3,2,1,0:T(8,128)(2,1)S(1)}, bf16[2,4,256,256]{3,2,1,0:T(8,128)(2,1)}, u32[]{:S(2)}) copy-start(bf16[2,4,256,256]{3,2,1,0:T(8,128)(2,1)} %right_env.1) | copy-start | bytes 3145732
  2.0 10.8 %collective-permute-start.2 = (bf16[2,64,256]{2,1,0:T(8,128)(2,1)S(1)}, bf16[2,64,256]{2,1,0:T(8,128)(2,1)S(1)}, u32[]{:S(2)}, u32[]{:S(2)}) collective-permute-start(bf16[2,64,256]{2,1,0:T(8,128)(2,1)S(1)} %get-tuple-element.50.after), channel_id=1, source_target_pairs={{0,1},{1,0},{2,3},{3,2},{4,5},{5,4},{6,7},{7,6},{8,9},{9,8},{10,11... | collective-permute-start | bytes 196616 | tf_op jit(solution)/shard_map/ppermute | solution.py:140
  5.1 7.9 %collective-permute-start.3 = (bf16[2,64,256]{2,1,0:T(8,128)(2,1)S(1)}, bf16[2,64,256]{2,1,0:T(8,128)(2,1)S(1)}, u32[]{:S(2)}, u32[]{:S(2)}) collective-permute-start(bf16[2,64,256]{2,1,0:T(8,128)(2,1)S(1)} %get-tuple-element.51), channel_id=1, source_target_pairs={{0,2},{1,3},{2,0},{3,1},{4,6},{5,7},{6,4},{7,5},{8,10},{9,11},{10,... | collective-permute-start | bytes 196616 | tf_op jit(solution)/shard_map/ppermute | solution.py:140
  7.7 6.8 %collective-permute-start.4 = (bf16[2,64,256]{2,1,0:T(8,128)(2,1)S(1)}, bf16[2,64,256]{2,1,0:T(8,128)(2,1)S(1)}, u32[]{:S(2)}, u32[]{:S(2)}) collective-permute-start(bf16[2,64,256]{2,1,0:T(8,128)(2,1)S(1)} %get-tuple-element.52), channel_id=1, source_target_pairs={{0,3},{1,2},{2,1},{3,0},{4,7},{5,6},{6,5},{7,4},{8,11},{9,10},{10,... | collective-permute-start | bytes 196616 | tf_op jit(solution)/shard_map/ppermute | solution.py:140
  7.7 14.3 %collective-permute-start.8 = (bf16[2,256,256]{2,1,0:T(8,128)(2,1)S(1)}, bf16[2,256,256]{2,1,0:T(8,128)(2,1)S(1)}, u32[]{:S(2)}, u32[]{:S(2)}) collective-permute-start(bf16[2,256,256]{2,1,0:T(8,128)(2,1)S(1)} %get-tuple-element.53), channel_id=1, source_target_pairs={{0,1},{1,0},{2,3},{3,2},{4,5},{5,4},{6,7},{7,6},{8,9},{9,8},{10,11... | collective-permute-start | bytes 786440 | tf_op jit(solution)/shard_map/ppermute | solution.py:140
  8.6 3.5 %copy-start.3 = (s32[16]{0:T(128)S(1)}, s32[16]{0:T(128)}, u32[]{:S(2)}) copy-start(s32[16]{0:T(128)} %place.7) | copy-start | bytes 196
  8.6 22.8 %collective-permute-start.12 = (bf16[2,256,256]{2,1,0:T(8,128)(2,1)S(1)}, bf16[2,256,256]{2,1,0:T(8,128)(2,1)S(1)}, u32[]{:S(2)}, u32[]{:S(2)}) collective-permute-start(bf16[2,256,256]{2,1,0:T(8,128)(2,1)S(1)} %get-tuple-element.57), channel_id=1, source_target_pairs={{0,2},{1,3},{2,0},{3,1},{4,6},{5,7},{6,4},{7,5},{8,10},{9,11},{10,... | collective-permute-start | bytes 786440 | tf_op jit(solution)/shard_map/ppermute | solution.py:140
  12.8 20.2 %collective-permute-start.9 = (bf16[2,256,256]{2,1,0:T(8,128)(2,1)S(1)}, bf16[2,256,256]{2,1,0:T(8,128)(2,1)S(1)}, u32[]{:S(2)}, u32[]{:S(2)}) collective-permute-start(bf16[2,256,256]{2,1,0:T(8,128)(2,1)S(1)} %get-tuple-element.54), channel_id=1, source_target_pairs={{0,3},{1,2},{2,1},{3,0},{4,7},{5,6},{6,5},{7,4},{8,11},{9,10},{10,... | collective-permute-start | bytes 786440 | tf_op jit(solution)/shard_map/ppermute | solution.py:140
  14.8 5.7 %collective-permute-start.6 = (bf16[3,2,64,256]{3,2,1,0:T(8,128)(2,1)S(1)}, bf16[3,2,64,256]{3,2,1,0:T(8,128)(2,1)S(1)}, u32[]{:S(2)}, u32[]{:S(2)}) collective-permute-start(bf16[3,2,64,256]{3,2,1,0:T(8,128)(2,1)S(1)} %stack.1.rest_1_), channel_id=1, source_target_pairs={{0,8},{4,12},{8,0},{12,4},{1,9},{5,13},{9,1},{13,5},{2,10},{6,14},... | collective-permute-start | bytes 589832 | tf_op jit(solution)/shard_map/ppermute | solution.py:140
  16.6 4.0 %collective-permute-start.5 = (bf16[3,2,64,256]{3,2,1,0:T(8,128)(2,1)S(1)}, bf16[3,2,64,256]{3,2,1,0:T(8,128)(2,1)S(1)}, u32[]{:S(2)}, u32[]{:S(2)}) collective-permute-start(bf16[3,2,64,256]{3,2,1,0:T(8,128)(2,1)S(1)} %stack.1.rest_1_), channel_id=1, source_target_pairs={{0,4},{4,0},{8,12},{12,8},{1,5},{5,1},{9,13},{13,9},{2,6},{6,2},{1... | collective-permute-start | bytes 589832 | tf_op jit(solution)/shard_map/ppermute | solution.py:140
  20.5 1.5 %collective-permute-start.7 = (bf16[3,2,64,256]{3,2,1,0:T(8,128)(2,1)S(1)}, bf16[3,2,64,256]{3,2,1,0:T(8,128)(2,1)S(1)}, u32[]{:S(2)}, u32[]{:S(2)}) collective-permute-start(bf16[3,2,64,256]{3,2,1,0:T(8,128)(2,1)S(1)} %collective-permute-done.6.rest_3_), channel_id=1, source_target_pairs={{0,4},{4,0},{8,12},{12,8},{1,5},{5,1},{9,13},{13,9},{2,6},{6,2},{1... | collective-permute-start | bytes 589832 | tf_op jit(solution)/shard_map/ppermute | solution.py:140
  20.5 1.5 %copy-start.4 = (s32[2,16]{1,0:T(2,128)S(1)}, s32[2,16]{1,0:T(2,128)}, u32[]{:S(2)}) copy-start(s32[2,16]{1,0:T(2,128)} %dims.3) | copy-start | bytes 388
  23.5 1.4 %collective-permute-start = (bf16[2,1,2,64,256]{4,3,2,1,0:T(8,128)(2,1)S(1)}, bf16[2,1,2,64,256]{4,3,2,1,0:T(8,128)(2,1)S(1)}, u32[]{:S(2)}, u32[]{:S(2)}) collective-permute-start(bf16[2,1,2,64,256]{4,3,2,1,0:T(8,128)(2,1)S(1)} %get-tuple-element.39), channel_id=1, source_target_pairs={{0,4},{4,0},{8,12},{12,8},{1,5},{5,1},{9,13},{13,9},{2,6},{6,2},{1... | collective-permute-start | bytes 393224 | tf_op jit(solution)/shard_map/cond/branch_1_fun/ppermute | solution.py:140
  25.0 4.3 %collective-permute-start.1 = (bf16[1,1,2,64,256]{4,3,2,1,0:T(8,128)(2,1)S(1)}, bf16[1,1,2,64,256]{4,3,2,1,0:T(8,128)(2,1)S(1)}, u32[]{:S(2)}, u32[]{:S(2)}) collective-permute-start(bf16[1,1,2,64,256]{4,3,2,1,0:T(8,128)(2,1)S(1)} %slice.59), channel_id=1, source_target_pairs={{0,8},{4,12},{8,0},{12,4},{1,9},{5,13},{9,1},{13,5},{2,10},{6,14},... | collective-permute-start | bytes 196616 | tf_op jit(solution)/shard_map/cond/branch_1_fun/ppermute | solution.py:140
  29.3 3.7 %copy-start.1 = (bf16[4,2,256,256]{3,2,1,0:T(8,128)(2,1)S(1)}, bf16[4,2,256,256]{3,2,1,0:T(8,128)(2,1)}, u32[]{:S(2)}) copy-start(bf16[4,2,256,256]{3,2,1,0:T(8,128)(2,1)} %psi.5) | copy-start | bytes 3145732
  29.3 3.7 %copy-start.2 = (bf16[2,4,256,256]{3,2,1,0:T(8,128)(2,1)S(1)}, bf16[2,4,256,256]{3,2,1,0:T(8,128)(2,1)}, u32[]{:S(2)}) copy-start(bf16[2,4,256,256]{3,2,1,0:T(8,128)(2,1)} %left_env.5) | copy-start | bytes 3145732
  32.9 3.0 %collective-permute-start.13 = (bf16[2,1,2,64,256]{4,3,2,1,0:T(8,128)(2,1)S(1)}, bf16[2,1,2,64,256]{4,3,2,1,0:T(8,128)(2,1)S(1)}, u32[]{:S(2)}, u32[]{:S(2)}) collective-permute-start(bf16[2,1,2,64,256]{4,3,2,1,0:T(8,128)(2,1)S(1)} %get-tuple-element.59), channel_id=1, source_target_pairs={{0,4},{4,0},{8,12},{12,8},{1,5},{5,1},{9,13},{13,9},{2,6},{6,2},{1... | collective-permute-start | bytes 393224 | tf_op jit(solution)/shard_map/ppermute | solution.py:140
  35.4 2.2 %collective-permute-start.10 = (bf16[2,2,2,64,256]{4,3,2,1,0:T(8,128)(2,1)S(1)}, bf16[2,2,2,64,256]{4,3,2,1,0:T(8,128)(2,1)S(1)}, u32[]{:S(2)}, u32[]{:S(2)}) collective-permute-start(bf16[2,2,2,64,256]{4,3,2,1,0:T(8,128)(2,1)S(1)} %get-tuple-element.56), channel_id=1, source_target_pairs={{0,4},{4,0},{8,12},{12,8},{1,5},{5,1},{9,13},{13,9},{2,6},{6,2},{1... | collective-permute-start | bytes 786440 | tf_op jit(solution)/shard_map/ppermute | solution.py:140
  36.0 4.5 %collective-permute-start.14 = (bf16[1,1,2,64,256]{4,3,2,1,0:T(8,128)(2,1)S(1)}, bf16[1,1,2,64,256]{4,3,2,1,0:T(8,128)(2,1)S(1)}, u32[]{:S(2)}, u32[]{:S(2)}) collective-permute-start(bf16[1,1,2,64,256]{4,3,2,1,0:T(8,128)(2,1)S(1)} %slice.61), channel_id=1, source_target_pairs={{0,8},{4,12},{8,0},{12,4},{1,9},{5,13},{9,1},{13,5},{2,10},{6,14},... | collective-permute-start | bytes 196616 | tf_op jit(solution)/shard_map/ppermute | solution.py:140
  37.6 5.5 %collective-permute-start.11 = (bf16[1,2,2,64,256]{4,3,2,1,0:T(8,128)(2,1)S(1)}, bf16[1,2,2,64,256]{4,3,2,1,0:T(8,128)(2,1)S(1)}, u32[]{:S(2)}, u32[]{:S(2)}) collective-permute-start(bf16[1,2,2,64,256]{4,3,2,1,0:T(8,128)(2,1)S(1)} %slice.60), channel_id=1, source_target_pairs={{0,8},{4,12},{8,0},{12,4},{1,9},{5,13},{9,1},{13,5},{2,10},{6,14},... | collective-permute-start | bytes 393224 | tf_op jit(solution)/shard_map/ppermute | solution.py:140
